TPU v7x, 32 devices: a whole 2x2x4 slice. The times are simulated.
32 devices in a mesh: dp: 16 (over z, x, core), tensor: 2 (over y).
Axes of the slice: x: 2, y: 2, z: 4, core: 2. Of those that a mesh axis runs over, the one named last changes fastest.
Arguments:
- frames: bfloat16 [2, 16384, 1280], P(None, ('dp', 'tensor')), may hold values from -6 to 6
- cotangent: bfloat16 [2, 16384, 1280], P(None, ('dp', 'tensor')), may hold values from -6 to 6
- segment_ids: int32 [2, 16384], replicated, may hold values from 0 to 11, as said below
- w_qkv: bfloat16 [1280, 3, 1280], P('dp', None, 'tensor'), may hold values from -0.15625 to 0.15625
- w_out: bfloat16 [1280, 1280], P('dp', 'tensor'), may hold values from -4 to 4
- w_fc1: bfloat16 [1280, 5120], P('dp', 'tensor'), may hold values from -0.15625 to 0.15625
- w_fc2: bfloat16 [1280, 5120], P('dp', 'tensor'), may hold values from -0.078125 to 0.078125
- bias_qv: bfloat16 [2, 1280], P(None, 'tensor'), may hold values from -2 to 2
- bias_fc1: bfloat16 [5120], P('tensor'), may hold values from -3 to 3
- norm_vectors: bfloat16 [6, 1280], replicated, may hold values from -1.2 to 1.6
Outputs:
- output: bfloat16 [2, 16384, 1280], P(None, ('dp', 'tensor'))
- frames_grad: float32 [2, 16384, 1280], P(None, ('dp', 'tensor'))
- grad_qkv: float32 [1280, 3, 1280], P('dp', None, 'tensor')
- grad_out: float32 [1280, 1280], P('dp', 'tensor')
- grad_fc1: float32 [1280, 5120], P('dp', 'tensor')
- grad_fc2: float32 [1280, 5120], P('dp', 'tensor')
- grad_bias_qv: float32 [2, 1280], P(None, 'tensor')
- grad_bias_fc1: float32 [5120], P('tensor')
- grad_norm: float32 [6, 1280], replicated
Inputs may be any that keep to these rules, and one draw needn't show every extreme that they name: `segment_ids`: each micro-batch's row numbers its clips 0, 1, 2, ... in order of frames, never falling; every clip has at most 1500 frames, and in every micro-batch one clip has exactly 1500.
All inputs are finite; a program needn't handle non-finite values.
Results may differ from a plain program's by a relative error of at most 0.02.
Values may be sent and summed in bfloat16 or wider, within the bound.
No kernel may reach another device: no remote copies, remote signals or barrier semaphores. Data moves between devices by JAX's collectives and lax.ppermute only.
A program may use at most 264 MiB of HBM per device.

v0:
```python
import math

import jax
import jax.numpy as jnp
from jax import lax
from jax.sharding import PartitionSpec as P

D = 1280
HD = 80
FR = 1024
MB = 2
REACH = 2


EPSILON = 1e-05
NEGATIVE = -1e30


def passed_along(x, axis, by):
    length = lax.axis_size(axis)
    pairs = [(i, i + by) for i in range(length) if 0 <= i + by < length]
    return lax.ppermute(x, axis, pairs)


def shortened(x):

    def short(part):
        return part.astype(jnp.bfloat16) if part.dtype == jnp.float32 else part

    return jax.tree.map(short, x)


def norm_rows(values, gain, shift):
    average = jnp.mean(values, axis=-1, keepdims=True)
    centred = values - average
    spread = jnp.mean(centred * centred, axis=-1, keepdims=True)
    return centred * lax.rsqrt(spread + EPSILON) * gain + shift


def gelu_exact(values):
    return jax.nn.gelu(values, approximate=False)


def collect_rows(values):
    return lax.all_gather(values, "tensor", axis=0, tiled=True)


def share_sums(values):
    return lax.psum_scatter(
        values.astype(jnp.bfloat16), "tensor", scatter_dimension=0, tiled=True
    ).astype(jnp.float32)


def collect_grads(values):
    return lax.all_gather(values, "tensor", axis=0, tiled=True)


def share_grads(values):
    return lax.psum_scatter(
        values.astype(jnp.bfloat16), "tensor", scatter_dimension=0, tiled=True
    ).astype(jnp.float32)


def fetch_near(stacked, distance):
    return passed_along(stacked, "dp", distance)


def return_near(stacked, distance):
    return passed_along(stacked.astype(jnp.bfloat16), "dp", distance).astype(stacked.dtype)


def gather_near(key_rows, val_rows):
    stacked = jnp.stack((key_rows, val_rows))
    pieces = []
    for offset in range(REACH):
        if offset == 0:
            pieces.append(fetch_near(stacked, REACH))
        else:
            pieces.append(fetch_near(stacked, REACH - offset))
    pieces.append(stacked)
    for offset in range(REACH):
        if offset == REACH - 1:
            pieces.append(fetch_near(stacked, -(offset + 1)))
        else:
            pieces.append(fetch_near(stacked, -(offset + 1)))
    return jnp.concatenate(pieces, axis=1)


def scatter_near(grad_pair, edge_rows):
    left_widths = [edge_rows] + [FR] * (REACH - 1)
    right_widths = [FR] * (REACH - 1) + [edge_rows]
    own_start = sum(left_widths)
    own_rows = grad_pair[:, own_start : own_start + FR]
    cursor = 0
    for offset in range(REACH):
        width_now = left_widths[offset]
        returned = return_near(grad_pair[:, cursor : cursor + width_now], -(REACH - offset))
        own_rows = own_rows + returned
        cursor = cursor + width_now
    cursor = cursor + FR
    for offset in range(REACH):
        width_now = right_widths[offset]
        returned = return_near(grad_pair[:, cursor : cursor + width_now], offset + 1)
        own_rows = own_rows + returned
        cursor = cursor + width_now
    return own_rows


def split_blocks(array, block_len):
    return array.reshape((array.shape[0] // block_len, block_len) + array.shape[1:])


def block_scores(queries, key_block, ids_query, ids_block):
    score_scale = 1.0 / math.sqrt(HD)
    raw_scores = (
        jnp.einsum("qhd,khd->hqk", queries, key_block, preferred_element_type=jnp.float32)
        * score_scale
    )
    same_clip = (ids_query[:, None] == ids_block[None, :])[None]
    return (raw_scores, same_clip)


def attend_forward(queries, key_all, val_all, ids_query, ids_keys):
    block_len = min(512, FR)
    key_blocks = split_blocks(key_all, block_len)
    val_blocks = split_blocks(val_all, block_len)
    id_blocks = split_blocks(ids_keys, block_len)

    def statistics(state_pair, blocks):
        row_top, row_total = state_pair
        raw_scores, same_clip = block_scores(queries, blocks[0], ids_query, blocks[1])
        masked = jnp.where(same_clip, raw_scores, NEGATIVE)
        new_top = jnp.maximum(row_top, jnp.max(masked, axis=-1))
        expo_rows = jnp.where(same_clip, jnp.exp(masked - new_top[:, :, None]), 0.0)
        row_total = row_total * jnp.exp(row_top - new_top) + jnp.sum(expo_rows, axis=-1)
        return ((new_top, row_total), None)

    start_top = jnp.full((queries.shape[1], queries.shape[0]), NEGATIVE, jnp.float32)
    state_pair, unused = lax.scan(
        statistics, (start_top, jnp.zeros_like(start_top)), (key_blocks, id_blocks)
    )
    log_total = state_pair[0] + jnp.log(state_pair[1])

    def outputs_of(running, blocks):
        raw_scores, same_clip = block_scores(queries, blocks[0], ids_query, blocks[1])
        prob_rows = jnp.where(same_clip, jnp.exp(raw_scores - log_total[:, :, None]), 0.0).astype(
            jnp.bfloat16
        )
        return (
            running
            + jnp.einsum("hqk,khd->qhd", prob_rows, blocks[2], preferred_element_type=jnp.float32),
            None,
        )

    mixed, unused = lax.scan(
        outputs_of, jnp.zeros(queries.shape, jnp.float32), (key_blocks, id_blocks, val_blocks)
    )
    return (mixed, log_total)


def attend_backward(
    queries, key_all, val_all, ids_query, ids_keys, log_total, grad_mixed, delta_rows
):
    block_len = min(512, FR)
    score_scale = 1.0 / math.sqrt(HD)
    key_blocks = split_blocks(key_all, block_len)
    val_blocks = split_blocks(val_all, block_len)
    id_blocks = split_blocks(ids_keys, block_len)

    def step_back(grad_query, blocks):
        key_block, id_block, val_block = blocks
        raw_scores, same_clip = block_scores(queries, key_block, ids_query, id_block)
        prob_rows = jnp.where(same_clip, jnp.exp(raw_scores - log_total[:, :, None]), 0.0)
        grad_val = jnp.einsum(
            "hqk,qhd->khd",
            prob_rows.astype(jnp.bfloat16),
            grad_mixed,
            preferred_element_type=jnp.float32,
        )
        grad_prob = jnp.einsum(
            "qhd,khd->hqk", grad_mixed, val_block, preferred_element_type=jnp.float32
        )
        grad_score = (prob_rows * (grad_prob - delta_rows[:, :, None])).astype(jnp.bfloat16)
        grad_query = (
            grad_query
            + jnp.einsum("hqk,khd->qhd", grad_score, key_block, preferred_element_type=jnp.float32)
            * score_scale
        )
        grad_key = (
            jnp.einsum("hqk,qhd->khd", grad_score, queries, preferred_element_type=jnp.float32)
            * score_scale
        )
        return (grad_query, (grad_key, grad_val))

    grad_query, grad_blocks = lax.scan(
        step_back, jnp.zeros(queries.shape, jnp.float32), (key_blocks, id_blocks, val_blocks)
    )
    key_count = key_all.shape[0]
    return (
        grad_query,
        grad_blocks[0].reshape(key_count, -1),
        grad_blocks[1].reshape(key_count, -1),
    )


def per_device(
    frames, cotangent, segment_ids, w_qkv, w_out, w_fc1, w_fc2, bias_qv, bias_fc1, norm_vectors
):
    dp_place = lax.axis_index("dp")
    local_width = w_qkv.shape[2]
    head_count = local_width // HD
    edge_rows = FR
    key_count = 2 * edge_rows + (2 * REACH - 1) * FR
    vectors = norm_vectors.astype(jnp.float32)
    biases_qv = bias_qv.astype(jnp.float32)
    biases_fc1 = bias_fc1.astype(jnp.float32)
    weights = (w_qkv, w_out, w_fc1, w_fc2)
    totals = tuple((jnp.zeros((D,) + weight.shape[1:], jnp.float32) for weight in weights))
    owned = tuple((jnp.zeros(weight.shape, jnp.float32) for weight in weights))
    grad_bias_qv = jnp.zeros((2, local_width), jnp.float32)
    grad_bias_fc1 = jnp.zeros(bias_fc1.shape, jnp.float32)
    grad_norm = jnp.zeros(vectors.shape, jnp.float32)
    outputs = []
    inputs_grad = []
    for number in range(MB):
        qkv_all, out_all, fc1_all, fc2_all = (
            lax.all_gather(weights[0], "dp", axis=0, tiled=True),
            lax.all_gather(weights[1], "dp", axis=0, tiled=True),
            lax.all_gather(weights[2], "dp", axis=0, tiled=True),
            lax.all_gather(weights[3], "dp", axis=0, tiled=True),
        )
        frame_rows = frames[number].astype(jnp.float32)
        normed_one = norm_rows(frame_rows, vectors[0], vectors[1]).astype(jnp.bfloat16)
        inputs_one = collect_rows(normed_one)
        projected = jnp.einsum(
            "sd,dtc->stc", inputs_one, qkv_all, preferred_element_type=jnp.float32
        )
        queries = (projected[:, 0] + biases_qv[0]).astype(jnp.bfloat16)
        key_rows = projected[:, 1].astype(jnp.bfloat16)
        val_rows = (projected[:, 2] + biases_qv[1]).astype(jnp.bfloat16)
        near_pair = gather_near(key_rows, val_rows)
        key_all = near_pair[0].reshape(key_count, head_count, HD)
        val_all = near_pair[1].reshape(key_count, head_count, HD)
        clip_ids = segment_ids[number]
        padded_ids = jnp.pad(clip_ids, (REACH * FR, REACH * FR), constant_values=-1)
        ids_keys = lax.dynamic_slice_in_dim(padded_ids, dp_place * FR + (FR - edge_rows), key_count)
        ids_query = lax.dynamic_slice_in_dim(clip_ids, dp_place * FR, FR)
        query_heads = queries.reshape(FR, head_count, HD)
        mixed_exact, log_total = attend_forward(query_heads, key_all, val_all, ids_query, ids_keys)
        mixed = mixed_exact.astype(jnp.bfloat16).reshape(FR, local_width)
        middle = (
            frame_rows
            + share_sums(
                jnp.einsum("sc,dc->sd", mixed, out_all, preferred_element_type=jnp.float32)
            )
            + vectors[4]
        )
        normed_two = norm_rows(middle, vectors[2], vectors[3]).astype(jnp.bfloat16)
        inputs_two = collect_rows(normed_two)
        hidden = jnp.dot(inputs_two, fc1_all, preferred_element_type=jnp.float32) + biases_fc1
        active = gelu_exact(hidden).astype(jnp.bfloat16)
        result = (
            middle
            + share_sums(
                jnp.einsum("sf,df->sd", active, fc2_all, preferred_element_type=jnp.float32)
            )
            + vectors[5]
        )
        outputs.append(result.astype(jnp.bfloat16))
        qkv_all, out_all, fc1_all, fc2_all = (
            lax.all_gather(weights[0], "dp", axis=0, tiled=True),
            lax.all_gather(weights[1], "dp", axis=0, tiled=True),
            lax.all_gather(weights[2], "dp", axis=0, tiled=True),
            lax.all_gather(weights[3], "dp", axis=0, tiled=True),
        )
        grad_rows = cotangent[number].astype(jnp.float32)
        grad_two = collect_grads(grad_rows.astype(jnp.bfloat16))
        term_fc2 = jnp.einsum("sd,sf->df", grad_two, active, preferred_element_type=jnp.float32)
        grad_active = jnp.einsum("sd,df->sf", grad_two, fc2_all, preferred_element_type=jnp.float32)
        unused, gelu_pull = jax.vjp(gelu_exact, hidden)
        grad_hidden = gelu_pull(grad_active)[0].astype(jnp.bfloat16)
        grad_bias_fc1 = grad_bias_fc1 + jnp.sum(grad_hidden, axis=0, dtype=jnp.float32)
        term_fc1 = jnp.einsum(
            "sd,sf->df", inputs_two, grad_hidden, preferred_element_type=jnp.float32
        )
        grad_normed_two = share_grads(
            jnp.einsum("sf,df->sd", grad_hidden, fc1_all, preferred_element_type=jnp.float32)
        )
        unused, norm_pull_two = jax.vjp(norm_rows, middle, vectors[2], vectors[3])
        grad_middle_part, gain_two, shift_two = norm_pull_two(grad_normed_two)
        grad_middle = grad_rows + grad_middle_part
        grad_one = collect_grads(grad_middle.astype(jnp.bfloat16))
        term_out = jnp.einsum("sd,sc->dc", grad_one, mixed, preferred_element_type=jnp.float32)
        grad_mixed = jnp.einsum(
            "sd,dc->sc", grad_one, out_all, preferred_element_type=jnp.float32
        ).astype(jnp.bfloat16)
        grad_heads = grad_mixed.reshape(FR, head_count, HD)
        delta_rows = jnp.einsum(
            "qhd,qhd->hq", grad_heads, mixed_exact, preferred_element_type=jnp.float32
        )
        grad_query, grad_keys, grad_vals = attend_backward(
            query_heads, key_all, val_all, ids_query, ids_keys, log_total, grad_heads, delta_rows
        )
        own_pair = scatter_near(jnp.stack((grad_keys, grad_vals)), edge_rows)
        grad_proj = jnp.stack(
            (
                grad_query.reshape(FR, local_width).astype(jnp.bfloat16),
                own_pair[0].astype(jnp.bfloat16),
                own_pair[1].astype(jnp.bfloat16),
            ),
            axis=1,
        )
        grad_bias_qv = grad_bias_qv + jnp.sum(grad_proj[:, 0::2], axis=0, dtype=jnp.float32)
        term_qkv = jnp.einsum(
            "sd,stc->dtc", inputs_one, grad_proj, preferred_element_type=jnp.float32
        )
        grad_normed_one = share_grads(
            jnp.einsum("stc,dtc->sd", grad_proj, qkv_all, preferred_element_type=jnp.float32)
        )
        unused, norm_pull_one = jax.vjp(norm_rows, frame_rows, vectors[0], vectors[1])
        grad_frame_part, gain_one, shift_one = norm_pull_one(grad_normed_one)
        inputs_grad.append(grad_middle + grad_frame_part)
        grad_norm = grad_norm + jnp.stack(
            (
                gain_one,
                shift_one,
                gain_two,
                shift_two,
                jnp.sum(grad_middle, axis=0),
                jnp.sum(grad_rows, axis=0),
            )
        )
        terms = (term_qkv, term_out, term_fc1, term_fc2)
        totals = tuple((running + update for running, update in zip(totals, terms)))
    owned = jax.tree.map(
        lambda part: part.astype(jnp.float32),
        lax.psum_scatter(shortened(totals), "dp", scatter_dimension=0, tiled=True),
    )
    bias_total = lax.psum((grad_bias_qv, grad_bias_fc1), "dp")
    norm_total = lax.psum(grad_norm, ("dp", "tensor"))
    return (
        jnp.stack(outputs),
        jnp.stack(inputs_grad),
        owned[0],
        owned[1],
        owned[2],
        owned[3],
        bias_total[0],
        bias_total[1],
        norm_total,
    )


def solution(mesh):
    in_specs = (
        P(None, ("dp", "tensor"), None),
        P(None, ("dp", "tensor"), None),
        P(),
        P("dp", None, "tensor"),
        P("dp", "tensor"),
        P("dp", "tensor"),
        P("dp", "tensor"),
        P(None, "tensor"),
        P("tensor"),
        P(),
    )
    out_specs = (
        P(None, ("dp", "tensor"), None),
        P(None, ("dp", "tensor"), None),
        P("dp", None, "tensor"),
        P("dp", "tensor"),
        P("dp", "tensor"),
        P("dp", "tensor"),
        P(None, "tensor"),
        P("tensor"),
        P(),
    )
    return jax.shard_map(
        per_device, mesh=mesh, in_specs=in_specs, out_specs=out_specs, check_vma=False
    )
```

profile of v0, /device:TPU:0, one launch (start us, length us, event | category | flops | bytes accessed | tf_op | source)
XLA Modules:
  0.0 3299.7 jit_solution(6152672970220381578)
XLA Ops:
  14.7 40.3 %all-gather.15.cloned.1.call-done = bf16[1024,1280]{1,0:T(8,128)(2,1)} async-done(((bf16[512,1280]{1,0:T(8,128)(2,1)}), bf16[1024,1280]{1,0:T(8,128)(2,1)}) %all-gather.15.cloned.1.call-update) | async-done | bytes 2621456 | tf_op jit(solution)/shard_map/all_gather | solution.py:45
  55.0 56.6 %all-gather.17.cloned.1.call-done = bf16[1280,3,640]{2,0,1:T(8,128)(2,1)} async-done(((bf16[80,3,640]{2,0,1:T(8,128)(2,1)}), bf16[1280,3,640]{2,0,1:T(8,128)(2,1)}) %all-gather.17.cloned.1.call-update) | async-done | bytes 4915216 | tf_op jit(solution)/shard_map/all_gather | solution.py:227
  136.9 134.6 %collective-permute-done = bf16[2,1024,640]{1,2,0:T(8,128)(2,1)} collective-permute-done((bf16[2,1024,640]{1,2,0:T(8,128)(2,1)}, bf16[2,1024,640]{1,2,0:T(8,128)(2,1)}, u32[]{:S(2)}, u32[]{:S(2)}) %collective-permute-start) | collective-permute-done | bytes 2621472 | tf_op jit(solution)/shard_map/ppermute | solution.py:22
  309.2 187.7 %while.78 = (s32[]{:T(128)}, f32[8,1024]{1,0:T(8,128)S(1)}, f32[8,1024]{1,0:T(8,128)S(1)}, s32[1024]{0:T(1024)S(1)}, s32[10,512]{1,0:T(8,128)S(1)}, /*index=5*/b...) while((s32[]{:T(128)}, f32[8,1024]{1,0:T(8,128)S(1)}, ...), condition=%wide.region_5.6_spmd.clone, body=%wide.region_2.5_spmd.clone.sunk | while | flops 705208320 | bytes 37530216 | solution.py:139
  521.0 94.3 %while.79 = (s32[]{:T(128)}, f32[1024,8,80]{0,2,1:T(8,128)}, bf16[10,512,8,80]{1,3,2,0:T(8,128)(2,1)}, s32[1024]{0:T(1024)S(1)}, s32[10,512]{1,0:T(8,128)S(1)}, ...) while((s32[]{:T(128)}, f32[1024,8,80]{0,2,1:T(8,128)}, ...), condition=%wide.region_7.8_spmd.clone, body=%wide.region_6.7_spmd.clone.sunk | while | flops 1360789504 | bytes 8957043 | solution.py:155
  624.4 62.7 %reduce-scatter.15.cloned.1.call-done = bf16[512,1280]{1,0:T(8,128)(2,1)} async-done(((bf16[1024,1280]{1,0:T(8,128)(2,1)}), bf16[512,1280]{1,0:T(8,128)(2,1)}) %reduce-scatter.15.cloned.1.call-update) | async-done | bytes 1310736 | tf_op jit(solution)/shard_map/reduce_scatter | solution.py:49
  690.9 39.1 %all-gather.27.cloned.1.call-done = bf16[1024,1280]{1,0:T(8,128)(2,1)} async-done(((bf16[512,1280]{1,0:T(8,128)(2,1)}), bf16[1024,1280]{1,0:T(8,128)(2,1)}) %all-gather.27.cloned.1.call-update) | async-done | bytes 2621456 | tf_op jit(solution)/shard_map/all_gather | solution.py:45
  755.2 131.5 %collective-permute-done.4 = bf16[2,1024,640]{1,2,0:T(8,128)(2,1)} collective-permute-done((bf16[2,1024,640]{1,2,0:T(8,128)(2,1)}, bf16[2,1024,640]{1,2,0:T(8,128)(2,1)}, u32[]{:S(2)}, u32[]{:S(2)}) %collective-permute-start.4) | collective-permute-done | bytes 2621472 | tf_op jit(solution)/shard_map/ppermute | solution.py:22
  924.3 187.7 %while.80 = (s32[]{:T(128)}, f32[8,1024]{1,0:T(8,128)S(1)}, f32[8,1024]{1,0:T(8,128)S(1)}, s32[1024]{0:T(1024)S(1)}, s32[10,512]{1,0:T(8,128)S(1)}, /*index=5*/b...) while((s32[]{:T(128)}, f32[8,1024]{1,0:T(8,128)S(1)}, ...), condition=%wide.region_17.18_spmd.clone, body=%wide.region_14.17_spmd.clone.sunk | while | flops 705208320 | bytes 37530216 | solution.py:139
  1136.2 94.4 %while.81 = (s32[]{:T(128)}, f32[1024,8,80]{0,2,1:T(8,128)}, bf16[10,512,8,80]{1,3,2,0:T(8,128)(2,1)}, s32[1024]{0:T(1024)S(1)}, s32[10,512]{1,0:T(8,128)S(1)}, ...) while((s32[]{:T(128)}, f32[1024,8,80]{0,2,1:T(8,128)}, ...), condition=%wide.region_19.20_spmd.clone, body=%wide.region_18.19_spmd.clone.sunk | while | flops 1360789504 | bytes 8957043 | solution.py:155
  1238.6 61.3 %reduce-scatter.19.cloned.1.call-done = bf16[512,1280]{1,0:T(8,128)(2,1)} async-done(((bf16[1024,1280]{1,0:T(8,128)(2,1)}), bf16[512,1280]{1,0:T(8,128)(2,1)}) %reduce-scatter.19.cloned.1.call-update) | async-done | bytes 1310736 | tf_op jit(solution)/shard_map/reduce_scatter | solution.py:49
  1311.9 53.8 %all-gather.23.cloned.1.call-done = bf16[1280,2560]{1,0:T(8,128)(2,1)} async-done(((bf16[80,2560]{1,0:T(8,128)(2,1)}), bf16[1280,2560]{1,0:T(8,128)(2,1)}) %all-gather.23.cloned.1.call-update) | async-done | bytes 6553616 | tf_op jit(solution)/shard_map/all_gather | solution.py:229
  1365.6 39.2 %all-gather.29.cloned.1.call-done = bf16[1024,1280]{1,0:T(8,128)(2,1)} async-done(((bf16[512,1280]{1,0:T(8,128)(2,1)}), bf16[1024,1280]{1,0:T(8,128)(2,1)}) %all-gather.29.cloned.1.call-update) | async-done | bytes 2621456 | tf_op jit(solution)/shard_map/all_gather | solution.py:45
  1417.5 28.4 all-gather.21.cloned.1.call-done
  1446.0 55.9 %multiply_convert_fusion.1 = (bf16[1024,2560]{1,0:T(8,128)(2,1)}, f32[1024,2560]{1,0:T(8,128)}, bf16[1024,2560]{1,0:T(8,128)(2,1)}, f32[1024,2560]{1,0:T(8,128)}, f32[1024,2560]{1,0:T(8,128)}) fusion(f32[2560]{0:T(1024)S(1)} %convert_element_type.346, f32[1024,2560]{1,0:T(8,128)} %fusion.200, bf16[1024,1280]{1,0:T(8,128)(2,1)} %all-gather.21.cloned.1.call-done, ...), kind=kOutput, calls=%fused_computation.127 | convolution fusion | flops 7056916480 | bytes 61614080 | tf_op jit(solution)/shard_map/dot_general | solution.py:260
  1501.9 50.2 %all-gather.25.cloned.1.call-done = bf16[1280,2560]{1,0:T(8,128)(2,1)} async-done(((bf16[80,2560]{1,0:T(8,128)(2,1)}), bf16[1280,2560]{1,0:T(8,128)(2,1)}) %all-gather.25.cloned.1.call-update) | async-done | bytes 6553616 | tf_op jit(solution)/shard_map/all_gather | solution.py:230
  1552.2 20.0 convert_reduce_fusion
  1646.5 24.4 reduce-scatter.23.cloned.1.call-done
  1670.8 39.7 %reduce-scatter.17.cloned.1.call-done = bf16[512,1280]{1,0:T(8,128)(2,1)} async-done(((bf16[1024,1280]{1,0:T(8,128)(2,1)}), bf16[512,1280]{1,0:T(8,128)(2,1)}) %reduce-scatter.17.cloned.1.call-update) | async-done | bytes 1310736 | tf_op jit(solution)/shard_map/reduce_scatter | solution.py:49
  1716.4 34.0 %reduce-scatter.21.cloned.1.call-done = bf16[512,1280]{1,0:T(8,128)(2,1)} async-done(((bf16[1024,1280]{1,0:T(8,128)(2,1)}), bf16[512,1280]{1,0:T(8,128)(2,1)}) %reduce-scatter.21.cloned.1.call-update) | async-done | bytes 1310736 | tf_op jit(solution)/shard_map/reduce_scatter | solution.py:49
  1839.5 412.7 %while.83 = (s32[]{:T(128)}, f32[1024,8,80]{0,2,1:T(8,128)}, f32[10,512,8,80]{1,3,2,0:T(8,128)}, f32[10,512,8,80]{1,3,2,0:T(8,128)}, bf16[10,512,8,80]{1,3,2,0:T...) while((s32[]{:T(128)}, f32[1024,8,80]{0,2,1:T(8,128)}, ...), condition=%wide.region_36.37_spmd.clone, body=%wide.region_35.36_spmd.clone.sunk | while | flops 3400204288 | bytes 180335360 | solution.py:195
  2252.2 19.6 copy.100
  2271.8 19.4 stack_reshape.14
  2301.5 19.4 copy.101
  2320.9 19.4 stack_reshape.15
  2393.8 406.3 %while.82 = (s32[]{:T(128)}, f32[1024,8,80]{0,2,1:T(8,128)}, f32[10,512,8,80]{1,3,2,0:T(8,128)}, f32[10,512,8,80]{1,3,2,0:T(8,128)}, bf16[10,512,8,80]{1,3,2,0:T...) while((s32[]{:T(128)}, f32[1024,8,80]{0,2,1:T(8,128)}, ...), condition=%wide.region_28.29_spmd.clone, body=%wide.region_27.28_spmd.clone.sunk | while | flops 3400204288 | bytes 180335360 | solution.py:195
  2806.2 19.4 copy.95
  2845.0 19.4 copy.96
  2864.4 19.5 stack_reshape.13
  2967.6 134.8 %collective-permute-done.11 = bf16[2,1024,640]{2,1,0:T(8,128)(2,1)} collective-permute-done((bf16[2,1024,640]{2,1,0:T(8,128)(2,1)}, bf16[2,1024,640]{2,1,0:T(8,128)(2,1)}, u32[]{:S(2)}, u32[]{:S(2)}) %collective-permute-start.11) | collective-permute-done | bytes 2621472 | tf_op jit(solution)/shard_map/ppermute | solution.py:22
  3152.1 86.2 %all-reduce.2 = (f32[2,640]{1,0:T(2,128)}, f32[2560]{0:T(1024)}) all-reduce(f32[2,640]{1,0:T(2,128)S(1)} %add.379, f32[2560]{0:T(1024)S(1)} %add.380), channel_id=1, replica_groups=mesh['dp'=16,'tensor'=2] {'dp'}, use_global_device_ids=true, to_apply=%region_46.47 | all-reduce | flops 3840 | bytes 30720 | tf_op jit(solution)/shard_map/psum | solution.py:339
  3245.0 38.8 %psum.23 = f32[6,1280]{1,0:T(8,128)} all-reduce(f32[6,1280]{1,0:T(8,128)S(1)} %add.381), channel_id=1, replica_groups=mesh['dp'=16,'tensor'=2] {'dp','tensor'}, use_global_device_ids=true, to_apply=%region_62.63 | all-reduce | flops 7680 | bytes 61440 | tf_op jit(solution)/shard_map/psum | solution.py:340
  (934 shorter events, 2012.4 us)
Async XLA Ops:
  13.8 604.4 %all-gather.19.cloned.1.call-start = ((), (), s32[]{:S(2)}) async-start(), calls=%async_computation.14 | async-start | bytes 1740800 | tf_op jit(solution)/shard_map/all_gather | solution.py:228
  14.6 672.4 %reduce-scatter.15.cloned.1.call-start = ((), (), s32[]{:S(2)}) async-start(), calls=%async_computation.15 | async-start | bytes 3932160 | tf_op jit(solution)/shard_map/reduce_scatter | solution.py:49
  122.9 148.6 %collective-permute-start = (bf16[2,1024,640]{1,2,0:T(8,128)(2,1)}, bf16[2,1024,640]{1,2,0:T(8,128)(2,1)}, u32[]{:S(2)}, u32[]{:S(2)}) collective-permute-start(bf16[2,1024,640]{1,2,0:T(8,128)(2,1)} %pad_maximum_fusion.3), channel_id=1, source_target_pairs={{0,4},{2,6},{4,8},{6,10},{8,12},{10,14},{12,16},{14,18},{16,20},{1... | collective-permute-start | bytes 7864328 | tf_op jit(solution)/shard_map/ppermute | solution.py:22
  126.9 146.7 %collective-permute-start.1 = (bf16[2,1024,640]{1,2,0:T(8,128)(2,1)}, bf16[2,1024,640]{1,2,0:T(8,128)(2,1)}, u32[]{:S(2)}, u32[]{:S(2)}) collective-permute-start(bf16[2,1024,640]{1,2,0:T(8,128)(2,1)} %pad_maximum_fusion.3), channel_id=1, source_target_pairs={{0,2},{2,4},{4,6},{6,8},{8,10},{10,12},{12,14},{14,16},{16,18},{18... | collective-permute-start | bytes 7864328 | tf_op jit(solution)/shard_map/ppermute | solution.py:22
  130.3 146.0 %collective-permute-start.2 = (bf16[2,1024,640]{1,2,0:T(8,128)(2,1)}, bf16[2,1024,640]{1,2,0:T(8,128)(2,1)}, u32[]{:S(2)}, u32[]{:S(2)}) collective-permute-start(bf16[2,1024,640]{1,2,0:T(8,128)(2,1)} %pad_maximum_fusion.3), channel_id=1, source_target_pairs={{2,0},{4,2},{6,4},{8,6},{10,8},{12,10},{14,12},{16,14},{18,16},{20... | collective-permute-start | bytes 7864328 | tf_op jit(solution)/shard_map/ppermute | solution.py:22
  131.6 146.7 %collective-permute-start.3 = (bf16[2,1024,640]{1,2,0:T(8,128)(2,1)}, bf16[2,1024,640]{1,2,0:T(8,128)(2,1)}, u32[]{:S(2)}, u32[]{:S(2)}) collective-permute-start(bf16[2,1024,640]{1,2,0:T(8,128)(2,1)} %pad_maximum_fusion.3), channel_id=1, source_target_pairs={{4,0},{6,2},{8,4},{10,6},{12,8},{14,10},{16,12},{18,14},{20,16},{2... | collective-permute-start | bytes 7864328 | tf_op jit(solution)/shard_map/ppermute | solution.py:22
  690.9 609.1 %reduce-scatter.19.cloned.1.call-start = ((), (), s32[]{:S(2)}) async-start(), calls=%async_computation.21 | async-start | bytes 3932160 | tf_op jit(solution)/shard_map/reduce_scatter | solution.py:49
  741.4 145.2 %collective-permute-start.4 = (bf16[2,1024,640]{1,2,0:T(8,128)(2,1)}, bf16[2,1024,640]{1,2,0:T(8,128)(2,1)}, u32[]{:S(2)}, u32[]{:S(2)}) collective-permute-start(bf16[2,1024,640]{1,2,0:T(8,128)(2,1)} %pad_maximum_fusion.4), channel_id=1, source_target_pairs={{0,4},{2,6},{4,8},{6,10},{8,12},{10,14},{12,16},{14,18},{16,20},{1... | collective-permute-start | bytes 7864328 | tf_op jit(solution)/shard_map/ppermute | solution.py:22
  746.3 142.3 %collective-permute-start.5 = (bf16[2,1024,640]{1,2,0:T(8,128)(2,1)}, bf16[2,1024,640]{1,2,0:T(8,128)(2,1)}, u32[]{:S(2)}, u32[]{:S(2)}) collective-permute-start(bf16[2,1024,640]{1,2,0:T(8,128)(2,1)} %pad_maximum_fusion.4), channel_id=1, source_target_pairs={{0,2},{2,4},{4,6},{6,8},{8,10},{10,12},{12,14},{14,16},{16,18},{18... | collective-permute-start | bytes 7864328 | tf_op jit(solution)/shard_map/ppermute | solution.py:22
  749.3 142.1 %collective-permute-start.6 = (bf16[2,1024,640]{1,2,0:T(8,128)(2,1)}, bf16[2,1024,640]{1,2,0:T(8,128)(2,1)}, u32[]{:S(2)}, u32[]{:S(2)}) collective-permute-start(bf16[2,1024,640]{1,2,0:T(8,128)(2,1)} %pad_maximum_fusion.4), channel_id=1, source_target_pairs={{2,0},{4,2},{6,4},{8,6},{10,8},{12,10},{14,12},{16,14},{18,16},{20... | collective-permute-start | bytes 7864328 | tf_op jit(solution)/shard_map/ppermute | solution.py:22
  750.6 142.8 %collective-permute-start.7 = (bf16[2,1024,640]{1,2,0:T(8,128)(2,1)}, bf16[2,1024,640]{1,2,0:T(8,128)(2,1)}, u32[]{:S(2)}, u32[]{:S(2)}) collective-permute-start(bf16[2,1024,640]{1,2,0:T(8,128)(2,1)} %pad_maximum_fusion.4), channel_id=1, source_target_pairs={{4,0},{6,2},{8,4},{10,6},{12,8},{14,10},{16,12},{18,14},{20,16},{2... | collective-permute-start | bytes 7864328 | tf_op jit(solution)/shard_map/ppermute | solution.py:22
  1238.4 166.4 %all-gather.29.cloned.1.call-start = ((), (), s32[]{:S(2)}) async-start(), calls=%async_computation.22 | async-start | bytes 3932160 | tf_op jit(solution)/shard_map/all_gather | solution.py:45
  1307.1 138.9 %all-gather.21.cloned.1.call-start = ((), (), s32[]{:S(2)}) async-start(), calls=%async_computation.16 | async-start | bytes 3932160 | tf_op jit(solution)/shard_map/all_gather | solution.py:45
  1307.8 194.1 %all-gather.37.cloned.1.call-start = ((), (), s32[]{:S(2)}) async-start(), calls=%async_computation.34 | async-start | bytes 3932160 | tf_op jit(solution)/shard_map/all_gather | solution.py:55
  1310.5 241.7 %all-gather.25.cloned.1.call-start = ((), (), s32[]{:S(2)}) async-start(), calls=%async_computation.18 | async-start | bytes 6963200 | tf_op jit(solution)/shard_map/all_gather | solution.py:230
  1311.2 279.9 %all-gather.35.cloned.1.call-start = ((), (), s32[]{:S(2)}) async-start(), calls=%async_computation.33 | async-start | bytes 3932160 | tf_op jit(solution)/shard_map/all_gather | solution.py:55
  1311.8 334.7 %reduce-scatter.27.cloned.1.call-start = ((), (), s32[]{:S(2)}) async-start(), calls=%async_computation.27 | async-start | bytes 3932160 | tf_op jit(solution)/shard_map/reduce_scatter | solution.py:59
  1646.4 175.0 %all-gather.33.cloned.1.call-start = ((), (), s32[]{:S(2)}) async-start(), calls=%async_computation.28 | async-start | bytes 3932160 | tf_op jit(solution)/shard_map/all_gather | solution.py:55
  1764.8 611.1 %all-gather.31.cloned.1.call-start = ((), (), s32[]{:S(2)}) async-start(), calls=%async_computation.25 | async-start | bytes 3932160 | tf_op jit(solution)/shard_map/all_gather | solution.py:55
  1767.1 1374.9 %reduce-scatter.37.cloned.1.call-start = ((), (), s32[]{:S(2)}) async-start(), calls=%async_computation.35 | async-start | bytes 6963200
  1798.1 1346.5 %reduce-scatter.35.cloned.1.call-start = ((), (), s32[]{:S(2)}) async-start(), calls=%async_computation.32 | async-start | bytes 6963200 | tf_op jit(solution)/shard_map/reduce_scatter | solution.py:337
  1821.3 1325.2 %reduce-scatter.33.cloned.1.call-start = ((), (), s32[]{:S(2)}) async-start(), calls=%async_computation.31 | async-start | bytes 1740800 | tf_op jit(solution)/shard_map/reduce_scatter | solution.py:337
  2363.9 564.3 %collective-permute-start.12 = (bf16[2,1024,640]{2,1,0:T(8,128)(2,1)}, bf16[2,1024,640]{2,1,0:T(8,128)(2,1)}, u32[]{:S(2)}, u32[]{:S(2)}) collective-permute-start(bf16[2,1024,640]{2,1,0:T(8,128)(2,1)} %get-tuple-element.840), channel_id=1, source_target_pairs={{4,0},{6,2},{8,4},{10,6},{12,8},{14,10},{16,12},{18,14},{20,16},{2... | collective-permute-start | bytes 7864328 | tf_op jit(solution)/shard_map/ppermute | solution.py:22
  2365.2 563.0 %collective-permute-start.13 = (bf16[2,1024,640]{2,1,0:T(8,128)(2,1)}, bf16[2,1024,640]{2,1,0:T(8,128)(2,1)}, u32[]{:S(2)}, u32[]{:S(2)}) collective-permute-start(bf16[2,1024,640]{2,1,0:T(8,128)(2,1)} %get-tuple-element.843), channel_id=1, source_target_pairs={{2,0},{4,2},{6,4},{8,6},{10,8},{12,10},{14,12},{16,14},{18,16},{20... | collective-permute-start | bytes 7864328 | tf_op jit(solution)/shard_map/ppermute | solution.py:22
  2366.5 561.7 %collective-permute-start.14 = (bf16[2,1024,640]{2,1,0:T(8,128)(2,1)}, bf16[2,1024,640]{2,1,0:T(8,128)(2,1)}, u32[]{:S(2)}, u32[]{:S(2)}) collective-permute-start(bf16[2,1024,640]{2,1,0:T(8,128)(2,1)} %get-tuple-element.842), channel_id=1, source_target_pairs={{0,2},{2,4},{4,6},{6,8},{8,10},{10,12},{12,14},{14,16},{16,18},{18... | collective-permute-start | bytes 7864328 | tf_op jit(solution)/shard_map/ppermute | solution.py:22
  2371.1 557.2 %collective-permute-start.15 = (bf16[2,1024,640]{2,1,0:T(8,128)(2,1)}, bf16[2,1024,640]{2,1,0:T(8,128)(2,1)}, u32[]{:S(2)}, u32[]{:S(2)}) collective-permute-start(bf16[2,1024,640]{2,1,0:T(8,128)(2,1)} %get-tuple-element.841), channel_id=1, source_target_pairs={{0,4},{2,6},{4,8},{6,10},{8,12},{10,14},{12,16},{14,18},{16,20},{1... | collective-permute-start | bytes 7864328 | tf_op jit(solution)/shard_map/ppermute | solution.py:22
  2890.1 348.3 %reduce-scatter.29.cloned.1.call-start = ((), (), s32[]{:S(2)}) async-start(), calls=%async_computation.29 | async-start | bytes 3932160 | tf_op jit(solution)/shard_map/reduce_scatter | solution.py:59
  2946.6 291.8 %reduce-scatter.25.cloned.1.call-start = ((), (), s32[]{:S(2)}) async-start(), calls=%async_computation.26 | async-start | bytes 3932160 | tf_op jit(solution)/shard_map/reduce_scatter | solution.py:59
  2959.2 143.2 %collective-permute-start.11 = (bf16[2,1024,640]{2,1,0:T(8,128)(2,1)}, bf16[2,1024,640]{2,1,0:T(8,128)(2,1)}, u32[]{:S(2)}, u32[]{:S(2)}) collective-permute-start(bf16[2,1024,640]{2,1,0:T(8,128)(2,1)} %get-tuple-element.837), channel_id=1, source_target_pairs={{0,4},{2,6},{4,8},{6,10},{8,12},{10,14},{12,16},{14,18},{16,20},{1... | collective-permute-start | bytes 7864328 | tf_op jit(solution)/shard_map/ppermute | solution.py:22
  2962.0 140.4 %collective-permute-start.8 = (bf16[2,1024,640]{2,1,0:T(8,128)(2,1)}, bf16[2,1024,640]{2,1,0:T(8,128)(2,1)}, u32[]{:S(2)}, u32[]{:S(2)}) collective-permute-start(bf16[2,1024,640]{2,1,0:T(8,128)(2,1)} %get-tuple-element.836), channel_id=1, source_target_pairs={{4,0},{6,2},{8,4},{10,6},{12,8},{14,10},{16,12},{18,14},{20,16},{2... | collective-permute-start | bytes 7864328 | tf_op jit(solution)/shard_map/ppermute | solution.py:22
  2963.2 139.1 %collective-permute-start.9 = (bf16[2,1024,640]{2,1,0:T(8,128)(2,1)}, bf16[2,1024,640]{2,1,0:T(8,128)(2,1)}, u32[]{:S(2)}, u32[]{:S(2)}) collective-permute-start(bf16[2,1024,640]{2,1,0:T(8,128)(2,1)} %get-tuple-element.839), channel_id=1, source_target_pairs={{2,0},{4,2},{6,4},{8,6},{10,8},{12,10},{14,12},{16,14},{18,16},{20... | collective-permute-start | bytes 7864328 | tf_op jit(solution)/shard_map/ppermute | solution.py:22
  3120.5 170.3 %reduce-scatter.31.cloned.1.call-start = ((), (), s32[]{:S(2)}) async-start(), calls=%async_computation.30 | async-start | bytes 5222400 | tf_op jit(solution)/shard_map/reduce_scatter | solution.py:337
  (181 other events, 4927.9 us)
Sparse Core Ops, SparseCore 0:
  13.2 41.7 all-gather.14
  57.2 54.3 all-gather.16
  113.8 116.2 all-gather.18
  624.0 62.9 reduce-scatter.14
  691.0 39.0 all-gather.26
  1237.7 62.1 reduce-scatter.18
  1302.2 63.3 all-gather.22
  1367.2 37.5 all-gather.28
  1406.9 39.0 all-gather.20
  1447.4 39.0 all-gather.36
  1488.7 63.3 all-gather.24
  1553.5 37.5 all-gather.34
  1593.4 37.5 reduce-scatter.26
  1633.2 37.5 reduce-scatter.22
  1672.9 37.6 reduce-scatter.16
  1712.8 37.5 reduce-scatter.20
  1765.0 39.0 all-gather.32
  1805.4 39.0 all-gather.30
  1848.4 86.8 reduce-scatter.36
  1939.7 85.9 reduce-scatter.34
  2890.3 59.9 reduce-scatter.32
  2952.6 36.7 reduce-scatter.28
  3120.6 64.4 reduce-scatter.24
  3189.4 77.7 reduce-scatter.30
where the time goes:
time: 3320 us; the launch traced here: 3300 us
  matrix products  1430 us (43%)
  waiting for transfers between devices  943 us (28%)
  local copies, waits for them, and re-layouts  444 us (13%)
  other arithmetic  293 us (9%)
  blocking collectives  125 us (4%)
  starting transfers between devices  44.6 us (1%)
    ppermute x16, waiting for transfers between devices, passed_along(): return lax.ppermute(x, axis, pairs)  401 us
    dot_general x40, matrix products, block_scores(): jnp.einsum('qhd,khd->hqk', queries, key_block, preferred_element_type=jnp...  286 us
    dot_general x20, matrix products, step_back(): jnp.einsum('hqk,qhd->khd', prob_rows.astype(jnp.bfloat16), grad_mixed, pr...  217 us
    dot_general x20, matrix products, step_back(): jnp.einsum('qhd,khd->hqk', grad_mixed, val_block, preferred_element_type=...  210 us
    reduce_scatter x4, waiting for transfers between devices, share_sums(): lax.psum_scatter(values.astype(jnp.bfloat16), 'tensor', scatter_dimension...  198 us
    dot_general x20, matrix products, outputs_of(): jnp.einsum('hqk,khd->qhd', prob_rows, blocks[2], preferred_element_type=j...  181 us
    reduce_sum x20, other arithmetic, statistics(): jnp.sum(expo_rows, axis=-1)  158 us
    dot_general x20, matrix products, step_back(): jnp.einsum('hqk,qhd->khd', grad_score, queries, preferred_element_type=jn...  150 us
  transfers between devices with their start and end apart: 40, of which 16 were waited for; matrix products, arithmetic and copies ran while one was open for 52% of the time, Pallas kernels for 0%

commit v1 on v0

v1 whole, which is shorter than its diff:
```python
import functools
import math

import jax
import jax.numpy as jnp
from jax import lax
from jax.experimental import pallas as pl
from jax.experimental.pallas import tpu as pltpu
from jax.sharding import PartitionSpec as P

HD = 80
MB = 2
EDGE = 512
EPSILON = 1e-05
NEGATIVE = -1e30
LOG2E = math.log2(math.e)
SCALE = 1.0 / math.sqrt(HD)
BF = jnp.bfloat16
F32 = jnp.float32


def head_spans(heads):
    spans = []
    for head in range(heads):
        first, last = head * HD, (head + 1) * HD
        start = first // 128 * 128
        spans.append((start, -(-last // 128) * 128 - start, first - start))
    return spans


def dot_on(a, b, a_dim, b_dim):
    return lax.dot_general(a, b, (((a_dim,), (b_dim,)), ((), ())), preferred_element_type=F32)


def in_head(rows, width, offset):
    lane = lax.broadcasted_iota(jnp.int32, (rows, width), 1)
    return (lane >= offset) & (lane < offset + HD)


def head_ones(width, offset):
    return jnp.where(in_head(1, width, offset), 1.0, 0.0).astype(BF)


def window_parts(refs, swap):
    parts, base = [], 0
    for ref in refs:
        rows = ref.shape[0]
        if rows == EDGE:
            parts.append((ref, 0, base, rows))
        else:
            half = rows // 2
            parts.append((ref, 0, base + swap * half, half))
            parts.append((ref, half, base + (1 - swap) * half, half))
        base += rows
    return parts


def fetch_window(refs, swap, window, sems):
    copies = []
    for number, (ref, row, at, rows) in enumerate(window_parts(refs, swap)):
        copies.append(
            pltpu.make_async_copy(
                ref.at[pl.ds(row, rows)],
                window.at[pl.ds(pl.multiple_of(at, EDGE), rows)],
                sems.at[number],
            )
        )
        copies[-1].start()
    for copy in copies:
        copy.wait()


def forward_kernel(
    heads, W, QB, KB, lo_ref, count_ref, swap_ref, st_ref, en_ref, q_ref, l2, l1, own, r1, r2,
    o_ref, lse_ref, window, sems, top_s, sum_s, acc_s,
):
    fetch_window((l2, l1, own, r1, r2), swap_ref[0], window, sems)
    spans = head_spans(heads)

    def query_block(i, carry):
        r = pl.multiple_of(i * QB, QB)
        top_s[...] = jnp.full(top_s.shape, NEGATIVE, F32)
        sum_s[...] = jnp.zeros(sum_s.shape, F32)
        acc_s[...] = jnp.zeros(acc_s.shape, F32)
        st = st_ref[pl.ds(r, QB), :]
        en = en_ref[pl.ds(r, QB), :]

        def chunk(c, inner):
            k0 = pl.multiple_of(lo_ref[i] + c * KB, 16)
            at = k0 + lax.broadcasted_iota(jnp.int32, (QB, KB), 1)
            mask = (at >= st) & (at < en)
            for h in range(heads):
                t, w, off = spans[h]
                q = q_ref[pl.ds(r, QB), t : t + w] * head_ones(w, off)
                s = dot_on(q, window[pl.ds(k0, KB), t : t + w], 1, 1)
                s = jnp.where(mask, s, NEGATIVE)
                before = top_s[h]
                top = jnp.maximum(before, jnp.max(s, axis=1, keepdims=True))
                p = jnp.exp2(s - top)
                shrink = jnp.exp2(before - top)
                sum_s[h] = sum_s[h] * shrink + jnp.sum(p, axis=1, keepdims=True)
                acc_s[h, :, :w] = acc_s[h, :, :w] * shrink + dot_on(
                    p.astype(BF), window[pl.ds(k0, KB), W + t : W + t + w], 1, 0
                )
                top_s[h] = top
            return inner

        lax.fori_loop(0, count_ref[i], chunk, 0)
        for h in range(heads):
            t, w, off = spans[h]
            total = sum_s[h]
            o = (acc_s[h, :, :w] / total).astype(BF)
            o_ref[pl.ds(r, QB), t : t + w] = jnp.where(
                in_head(QB, w, off), o, o_ref[pl.ds(r, QB), t : t + w]
            )
            lse_ref[pl.ds(r, QB), h : h + 1] = top_s[h] + jnp.log2(total)
        return carry

    lax.fori_loop(0, q_ref.shape[0] // QB, query_block, 0)


SMEM = pl.BlockSpec(memory_space=pltpu.SMEM)
VMEM = pl.BlockSpec(memory_space=pltpu.VMEM)
ANY = pl.BlockSpec(memory_space=pl.ANY)


def attend_forward(q, pieces, ranges, swap, heads, QB=256, KB=768):
    st, en = ranges
    FR, W = q.shape
    rows = sum(p.shape[0] for p in pieces)
    lo, count = key_chunks(st, en, QB, KB, rows)
    flops = 2 * 2 * FR * 1792 * 256 * heads
    return pl.pallas_call(
        functools.partial(forward_kernel, heads, W, QB, KB),
        out_shape=(
            jax.ShapeDtypeStruct((FR, W), BF),
            jax.ShapeDtypeStruct((FR, heads), F32),
        ),
        in_specs=[SMEM] * 3 + [VMEM] * 3 + [ANY] * 5,
        out_specs=(VMEM, VMEM),
        scratch_shapes=[
            pltpu.VMEM((rows, 2 * W), BF),
            pltpu.SemaphoreType.DMA((8,)),
            pltpu.VMEM((heads, QB, 1), F32),
            pltpu.VMEM((heads, QB, 1), F32),
            pltpu.VMEM((heads, QB, 256), F32),
        ],
        compiler_params=pltpu.CompilerParams(vmem_limit_bytes=56 << 20),
        cost_estimate=pl.CostEstimate(flops=flops * 4, bytes_accessed=rows * W * 4, transcendentals=0),
        name="attend_forward",
    )(lo, count, swap[None], st[:, None], en[:, None], q, *pieces)


def backward_kernel(
    heads, W, QB, KB, lo_ref, count_ref, swap_ref, se_ref, lse_ref, delta_ref, q_ref, do_ref,
    l2, l1, own, r1, r2, dq_ref, g_l2, g_l1, g_own, g_r1, g_r2, window, grads, dq_s, sems,
):
    swap = swap_ref[0]
    fetch_window((l2, l1, own, r1, r2), swap, window, sems)
    spans = head_spans(heads)
    grads[...] = jnp.zeros(grads.shape, F32)

    def query_block(i, carry):
        r = pl.multiple_of(i * QB, QB)
        dq_s[...] = jnp.zeros(dq_s.shape, F32)
        st = se_ref[0:1, pl.ds(r, QB)]
        en = se_ref[1:2, pl.ds(r, QB)]

        def chunk(c, inner):
            k0 = pl.multiple_of(lo_ref[i] + c * KB, 16)
            at = k0 + lax.broadcasted_iota(jnp.int32, (KB, QB), 0)
            mask = (at >= st) & (at < en)
            for h in range(heads):
                t, w, off = spans[h]
                ones = head_ones(w, off)
                q = q_ref[pl.ds(r, QB), t : t + w] * ones
                do = do_ref[pl.ds(r, QB), t : t + w] * ones
                k = window[pl.ds(k0, KB), t : t + w]
                v = window[pl.ds(k0, KB), W + t : W + t + w]
                s = dot_on(k, q, 1, 1)
                p = jnp.exp2(jnp.where(mask, s - lse_ref[h : h + 1, pl.ds(r, QB)], NEGATIVE))
                dp = dot_on(v, do, 1, 1)
                ds = (p * (dp - delta_ref[h : h + 1, pl.ds(r, QB)])).astype(BF)
                grads[pl.ds(k0, KB), W + t : W + t + w] += dot_on(p.astype(BF), do, 1, 0)
                grads[pl.ds(k0, KB), t : t + w] += dot_on(ds, q, 1, 0)
                dq_s[h, :, :w] += dot_on(ds, k, 0, 0)
            return inner

        lax.fori_loop(0, count_ref[i], chunk, 0)
        for h in range(heads):
            t, w, off = spans[h]
            dq = (dq_s[h, :, :w] * SCALE).astype(BF)
            dq_ref[pl.ds(r, QB), t : t + w] = jnp.where(
                in_head(QB, w, off), dq, dq_ref[pl.ds(r, QB), t : t + w]
            )
        return carry

    lax.fori_loop(0, q_ref.shape[0] // QB, query_block, 0)
    for ref, row, at, rows in window_parts((g_l2, g_l1, g_own, g_r1, g_r2), swap):

        def store(j, carry, ref=ref, row=row, at=at):
            to = pl.multiple_of(row + j * 128, 128)
            here = pl.multiple_of(at + j * 128, 128)
            ref[pl.ds(to, 128), :W] = (grads[pl.ds(here, 128), :W] * math.log(2.0)).astype(BF)
            ref[pl.ds(to, 128), W:] = grads[pl.ds(here, 128), W:].astype(BF)
            return carry

        lax.fori_loop(0, rows // 128, store, 0)


def attend_backward(q, do, pieces, ranges, lse, delta, swap, heads, QB=256, KB=768):
    st, en = ranges
    FR, W = q.shape
    rows = sum(p.shape[0] for p in pieces)
    lo, count = key_chunks(st, en, QB, KB, rows)
    flops = 5 * 2 * FR * 1792 * 256 * heads
    return pl.pallas_call(
        functools.partial(backward_kernel, heads, W, QB, KB),
        out_shape=(jax.ShapeDtypeStruct((FR, W), BF),)
        + tuple(jax.ShapeDtypeStruct(p.shape, BF) for p in pieces),
        in_specs=[SMEM] * 3 + [VMEM] * 5 + [ANY] * 5,
        out_specs=(VMEM,) * 6,
        scratch_shapes=[
            pltpu.VMEM((rows, 2 * W), BF),
            pltpu.VMEM((rows, 2 * W), F32),
            pltpu.VMEM((heads, QB, 256), F32),
            pltpu.SemaphoreType.DMA((8,)),
        ],
        compiler_params=pltpu.CompilerParams(vmem_limit_bytes=60 << 20),
        cost_estimate=pl.CostEstimate(flops=flops * 2, bytes_accessed=rows * W * 8, transcendentals=0),
        name="attend_backward",
    )(lo, count, swap[None], jnp.stack((st, en)), lse, delta, q, do, *pieces)


def key_chunks(st, en, QB, KB, rows):
    lo = st[::QB] // 16 * 16
    count = (en[QB - 1 :: QB] - lo + KB - 1) // KB
    return jnp.minimum(lo, rows - count * KB), count


def over_dp(x, by):
    length = lax.axis_size("dp")
    pairs = [(i, i + by) for i in range(length) if 0 <= i + by < length]
    return lax.ppermute(x, "dp", pairs)


def partner(x):
    return lax.ppermute(x, "tensor", [(0, 1), (1, 0)])


def collect(x):
    if lax.axis_size("tensor") != 2:
        return lax.all_gather(x, "tensor", axis=0, tiled=True)
    return jnp.concatenate((x, partner(x)), axis=0)


def summed(parts):
    def product(first, last):
        return sum(dot_on(x[first:last], w, 1, dim) for x, w, dim in parts)

    rows = parts[0][0].shape[0]
    if lax.axis_size("tensor") != 2:
        whole = product(0, rows).astype(BF)
        return lax.psum_scatter(whole, "tensor", scatter_dimension=0, tiled=True).astype(F32)
    half = rows // 2
    received = partner(product(half, rows).astype(BF))
    return product(0, half) + received.astype(F32)


def norm_parts(x):
    centred = x - jnp.mean(x, axis=-1, keepdims=True)
    scale = lax.rsqrt(jnp.mean(centred * centred, axis=-1, keepdims=True) + EPSILON)
    return centred * scale, scale


def norm_back(grad, z, scale, gain):
    e = grad * gain
    mean_e = jnp.mean(e, axis=-1, keepdims=True)
    mean_ez = jnp.mean(e * z, axis=-1, keepdims=True)
    return scale * (e - mean_e - z * mean_ez)


def gelu_both(u):
    below = 0.5 * (1.0 + lax.erf(u * math.sqrt(0.5)))
    density = jnp.exp(-0.5 * u * u) * (1.0 / math.sqrt(2.0 * math.pi))
    return (u * below).astype(BF), (below + u * density).astype(BF)


def per_device(
    frames, cotangent, segment_ids, w_qkv, w_out, w_fc1, w_fc2, bias_qv, bias_fc1, norm_vectors
):
    dp_place = lax.axis_index("dp")
    paired = lax.axis_size("tensor") == 2
    swap = lax.axis_index("tensor").astype(jnp.int32) if paired else jnp.int32(0)
    own = frames.shape[1]
    FR = own * lax.axis_size("tensor")
    half = FR // 2
    rows = 2 * EDGE + 3 * FR
    local = w_qkv.shape[2]
    heads = local // HD
    W = -(-local // 128) * 128
    fill = W - local
    vectors = norm_vectors.astype(F32)

    def widened(x):
        return jnp.pad(x, [(0, 0)] * (x.ndim - 1) + [(0, fill)]) if fill else x

    def gathered(w):
        return lax.all_gather(w, "dp", axis=0, tiled=True)

    qkv_all = gathered(widened(w_qkv).reshape(w_qkv.shape[0], 3 * W))
    out_all = gathered(widened(w_out))
    fc1_all = gathered(w_fc1)
    fc2_all = gathered(w_fc2)
    wq, wkv = qkv_all[:, :W], qkv_all[:, W:]
    bias_q = widened(bias_qv[0].astype(F32))
    bias_kv = jnp.concatenate((jnp.zeros((W,), F32), widened(bias_qv[1].astype(F32))))

    z1s, r1s, h1s, qs, pieces, ranges, mixeds, lses = [], [], [], [], [], [], [], []
    for b in range(MB):
        z1, r1 = norm_parts(frames[b].astype(F32))
        h1 = collect((z1 * vectors[0] + vectors[1]).astype(BF))
        q = ((dot_on(h1, wq, 1, 0) + bias_q) * (LOG2E * SCALE)).astype(BF)
        kv = (dot_on(h1, wkv, 1, 0) + bias_kv).astype(BF)
        head = lax.dynamic_slice_in_dim(kv, swap * half, EDGE)
        tail = lax.dynamic_slice_in_dim(kv, (1 - swap) * half, EDGE)
        pieces.append((over_dp(tail, 2), over_dp(kv, 1), kv, over_dp(kv, -1), over_dp(head, -2)))
        ids = segment_ids[b]
        reach = FR + EDGE
        padded = jnp.concatenate(
            (jnp.full((reach,), -1, jnp.int32), ids, jnp.full((reach,), 1 << 30, jnp.int32))
        )
        near = lax.dynamic_slice_in_dim(padded, dp_place * FR, rows)
        mine = jnp.concatenate(
            (
                lax.dynamic_slice_in_dim(ids, dp_place * FR + swap * half, half),
                lax.dynamic_slice_in_dim(ids, dp_place * FR + (1 - swap) * half, half),
            )
        )
        st = jnp.sum((near[None, :] < mine[:, None]).astype(jnp.int32), axis=1)
        en = jnp.sum((near[None, :] <= mine[:, None]).astype(jnp.int32), axis=1)
        z1s.append(z1)
        r1s.append(r1)
        h1s.append(h1)
        qs.append(q)
        ranges.append((st, en))

    middles, h2s, actives, slopes, outputs = [], [], [], [], []
    for b in range(MB):
        mixed, lse = attend_forward(qs[b], pieces[b], ranges[b], swap, heads)
        middle = frames[b].astype(F32) + summed([(mixed, out_all, 1)]) + vectors[4]
        z2, r2 = norm_parts(middle)
        h2 = collect((z2 * vectors[2] + vectors[3]).astype(BF))
        hidden = dot_on(h2, fc1_all, 1, 0) + bias_fc1.astype(F32)
        active, slope = gelu_both(hidden)
        result = middle + summed([(active, fc2_all, 1)]) + vectors[5]
        outputs.append(result.astype(BF))
        mixeds.append(mixed)
        lses.append(lse)
        middles.append(middle)
        h2s.append(h2)
        actives.append(active)
        slopes.append(slope)

    term_fc2 = term_fc1 = term_out = term_q = term_kv = 0.0
    bias_q_sum = bias_v_sum = bias_fc1_sum = 0.0
    norm_sums = 0.0
    inputs_grad = []
    for b in range(MB):
        grad_rows = cotangent[b].astype(F32)
        grad_f = collect(cotangent[b])
        grad_hidden = (dot_on(grad_f, fc2_all, 1, 0) * slopes[b].astype(F32)).astype(BF)
        term_fc2 = term_fc2 + dot_on(grad_f, actives[b], 0, 0)
        bias_fc1_sum = bias_fc1_sum + jnp.sum(grad_hidden, axis=0, dtype=F32)
        term_fc1 = term_fc1 + dot_on(h2s[b], grad_hidden, 0, 0)
        grad_h2 = summed([(grad_hidden, fc1_all, 1)])
        z2, r2 = norm_parts(middles[b])
        grad_middle = grad_rows + norm_back(grad_h2, z2, r2, vectors[2])
        grad_a = collect(grad_middle.astype(BF))
        term_out = term_out + dot_on(grad_a, mixeds[b], 0, 0)
        grad_mixed = dot_on(grad_a, out_all, 1, 0).astype(BF)
        chosen = (jnp.arange(W)[:, None] // HD == jnp.arange(heads)[None, :]).astype(F32)
        delta = lax.dot_general(
            chosen,
            grad_mixed.astype(F32) * mixeds[b].astype(F32),
            (((0,), (1,)), ((), ())),
            precision=lax.Precision.HIGHEST,
        )
        grad_q, g_l2, g_l1, g_own, g_r1, g_r2 = attend_backward(
            qs[b], grad_mixed, pieces[b], ranges[b], lses[b].T, delta, swap, heads
        )
        to_tail = over_dp(g_l2, -2).astype(F32)
        to_head = over_dp(g_r2, 2).astype(F32)
        first = jnp.where(swap == 1, to_tail, to_head)
        second = jnp.where(swap == 1, to_head, to_tail)
        grad_kv = (
            g_own.astype(F32)
            + over_dp(g_l1, -1).astype(F32)
            + over_dp(g_r1, 1).astype(F32)
            + jnp.concatenate((first, second))
        ).astype(BF)
        bias_q_sum = bias_q_sum + jnp.sum(grad_q, axis=0, dtype=F32)
        bias_v_sum = bias_v_sum + jnp.sum(grad_kv[:, W:], axis=0, dtype=F32)
        term_q = term_q + dot_on(h1s[b], grad_q, 0, 0)
        term_kv = term_kv + dot_on(h1s[b], grad_kv, 0, 0)
        grad_h1 = summed([(grad_q, wq, 1), (grad_kv, wkv, 1)])
        inputs_grad.append(grad_middle + norm_back(grad_h1, z1s[b], r1s[b], vectors[0]))
        norm_sums = norm_sums + jnp.stack(
            (
                jnp.sum(grad_h1 * z1s[b], axis=0),
                jnp.sum(grad_h1, axis=0),
                jnp.sum(grad_h2 * z2, axis=0),
                jnp.sum(grad_h2, axis=0),
                jnp.sum(grad_middle, axis=0),
                jnp.sum(grad_rows, axis=0),
            )
        )

    def owned(term):
        return lax.psum_scatter(term.astype(BF), "dp", scatter_dimension=0, tiled=True).astype(F32)

    own_fc2 = owned(term_fc2)
    own_fc1 = owned(term_fc1)
    own_out = owned(term_out)[:, :local]
    own_qkv = owned(jnp.concatenate((term_q, term_kv), axis=1))
    own_qkv = own_qkv.reshape(own_qkv.shape[0], 3, W)[:, :, :local]
    bias_total = lax.psum((jnp.stack((bias_q_sum, bias_v_sum))[:, :local], bias_fc1_sum), "dp")
    norm_total = lax.psum(norm_sums, ("dp", "tensor"))
    return (
        jnp.stack(outputs),
        jnp.stack(inputs_grad),
        own_qkv,
        own_out,
        own_fc1,
        own_fc2,
        bias_total[0],
        bias_total[1],
        norm_total,
    )


def solution(mesh):
    in_specs = (
        P(None, ("dp", "tensor"), None),
        P(None, ("dp", "tensor"), None),
        P(),
        P("dp", None, "tensor"),
        P("dp", "tensor"),
        P("dp", "tensor"),
        P("dp", "tensor"),
        P(None, "tensor"),
        P("tensor"),
        P(),
    )
    out_specs = (
        P(None, ("dp", "tensor"), None),
        P(None, ("dp", "tensor"), None),
        P("dp", None, "tensor"),
        P("dp", "tensor"),
        P("dp", "tensor"),
        P("dp", "tensor"),
        P(None, "tensor"),
        P("tensor"),
        P(),
    )
    return jax.shard_map(
        per_device, mesh=mesh, in_specs=in_specs, out_specs=out_specs, check_vma=False
    )
```

time: 3320 us -> 1320 us (0.40)
  matrix products: 1430 us -> 260 us
  waiting for transfers between devices: 943 us -> 367 us
  local copies, waits for them, and re-layouts: 444 us -> 29.4 us
  other arithmetic: 293 us -> 53.8 us
  Pallas kernels: 0 us -> 185 us
  starting transfers between devices: 44.6 us -> 206 us
  blocking collectives: 125 us -> 195 us
    dot_general x164 -> x42, matrix products: 1430 us -> 260 us  [the longest x40 256 us: dot_on(): lax.dot_general(a, b, (((a_dim,), (b_dim,)), ((), ())), preferred_element...]
    all_gather x12 -> x4, waiting for transfers between devices: 316 us -> 17.7 us  [gathered(): return lax.all_gather(w, 'dp', axis=0, tiled=True)]
    reduce_scatter x11 -> x3, waiting for transfers between devices: 222 us -> 0.02 us  [owned(): lax.psum_scatter(term.astype(BF), 'dp', scatter_dimension=0, tiled=True)]
    pallas_call x0 -> x4, Pallas kernels: none -> 185 us  [the longest x2 100 us: attend_backward(): pl.pallas_call(functools.partial(backward_kernel, heads, W, QB, KB), out_...]
    another operation x20 -> x16, local copies, waits for them, and re-layouts: 178 us -> 0.19 us  [the longest x14 0.18 us: per_device(): jnp.stack((jnp.sum(grad_h1 * z1s[b], axis=0), jnp.sum(grad_h1, axis=0), j...]
    reduce_sum x31 -> x10, other arithmetic: 187 us -> 14.2 us  [the longest x2 6.8 us: per_device(): en = jnp.sum((near[None, :] <= mine[:, None]).astype(jnp.int32), axis=1)]
    ppermute x16 -> x32, starting transfers between devices: 42.8 us -> 206 us  [the longest x16 185 us: over_dp(): return lax.ppermute(x, 'dp', pairs)]
    while x144 -> x0, local copies, waits for them, and re-layouts: 108 us -> none  [the longest x4 77.9 us: attend_backward(): lax.scan(step_back, jnp.zeros(queries.shape, jnp.float32), (key_blocks, i...]
  transfers between devices with their start and end apart: 40 -> 40, of which waited for: 16 -> 15; matrix products, arithmetic and copies ran while one was open for 52% -> 24% of each run, Pallas kernels for 0% -> 14%
where the time goes in v1:
time: 1320 us; the launch traced here: 1310 us
  waiting for transfers between devices  367 us (28%)
  matrix products  260 us (20%)
  starting transfers between devices  206 us (16%)
  blocking collectives  195 us (15%)
  Pallas kernels  185 us (14%)
  other arithmetic  53.8 us (4%)
  local copies, waits for them, and re-layouts  29.4 us (2%)
  between operations  16 us (1%)
    dot_general x40, matrix products, dot_on(): lax.dot_general(a, b, (((a_dim,), (b_dim,)), ((), ())), preferred_element...  256 us
    ppermute x16, starting transfers between devices, over_dp(): return lax.ppermute(x, 'dp', pairs)  185 us
    ppermute x16, waiting for transfers between devices, over_dp(): return lax.ppermute(x, 'dp', pairs)  184 us
    ppermute x16, waiting for transfers between devices, partner(): return lax.ppermute(x, 'tensor', [(0, 1), (1, 0)])  164 us
    psum x1, blocking collectives, per_device(): lax.psum((jnp.stack((bias_q_sum, bias_v_sum))[:, :local], bias_fc1_sum),...  157 us
    pallas_call x2, Pallas kernels, attend_backward(): pl.pallas_call(functools.partial(backward_kernel, heads, W, QB, KB), out_...  100 us
    pallas_call x2, Pallas kernels, attend_forward(): pl.pallas_call(functools.partial(forward_kernel, heads, W, QB, KB), out_s...  84.6 us
    psum x1, blocking collectives, per_device(): norm_total = lax.psum(norm_sums, ('dp', 'tensor'))  37.7 us
  transfers between devices with their start and end apart: 40, of which 15 were waited for; matrix products, arithmetic and copies ran while one was open for 24% of the time, Pallas kernels for 14%

profile of v1, /device:TPU:0, one launch (start us, length us, event | category | flops | bytes accessed | tf_op | source)
XLA Modules:
  0.0 1312.0 jit_solution(17970649516145252172)
XLA Ops:
  33.0 17.2 %collective-permute-done = bf16[512,1280]{1,0:T(8,128)(2,1)S(1)} collective-permute-done((bf16[512,1280]{1,0:T(8,128)(2,1)}, bf16[512,1280]{1,0:T(8,128)(2,1)S(1)}, u32[]{:S(2)}, u32[]{:S(2)}) %collective-permute-start) | collective-permute-done | bytes 1310752 | tf_op jit(solution)/shard_map/ppermute | solution.py:248
  50.3 17.7 %all-gather.5.cloned.1.call-done = bf16[1280,1920]{1,0:T(8,128)(2,1)} async-done(((bf16[80,1920]{1,0:T(8,128)(2,1)}), bf16[1280,1920]{1,0:T(8,128)(2,1)}) %all-gather.5.cloned.1.call-update) | async-done | bytes 4915216 | tf_op jit(solution)/shard_map/all_gather | solution.py:309
  104.1 36.8 %collective-permute-done.4.r2 = bf16[512,1280]{1,0:T(8,128)(2,1)S(1)} collective-permute-done((bf16[512,1280]{1,0:T(8,128)(2,1)S(1)}, bf16[512,1280]{1,0:T(8,128)(2,1)S(1)}, u32[]{:S(2)}, u32[]{:S(2)}) %collective-permute-start.4) | collective-permute-done | bytes 1310752 | tf_op jit(solution)/shard_map/ppermute | solution.py:244
  143.7 58.0 %collective-permute-done.1.l2 = bf16[512,1280]{1,0:T(8,128)(2,1)S(1)} collective-permute-done((bf16[512,1280]{1,0:T(8,128)(2,1)S(1)}, bf16[512,1280]{1,0:T(8,128)(2,1)S(1)}, u32[]{:S(2)}, u32[]{:S(2)}) %collective-permute-start.1) | collective-permute-done | bytes 1310752 | tf_op jit(solution)/shard_map/ppermute | solution.py:244
  210.6 42.2 %attend_forward.2 = (bf16[1024,640]{1,0:T(8,128)(2,1)}, f32[1024,8]{1,0:T(8,128)}) custom-call(s32[4]{0:T(128)} %get-tuple-element.117.lo_ref, s32[4]{0:T(128)} %get-tuple-element.118.count_ref, s32[1]{0:T(128)} %bitcast.4.swap_ref, s32[1024,1]{1,0:T(8,128)} %copy.39.st_ref, s32[1024,1]{1,0:T(8,128)} %copy.40.en_ref, ...), custom_call_target="tpu_custom_call" | custom-call | flops 60129542144 | bytes 10485760 | tf_op jit(solution)/shard_map/attend_forward/pallas_call | solution.py:133
  256.9 11.9 collective-permute-done.9.l2
  268.8 42.4 %attend_forward.3 = (bf16[1024,640]{1,0:T(8,128)(2,1)}, f32[1024,8]{1,0:T(8,128)}) custom-call(s32[4]{0:T(128)} %get-tuple-element.119.lo_ref, s32[4]{0:T(128)} %get-tuple-element.120.count_ref, s32[1]{0:T(128)} %bitcast.4.swap_ref, s32[1024,1]{1,0:T(8,128)} %copy.41.st_ref, s32[1024,1]{1,0:T(8,128)} %copy.42.en_ref, ...), custom_call_target="tpu_custom_call" | custom-call | flops 60129542144 | bytes 10485760 | tf_op jit(solution)/shard_map/attend_forward/pallas_call | solution.py:133
  316.9 14.4 %collective-permute-done.13 = bf16[512,1280]{1,0:T(8,128)(2,1)S(1)} collective-permute-done((bf16[512,1280]{1,0:T(8,128)(2,1)S(1)}, bf16[512,1280]{1,0:T(8,128)(2,1)S(1)}, u32[]{:S(2)}, u32[]{:S(2)}) %collective-permute-start.13) | collective-permute-done | bytes 1310752 | tf_op jit(solution)/shard_map/ppermute | solution.py:248
  341.7 24.9 %collective-permute-done.14 = bf16[512,1280]{1,0:T(8,128)(2,1)} collective-permute-done((bf16[512,1280]{1,0:T(8,128)(2,1)}, bf16[512,1280]{1,0:T(8,128)(2,1)}, u32[]{:S(2)}, u32[]{:S(2)}) %collective-permute-start.14) | collective-permute-done | bytes 1310752 | tf_op jit(solution)/shard_map/ppermute | solution.py:248
  366.6 12.3 fusion.82
  378.9 16.9 %collective-permute-done.24 = bf16[512,1280]{1,0:T(8,128)(2,1)} collective-permute-done((bf16[512,1280]{1,0:T(8,128)(2,1)}, bf16[512,1280]{1,0:T(8,128)(2,1)}, u32[]{:S(2)}, u32[]{:S(2)}) %collective-permute-start.24) | collective-permute-done | bytes 1310752 | tf_op jit(solution)/shard_map/ppermute | solution.py:248
  395.8 13.7 %convert_reduce_fusion.4 = (f32[2560]{0:T(1024)}, bf16[1024,2560]{1,0:T(8,128)(2,1)S(1)}) fusion(f32[1024,2560]{1,0:T(8,128)} %fusion.82, f32[2560]{0:T(1024)S(1)} %convert_element_type.259, bf16[1280,2560]{1,0:T(8,128)(2,1)} %all-gather.11.cloned.1.call-done, bf16[512,1280]{1,0:T(8,128)(2,1)} %collective-permute-done.24, ...), kind=kOutput, calls=%fused_computation.20 | convolution fusion | flops 6755448320 | bytes 24924160 | tf_op jit(solution)/shard_map/dot_general | solution.py:32
  409.6 8.4 convolution_convert_fusion.2
  422.8 13.9 %multiply_convert_fusion.3 = (bf16[1024,2560]{1,0:T(8,128)(2,1)}, bf16[1024,2560]{1,0:T(8,128)(2,1)S(1)}, f32[1024,2560]{1,0:T(8,128)}) fusion(f32[2560]{0:T(1024)S(1)} %convert_element_type.259, f32[1024,2560]{1,0:T(8,128)} %fusion.82, bf16[1280,2560]{1,0:T(8,128)(2,1)S(1)} %copy-done.68, bf16[512,1280]{1,0:T(8,128)(2,1)} %collective-permute-done.6, ...), kind=kOutput, calls=%fused_computation.26 | convolution fusion | flops 6747586560 | bytes 40642560 | tf_op jit(solution)/shard_map/dot_general | solution.py:32
  450.0 14.3 %convert_reduce_fusion.5 = (f32[2560]{0:T(1024)}, bf16[1024,2560]{1,0:T(8,128)(2,1)}) fusion(f32[1024,2560]{1,0:T(8,128)} %get-tuple-element.160, f32[2560]{0:T(1024)S(1)} %convert_element_type.259, bf16[1280,2560]{1,0:T(8,128)(2,1)S(1)} %bitcast.166, bf16[512,1280]{1,0:T(8,128)(2,1)} %collective-permute-done.16, bf16[512,1280]{1,0:T(8,128)(2,1)} %get-tuple-element.130), kind=kOutput, calls=%fused_computation.21 | convolution fusion | flops 6755448320 | bytes 24924160 | tf_op jit(solution)/shard_map/dot_general | solution.py:32
  491.1 10.3 collective-permute-done.7
  501.4 28.2 %collective-permute-done.17 = bf16[512,1280]{1,0:T(8,128)(2,1)} collective-permute-done((bf16[512,1280]{1,0:T(8,128)(2,1)}, bf16[512,1280]{1,0:T(8,128)(2,1)}, u32[]{:S(2)}, u32[]{:S(2)}) %collective-permute-start.17) | collective-permute-done | bytes 1310752 | tf_op jit(solution)/shard_map/ppermute | solution.py:248
  529.7 14.2 %multiply_reduce_fusion = (f32[1280]{0:T(1024)}, f32[512]{0:T(512)S(1)}, f32[512]{0:T(512)S(1)}, f32[1280]{0:T(1024)}, bf16[1,512,1280]{2,1,0:T(8,128)(2,1)}, /*...) fusion(f32[512,1280]{1,0:T(8,128)S(1)} %copy-done.10, ...), kind=kOutput, calls=%fused_computation.127 | convolution fusion | flops 3376407552 | bytes 30193664 | tf_op jit(solution)/shard_map/dot_general | solution.py:32
  553.0 23.6 %collective-permute-done.26 = bf16[512,1280]{1,0:T(8,128)(2,1)S(1)} collective-permute-done((bf16[512,1280]{1,0:T(8,128)(2,1)S(1)}, bf16[512,1280]{1,0:T(8,128)(2,1)S(1)}, u32[]{:S(2)}, u32[]{:S(2)}) %collective-permute-start.26) | collective-permute-done | bytes 1310752 | tf_op jit(solution)/shard_map/ppermute | solution.py:248
  579.0 25.8 %collective-permute-done.18 = bf16[512,1280]{1,0:T(8,128)(2,1)S(1)} collective-permute-done((bf16[512,1280]{1,0:T(8,128)(2,1)S(1)}, bf16[512,1280]{1,0:T(8,128)(2,1)S(1)}, u32[]{:S(2)}, u32[]{:S(2)}) %collective-permute-start.18) | collective-permute-done | bytes 1310752 | tf_op jit(solution)/shard_map/ppermute | solution.py:248
  609.3 9.9 fusion.81
  619.2 12.2 fusion
  636.0 10.1 fusion.79
  646.1 12.3 fusion.1
  665.2 50.1 %attend_backward.3 = (bf16[1024,640]{1,0:T(8,128)(2,1)}, bf16[512,1280]{1,0:T(8,128)(2,1)}, bf16[1024,1280]{1,0:T(8,128)(2,1)}, bf16[1024,1280]{1,0:T(8,128)(2,1...) custom-call(s32[4]{0:T(128)} %get-tuple-element.119.lo_ref, s32[4]{0:T(128)} %get-tuple-element.120.count_ref, ...), custom_call_target="tpu_custom_call" | custom-call | flops 75161927680 | bytes 20971520 | tf_op jit(solution)/shard_map/attend_backward/pallas_call | solution.py:217
  723.3 50.1 %attend_backward.2 = (bf16[1024,640]{1,0:T(8,128)(2,1)}, bf16[512,1280]{1,0:T(8,128)(2,1)}, bf16[1024,1280]{1,0:T(8,128)(2,1)}, bf16[1024,1280]{1,0:T(8,128)(2,1...) custom-call(s32[4]{0:T(128)} %get-tuple-element.117.lo_ref, s32[4]{0:T(128)} %get-tuple-element.118.count_ref, ...), custom_call_target="tpu_custom_call" | custom-call | flops 75161927680 | bytes 20971520 | tf_op jit(solution)/shard_map/attend_backward/pallas_call | solution.py:217
  774.9 112.7 %collective-permute-start.22 = (bf16[512,1280]{1,0:T(8,128)(2,1)}, bf16[512,1280]{1,0:T(8,128)(2,1)}, u32[]{:S(2)}, u32[]{:S(2)}) collective-permute-start(bf16[512,1280]{1,0:T(8,128)(2,1)} %get-tuple-element.33), channel_id=1, source_target_pairs={{0,4},{2,6},{4,8},{6,10},{8,12},{10,14},{12,16},{14,18},{16,20},{1... | collective-permute-start | bytes 3932168 | tf_op jit(solution)/shard_map/ppermute | solution.py:244
  896.0 39.5 %collective-permute-start.30 = (bf16[512,1280]{1,0:T(8,128)(2,1)S(1)}, bf16[512,1280]{1,0:T(8,128)(2,1)S(1)}, u32[]{:S(2)}, u32[]{:S(2)}) collective-permute-start(bf16[512,1280]{1,0:T(8,128)(2,1)S(1)} %copy-done.80), channel_id=1, source_target_pairs={{0,4},{2,6},{4,8},{6,10},{8,12},{10,14},{12,16},{14,18},{16,20},{1... | collective-permute-start | bytes 3932168 | tf_op jit(solution)/shard_map/ppermute | solution.py:244
  944.6 45.3 %collective-permute-done.22 = bf16[512,1280]{1,0:T(8,128)(2,1)} collective-permute-done((bf16[512,1280]{1,0:T(8,128)(2,1)}, bf16[512,1280]{1,0:T(8,128)(2,1)}, u32[]{:S(2)}, u32[]{:S(2)}) %collective-permute-start.22) | collective-permute-done | bytes 1310752 | tf_op jit(solution)/shard_map/ppermute | solution.py:244
  993.6 31.9 %collective-permute-done.30 = bf16[512,1280]{1,0:T(8,128)(2,1)S(1)} collective-permute-done((bf16[512,1280]{1,0:T(8,128)(2,1)S(1)}, bf16[512,1280]{1,0:T(8,128)(2,1)S(1)}, u32[]{:S(2)}, u32[]{:S(2)}) %collective-permute-start.30) | collective-permute-done | bytes 1310752 | tf_op jit(solution)/shard_map/ppermute | solution.py:244
  1079.0 157.0 %all-reduce.1 = (f32[2,640]{1,0:T(2,128)}, f32[2560]{0:T(1024)}) all-reduce(f32[2,640]{1,0:T(2,128)S(1)} %pad_maximum_fusion.27, f32[2560]{0:T(1024)S(1)} %add.423), channel_id=1, replica_groups=mesh['dp'=16,'tensor'=2] {'dp'}, use_global_device_ids=true, to_apply=%region_28.29 | all-reduce | flops 3840 | bytes 30720 | tf_op jit(solution)/shard_map/psum | solution.py:427
  1253.2 37.7 %psum.23 = f32[6,1280]{1,0:T(8,128)} all-reduce(f32[6,1280]{1,0:T(8,128)S(1)} %add.424), channel_id=1, replica_groups=mesh['dp'=16,'tensor'=2] {'dp','tensor'}, use_global_device_ids=true, to_apply=%region_44.45 | all-reduce | flops 7680 | bytes 61440 | tf_op jit(solution)/shard_map/psum | solution.py:428
  (391 shorter events, 280.0 us)
Async XLA Ops:
  7.2 60.8 %all-gather.5.cloned.1.call-start = ((), (), s32[]{:S(2)}) async-start(), calls=%async_computation.4 | async-start | bytes 5222400 | tf_op jit(solution)/shard_map/all_gather | solution.py:309
  9.1 243.7 %all-gather.7.cloned.1.call-start = ((), (), s32[]{:S(2)}) async-start(), calls=%async_computation.5 | async-start | bytes 1740800 | tf_op jit(solution)/shard_map/all_gather | solution.py:309
  9.9 331.9 %all-gather.9.cloned.1.call-start = ((), (), s32[]{:S(2)}) async-start(), calls=%async_computation.6 | async-start | bytes 6963200 | tf_op jit(solution)/shard_map/all_gather | solution.py:309
  10.6 385.2 %all-gather.11.cloned.1.call-start = ((), (), s32[]{:S(2)}) async-start(), calls=%async_computation.7 | async-start | bytes 6963200 | tf_op jit(solution)/shard_map/all_gather | solution.py:309
  20.4 65.4 %collective-permute-start.8 = (bf16[512,1280]{1,0:T(8,128)(2,1)}, bf16[512,1280]{1,0:T(8,128)(2,1)}, u32[]{:S(2)}, u32[]{:S(2)}) collective-permute-start(bf16[512,1280]{1,0:T(8,128)(2,1)} %get-tuple-element.122), channel_id=1, source_target_pairs={{0,1},{1,0},{2,3},{3,2},{4,5},{5,4},{6,7},{7,6},{8,9},{9,8},{10,11... | collective-permute-start | bytes 3932168 | tf_op jit(solution)/shard_map/ppermute | solution.py:248
  20.5 1038.3 %reduce-scatter.7.cloned.1.call-start = ((), (), s32[]{:S(2)}) async-start(), calls=%async_computation.8 | async-start | bytes 1740800 | tf_op jit(solution)/shard_map/reduce_scatter | solution.py:420
  73.9 129.0 %collective-permute-start.3 = (bf16[1024,1280]{1,0:T(8,128)(2,1)S(1)}, bf16[1024,1280]{1,0:T(8,128)(2,1)S(1)}, u32[]{:S(2)}, u32[]{:S(2)}) collective-permute-start(bf16[1024,1280]{1,0:T(8,128)(2,1)S(1)} %add_convert_fusion.1.own), channel_id=1, source_target_pairs={{2,0},{4,2},{6,4},{8,6},{10,8},{12,10},{14,12},{16,14},{18,16},{20... | collective-permute-start | bytes 7864328 | tf_op jit(solution)/shard_map/ppermute | solution.py:244
  75.2 133.9 %collective-permute-start.2 = (bf16[1024,1280]{1,0:T(8,128)(2,1)S(1)}, bf16[1024,1280]{1,0:T(8,128)(2,1)S(1)}, u32[]{:S(2)}, u32[]{:S(2)}) collective-permute-start(bf16[1024,1280]{1,0:T(8,128)(2,1)S(1)} %add_convert_fusion.1.own), channel_id=1, source_target_pairs={{0,2},{2,4},{4,6},{6,8},{8,10},{10,12},{12,14},{14,16},{16,18},{18... | collective-permute-start | bytes 7864328 | tf_op jit(solution)/shard_map/ppermute | solution.py:244
  79.2 61.7 %collective-permute-start.4 = (bf16[512,1280]{1,0:T(8,128)(2,1)S(1)}, bf16[512,1280]{1,0:T(8,128)(2,1)S(1)}, u32[]{:S(2)}, u32[]{:S(2)}) collective-permute-start(bf16[512,1280]{1,0:T(8,128)(2,1)S(1)} %get-tuple-element.135), channel_id=1, source_target_pairs={{4,0},{6,2},{8,4},{10,6},{12,8},{14,10},{16,12},{18,14},{20,16},{2... | collective-permute-start | bytes 3932168 | tf_op jit(solution)/shard_map/ppermute | solution.py:244
  80.8 120.9 %collective-permute-start.1 = (bf16[512,1280]{1,0:T(8,128)(2,1)S(1)}, bf16[512,1280]{1,0:T(8,128)(2,1)S(1)}, u32[]{:S(2)}, u32[]{:S(2)}) collective-permute-start(bf16[512,1280]{1,0:T(8,128)(2,1)S(1)} %get-tuple-element.136), channel_id=1, source_target_pairs={{0,4},{2,6},{4,8},{6,10},{8,12},{10,14},{12,16},{14,18},{16,20},{1... | collective-permute-start | bytes 3932168 | tf_op jit(solution)/shard_map/ppermute | solution.py:244
  91.2 177.6 %collective-permute-start.11 = (bf16[1024,1280]{1,0:T(8,128)(2,1)S(1)}, bf16[1024,1280]{1,0:T(8,128)(2,1)}, u32[]{:S(2)}, u32[]{:S(2)}) collective-permute-start(bf16[1024,1280]{1,0:T(8,128)(2,1)S(1)} %add_convert_fusion.own), channel_id=1, source_target_pairs={{2,0},{4,2},{6,4},{8,6},{10,8},{12,10},{14,12},{16,14},{18,16},{20... | collective-permute-start | bytes 7864328 | tf_op jit(solution)/shard_map/ppermute | solution.py:244
  140.9 127.9 %collective-permute-start.10 = (bf16[1024,1280]{1,0:T(8,128)(2,1)S(1)}, bf16[1024,1280]{1,0:T(8,128)(2,1)}, u32[]{:S(2)}, u32[]{:S(2)}) collective-permute-start(bf16[1024,1280]{1,0:T(8,128)(2,1)S(1)} %add_convert_fusion.own), channel_id=1, source_target_pairs={{0,2},{2,4},{4,6},{6,8},{8,10},{10,12},{12,14},{14,16},{16,18},{18... | collective-permute-start | bytes 7864328 | tf_op jit(solution)/shard_map/ppermute | solution.py:244
  201.7 55.2 %collective-permute-start.12 = (bf16[512,1280]{1,0:T(8,128)(2,1)}, bf16[512,1280]{1,0:T(8,128)(2,1)}, u32[]{:S(2)}, u32[]{:S(2)}) collective-permute-start(bf16[512,1280]{1,0:T(8,128)(2,1)} %get-tuple-element.137), channel_id=1, source_target_pairs={{4,0},{6,2},{8,4},{10,6},{12,8},{14,10},{16,12},{18,14},{20,16},{2... | collective-permute-start | bytes 3932168 | tf_op jit(solution)/shard_map/ppermute | solution.py:244
  203.0 65.8 %collective-permute-start.9 = (bf16[512,1280]{1,0:T(8,128)(2,1)}, bf16[512,1280]{1,0:T(8,128)(2,1)}, u32[]{:S(2)}, u32[]{:S(2)}) collective-permute-start(bf16[512,1280]{1,0:T(8,128)(2,1)} %get-tuple-element.138), channel_id=1, source_target_pairs={{0,4},{2,6},{4,8},{6,10},{8,12},{10,14},{12,16},{14,18},{16,20},{1... | collective-permute-start | bytes 3932168 | tf_op jit(solution)/shard_map/ppermute | solution.py:244
  255.7 59.3 %collective-permute-start.5 = (bf16[512,1280]{1,0:T(8,128)(2,1)S(1)}, bf16[512,1280]{1,0:T(8,128)(2,1)S(1)}, u32[]{:S(2)}, u32[]{:S(2)}) collective-permute-start(bf16[512,1280]{1,0:T(8,128)(2,1)S(1)} %convolution_convert_fusion.1), channel_id=1, source_target_pairs={{0,1},{1,0},{2,3},{3,2},{4,5},{5,4},{6,7},{7,6},{8,9},{9,8},{10,11... | collective-permute-start | bytes 3932168 | tf_op jit(solution)/shard_map/ppermute | solution.py:248
  338.9 111.0 %collective-permute-start.16 = (bf16[512,1280]{1,0:T(8,128)(2,1)}, bf16[512,1280]{1,0:T(8,128)(2,1)}, u32[]{:S(2)}, u32[]{:S(2)}) collective-permute-start(bf16[512,1280]{1,0:T(8,128)(2,1)} %get-tuple-element.130), channel_id=1, source_target_pairs={{0,1},{1,0},{2,3},{3,2},{4,5},{5,4},{6,7},{7,6},{8,9},{9,8},{10,11... | collective-permute-start | bytes 3932168 | tf_op jit(solution)/shard_map/ppermute | solution.py:248
  339.7 56.1 %collective-permute-start.24 = (bf16[512,1280]{1,0:T(8,128)(2,1)}, bf16[512,1280]{1,0:T(8,128)(2,1)}, u32[]{:S(2)}, u32[]{:S(2)}) collective-permute-start(bf16[512,1280]{1,0:T(8,128)(2,1)} %get-tuple-element.131), channel_id=1, source_target_pairs={{0,1},{1,0},{2,3},{3,2},{4,5},{5,4},{6,7},{7,6},{8,9},{9,8},{10,11... | collective-permute-start | bytes 3932168 | tf_op jit(solution)/shard_map/ppermute | solution.py:248
  341.0 81.8 %collective-permute-start.6 = (bf16[512,1280]{1,0:T(8,128)(2,1)}, bf16[512,1280]{1,0:T(8,128)(2,1)}, u32[]{:S(2)}, u32[]{:S(2)}) collective-permute-start(bf16[512,1280]{1,0:T(8,128)(2,1)} %get-tuple-element.150), channel_id=1, source_target_pairs={{0,1},{1,0},{2,3},{3,2},{4,5},{5,4},{6,7},{7,6},{8,9},{9,8},{10,11... | collective-permute-start | bytes 3932168 | tf_op jit(solution)/shard_map/ppermute | solution.py:248
  418.0 73.1 %collective-permute-start.25 = (bf16[512,1280]{1,0:T(8,128)(2,1)S(1)}, bf16[512,1280]{1,0:T(8,128)(2,1)}, u32[]{:S(2)}, u32[]{:S(2)}) collective-permute-start(bf16[512,1280]{1,0:T(8,128)(2,1)S(1)} %convolution_convert_fusion.2), channel_id=1, source_target_pairs={{0,1},{1,0},{2,3},{3,2},{4,5},{5,4},{6,7},{7,6},{8,9},{9,8},{10,11... | collective-permute-start | bytes 3932168 | tf_op jit(solution)/shard_map/ppermute | solution.py:248
  470.7 58.9 %collective-permute-start.17 = (bf16[512,1280]{1,0:T(8,128)(2,1)}, bf16[512,1280]{1,0:T(8,128)(2,1)}, u32[]{:S(2)}, u32[]{:S(2)}) collective-permute-start(bf16[512,1280]{1,0:T(8,128)(2,1)} %convolution_convert_fusion.3), channel_id=1, source_target_pairs={{0,1},{1,0},{2,3},{3,2},{4,5},{5,4},{6,7},{7,6},{8,9},{9,8},{10,11... | collective-permute-start | bytes 3932168 | tf_op jit(solution)/shard_map/ppermute | solution.py:248
  609.3 689.4 %reduce-scatter.9.cloned.1.call-start = ((), (), s32[]{:S(2)}) async-start(), calls=%async_computation.9 | async-start | bytes 6963200 | tf_op jit(solution)/shard_map/reduce_scatter | solution.py:420
  631.5 669.2 %reduce-scatter.11.cloned.1.call-start = ((), (), s32[]{:S(2)}) async-start(), calls=%async_computation.10 | async-start | bytes 6963200 | tf_op jit(solution)/shard_map/reduce_scatter | solution.py:420
  658.4 644.2 %reduce-scatter.13.cloned.1.call-start = ((), (), s32[]{:S(2)}) async-start(), calls=%async_computation.11 | async-start | bytes 5222400
  715.3 180.7 %collective-permute-start.29 = (bf16[512,1280]{1,0:T(8,128)(2,1)}, bf16[512,1280]{1,0:T(8,128)(2,1)}, u32[]{:S(2)}, u32[]{:S(2)}) collective-permute-start(bf16[512,1280]{1,0:T(8,128)(2,1)} %get-tuple-element.39), channel_id=1, source_target_pairs={{4,0},{6,2},{8,4},{10,6},{12,8},{14,10},{16,12},{18,14},{20,16},{2... | collective-permute-start | bytes 3932168 | tf_op jit(solution)/shard_map/ppermute | solution.py:244
  773.5 169.8 %collective-permute-start.21 = (bf16[512,1280]{1,0:T(8,128)(2,1)}, bf16[512,1280]{1,0:T(8,128)(2,1)}, u32[]{:S(2)}, u32[]{:S(2)}) collective-permute-start(bf16[512,1280]{1,0:T(8,128)(2,1)} %get-tuple-element.32), channel_id=1, source_target_pairs={{4,0},{6,2},{8,4},{10,6},{12,8},{14,10},{16,12},{18,14},{20,16},{2... | collective-permute-start | bytes 3932168 | tf_op jit(solution)/shard_map/ppermute | solution.py:244
  774.9 214.9 %collective-permute-start.22 = (bf16[512,1280]{1,0:T(8,128)(2,1)}, bf16[512,1280]{1,0:T(8,128)(2,1)}, u32[]{:S(2)}, u32[]{:S(2)}) collective-permute-start(bf16[512,1280]{1,0:T(8,128)(2,1)} %get-tuple-element.33), channel_id=1, source_target_pairs={{0,4},{2,6},{4,8},{6,10},{8,12},{10,14},{12,16},{14,18},{16,20},{1... | collective-permute-start | bytes 3932168 | tf_op jit(solution)/shard_map/ppermute | solution.py:244
  888.1 139.1 %collective-permute-start.27 = (bf16[1024,1280]{1,0:T(8,128)(2,1)}, bf16[1024,1280]{1,0:T(8,128)(2,1)S(1)}, u32[]{:S(2)}, u32[]{:S(2)}) collective-permute-start(bf16[1024,1280]{1,0:T(8,128)(2,1)} %get-tuple-element.37), channel_id=1, source_target_pairs={{2,0},{4,2},{6,4},{8,6},{10,8},{12,10},{14,12},{16,14},{18,16},{20... | collective-permute-start | bytes 7864328 | tf_op jit(solution)/shard_map/ppermute | solution.py:244
  889.4 137.8 %collective-permute-start.28 = (bf16[1024,1280]{1,0:T(8,128)(2,1)}, bf16[1024,1280]{1,0:T(8,128)(2,1)S(1)}, u32[]{:S(2)}, u32[]{:S(2)}) collective-permute-start(bf16[1024,1280]{1,0:T(8,128)(2,1)} %get-tuple-element.38), channel_id=1, source_target_pairs={{0,2},{2,4},{4,6},{6,8},{8,10},{10,12},{12,14},{14,16},{16,18},{18... | collective-permute-start | bytes 7864328 | tf_op jit(solution)/shard_map/ppermute | solution.py:244
  896.0 129.5 %collective-permute-start.30 = (bf16[512,1280]{1,0:T(8,128)(2,1)S(1)}, bf16[512,1280]{1,0:T(8,128)(2,1)S(1)}, u32[]{:S(2)}, u32[]{:S(2)}) collective-permute-start(bf16[512,1280]{1,0:T(8,128)(2,1)S(1)} %copy-done.80), channel_id=1, source_target_pairs={{0,4},{2,6},{4,8},{6,10},{8,12},{10,14},{12,16},{14,18},{16,20},{1... | collective-permute-start | bytes 3932168 | tf_op jit(solution)/shard_map/ppermute | solution.py:244
  943.3 92.8 %collective-permute-start.19 = (bf16[1024,1280]{1,0:T(8,128)(2,1)S(1)}, bf16[1024,1280]{1,0:T(8,128)(2,1)S(1)}, u32[]{:S(2)}, u32[]{:S(2)}) collective-permute-start(bf16[1024,1280]{1,0:T(8,128)(2,1)S(1)} %copy-done.72), channel_id=1, source_target_pairs={{2,0},{4,2},{6,4},{8,6},{10,8},{12,10},{14,12},{16,14},{18,16},{20... | collective-permute-start | bytes 7864328 | tf_op jit(solution)/shard_map/ppermute | solution.py:244
  1068.6 178.7 %collective-permute-start.23 = (bf16[512,1280]{1,0:T(8,128)(2,1)}, bf16[512,1280]{1,0:T(8,128)(2,1)}, u32[]{:S(2)}, u32[]{:S(2)}) collective-permute-start(bf16[512,1280]{1,0:T(8,128)(2,1)} %fusion.37), channel_id=1, source_target_pairs={{0,1},{1,0},{2,3},{3,2},{4,5},{5,4},{6,7},{7,6},{8,9},{9,8},{10,11... | collective-permute-start | bytes 3932168 | tf_op jit(solution)/shard_map/ppermute | solution.py:248
  1078.4 166.0 %collective-permute-start.31 = (bf16[512,1280]{1,0:T(8,128)(2,1)}, bf16[512,1280]{1,0:T(8,128)(2,1)}, u32[]{:S(2)}, u32[]{:S(2)}) collective-permute-start(bf16[512,1280]{1,0:T(8,128)(2,1)} %fusion.38), channel_id=1, source_target_pairs={{0,1},{1,0},{2,3},{3,2},{4,5},{5,4},{6,7},{7,6},{8,9},{9,8},{10,11... | collective-permute-start | bytes 3932168 | tf_op jit(solution)/shard_map/ppermute | solution.py:248
  (101 other events, 2067.4 us)
Sparse Core Ops, SparseCore 0:
  10.8 57.1 all-gather.4
  70.1 104.7 all-gather.6
  177.2 118.4 all-gather.8
  297.8 81.7 all-gather.10
  609.4 183.4 reduce-scatter.6
  797.2 106.7 reduce-scatter.8
  908.0 172.5 reduce-scatter.10
  1085.1 147.0 reduce-scatter.12

commit v2 on v1

v2 whole, which is shorter than its diff:
```python
import functools
import math

import jax
import jax.numpy as jnp
from jax import lax
from jax.experimental import pallas as pl
from jax.experimental.pallas import tpu as pltpu
from jax.sharding import PartitionSpec as P

HD = 80
MB = 2
EDGE = 512
EPSILON = 1e-05
NEGATIVE = -1e30
LOG2E = math.log2(math.e)
SCALE = 1.0 / math.sqrt(HD)
BF = jnp.bfloat16
F32 = jnp.float32


def head_spans(heads):
    spans = []
    for head in range(heads):
        first, last = head * HD, (head + 1) * HD
        start = first // 128 * 128
        spans.append((start, -(-last // 128) * 128 - start, first - start))
    return spans


def dot_on(a, b, a_dim, b_dim):
    return lax.dot_general(a, b, (((a_dim,), (b_dim,)), ((), ())), preferred_element_type=F32)


def in_head(rows, width, offset):
    lane = lax.broadcasted_iota(jnp.int32, (rows, width), 1)
    return (lane >= offset) & (lane < offset + HD)


def head_ones(width, offset):
    return jnp.where(in_head(1, width, offset), 1.0, 0.0).astype(BF)


def window_parts(refs, swap, FR):
    half = FR // 2
    both = (swap * half, (1 - swap) * half)
    bases = [[base + add for add in both] for base in (EDGE, EDGE + FR, EDGE + 2 * FR)]
    bases = [[0]] + bases + [[EDGE + 3 * FR]]
    return [
        (ref, number * half, base, half)
        for ref, group in zip(refs, bases)
        for number, base in enumerate(group)
    ]


def fetch_window(refs, place, FR, window, sems):
    swap, core = place[0], place[1]
    left_direct, left_relayed, *near, right_direct, right_relayed = refs
    copies = []
    for number, (ref, row, at, rows) in enumerate(window_parts([left_direct, *near, right_direct], swap, FR)):
        to = window.at[pl.ds(pl.multiple_of(at, EDGE), rows)]
        copies.append(pltpu.make_async_copy(ref.at[pl.ds(row, rows)], to, sems.at[number]))
        if ref is left_direct or ref is right_direct:
            other = pltpu.make_async_copy(
                left_relayed if ref is left_direct else right_relayed, to, sems.at[number]
            )
            here = core == (0 if ref is left_direct else 1)
            pl.when(here)(copies[-1].start)
            pl.when(jnp.logical_not(here))(other.start)
        else:
            copies[-1].start()
    for copy in copies:
        copy.wait()


def forward_kernel(heads, W, QB, KB, lo_ref, count_ref, place_ref, se_ref, q_ref, *refs):
    *pieces, o_ref, lse_ref, window, sems, top_s, sum_s, acc_s = refs
    fetch_window(pieces, place_ref, q_ref.shape[0], window, sems)
    spans = head_spans(heads)

    def query_block(i, carry):
        r = pl.multiple_of(i * QB, QB)
        top_s[...] = jnp.full(top_s.shape, NEGATIVE, F32)
        sum_s[...] = jnp.zeros(sum_s.shape, F32)
        acc_s[...] = jnp.zeros(acc_s.shape, F32)
        st = se_ref[0:1, pl.ds(r, QB)]
        en = se_ref[1:2, pl.ds(r, QB)]

        def chunk(c, inner):
            k0 = pl.multiple_of(lo_ref[i] + c * KB, 16)
            at = k0 + lax.broadcasted_iota(jnp.int32, (KB, QB), 0)
            mask = (at >= st) & (at < en)
            for h in range(heads):
                t, w, off = spans[h]
                q = q_ref[pl.ds(r, QB), t : t + w] * head_ones(w, off)
                v = window[pl.ds(k0, KB), W + t : W + t + w]
                s = dot_on(window[pl.ds(k0, KB), t : t + w], q, 1, 1)
                s = jnp.where(mask, s, NEGATIVE)
                before = top_s[h : h + 1, :]
                top = jnp.maximum(before, jnp.max(s, axis=0, keepdims=True))
                p = jnp.exp2(s - top)
                shrink = jnp.exp2(before - top)
                sum_s[h : h + 1, :] = sum_s[h : h + 1, :] * shrink + jnp.sum(p, axis=0, keepdims=True)
                acc_s[h, :w, :] = acc_s[h, :w, :] * shrink + dot_on(v, p.astype(BF), 0, 0)
                top_s[h : h + 1, :] = top
            return inner

        lax.fori_loop(0, count_ref[i], chunk, 0)
        for h in range(heads):
            t, w, off = spans[h]
            o = (acc_s[h, :w, :] / sum_s[h : h + 1, :]).T.astype(BF)
            o_ref[pl.ds(r, QB), t : t + w] = jnp.where(
                in_head(QB, w, off), o, o_ref[pl.ds(r, QB), t : t + w]
            )
        lse_ref[:, pl.ds(r, QB)] = top_s[...] + jnp.log2(sum_s[...])
        return carry

    lax.fori_loop(0, q_ref.shape[0] // QB, query_block, 0)


SMEM = pl.BlockSpec(memory_space=pltpu.SMEM)
VMEM = pl.BlockSpec(memory_space=pltpu.VMEM)
ANY = pl.BlockSpec(memory_space=pl.ANY)


def attend_forward(q, pieces, ranges, swap, heads, QB=256, KB=768):
    st, en = ranges
    FR, W = q.shape
    rows = 3 * FR + 2 * EDGE
    lo, count = key_chunks(st, en, QB, KB, rows)
    return pl.pallas_call(
        functools.partial(forward_kernel, heads, W, QB, KB),
        out_shape=(
            jax.ShapeDtypeStruct((FR, W), BF),
            jax.ShapeDtypeStruct((heads, FR), F32),
        ),
        in_specs=[SMEM] * 3 + [VMEM] * 2 + [ANY] * len(pieces),
        out_specs=(VMEM, VMEM),
        scratch_shapes=[
            pltpu.VMEM((rows, 2 * W), BF),
            pltpu.SemaphoreType.DMA((8,)),
            pltpu.VMEM((heads, QB), F32),
            pltpu.VMEM((heads, QB), F32),
            pltpu.VMEM((heads, 256, QB), F32),
        ],
        compiler_params=pltpu.CompilerParams(vmem_limit_bytes=56 << 20),
        cost_estimate=pl.CostEstimate(flops=0, bytes_accessed=0, transcendentals=0),
        name="attend_forward",
    )(lo, count, swap, jnp.stack((st, en)), q, *pieces)


def backward_kernel(
    heads, W, QB, KB, lo_ref, count_ref, swap_ref, se_ref, lse_ref, delta_ref, q_ref, do_ref, *refs
):
    *refs, window, grads, dq_s, sems = refs
    number = len(refs) - 6
    pieces, dq_ref, outs = refs[:number], refs[number], refs[number + 1 :]
    swap = swap_ref[0]
    fetch_window(pieces, swap_ref, q_ref.shape[0], window, sems)
    spans = head_spans(heads)
    grads[...] = jnp.zeros(grads.shape, F32)

    def query_block(i, carry):
        r = pl.multiple_of(i * QB, QB)
        dq_s[...] = jnp.zeros(dq_s.shape, F32)
        st = se_ref[0:1, pl.ds(r, QB)]
        en = se_ref[1:2, pl.ds(r, QB)]

        def chunk(c, inner):
            k0 = pl.multiple_of(lo_ref[i] + c * KB, 16)
            at = k0 + lax.broadcasted_iota(jnp.int32, (KB, QB), 0)
            mask = (at >= st) & (at < en)
            for h in range(heads):
                t, w, off = spans[h]
                ones = head_ones(w, off)
                q = q_ref[pl.ds(r, QB), t : t + w] * ones
                do = do_ref[pl.ds(r, QB), t : t + w] * ones
                k = window[pl.ds(k0, KB), t : t + w]
                v = window[pl.ds(k0, KB), W + t : W + t + w]
                s = dot_on(k, q, 1, 1)
                p = jnp.exp2(jnp.where(mask, s - lse_ref[h : h + 1, pl.ds(r, QB)], NEGATIVE))
                dp = dot_on(v, do, 1, 1)
                ds = (p * (dp - delta_ref[h : h + 1, pl.ds(r, QB)])).astype(BF)
                grads[pl.ds(k0, KB), W + t : W + t + w] += dot_on(p.astype(BF), do, 1, 0)
                grads[pl.ds(k0, KB), t : t + w] += dot_on(ds, q, 1, 0)
                dq_s[h, :, :w] += dot_on(ds, k, 0, 0)
            return inner

        lax.fori_loop(0, count_ref[i], chunk, 0)
        for h in range(heads):
            t, w, off = spans[h]
            dq = (dq_s[h, :, :w] * SCALE).astype(BF)
            dq_ref[pl.ds(r, QB), t : t + w] = jnp.where(
                in_head(QB, w, off), dq, dq_ref[pl.ds(r, QB), t : t + w]
            )
        return carry

    lax.fori_loop(0, q_ref.shape[0] // QB, query_block, 0)
    for ref, row, at, rows in window_parts(outs, swap, q_ref.shape[0]):

        def store(j, carry, ref=ref, row=row, at=at):
            to = pl.multiple_of(row + j * 128, 128)
            here = pl.multiple_of(at + j * 128, 128)
            ref[pl.ds(to, 128), :W] = (grads[pl.ds(here, 128), :W] * math.log(2.0)).astype(BF)
            ref[pl.ds(to, 128), W:] = grads[pl.ds(here, 128), W:].astype(BF)
            return carry

        lax.fori_loop(0, rows // 128, store, 0)


def attend_backward(q, do, pieces, ranges, lse, delta, swap, heads, QB=256, KB=768):
    st, en = ranges
    FR, W = q.shape
    rows = 3 * FR + 2 * EDGE
    lo, count = key_chunks(st, en, QB, KB, rows)
    grads = [(piece, 2 * W) for piece in (EDGE, FR, FR, FR, EDGE)]
    return pl.pallas_call(
        functools.partial(backward_kernel, heads, W, QB, KB),
        out_shape=(jax.ShapeDtypeStruct((FR, W), BF),)
        + tuple(jax.ShapeDtypeStruct(shape, BF) for shape in grads),
        in_specs=[SMEM] * 3 + [VMEM] * 5 + [ANY] * len(pieces),
        out_specs=(VMEM,) * (1 + len(grads)),
        scratch_shapes=[
            pltpu.VMEM((rows, 2 * W), BF),
            pltpu.VMEM((rows, 2 * W), F32),
            pltpu.VMEM((heads, QB, 256), F32),
            pltpu.SemaphoreType.DMA((8,)),
        ],
        compiler_params=pltpu.CompilerParams(vmem_limit_bytes=60 << 20),
        cost_estimate=pl.CostEstimate(flops=0, bytes_accessed=0, transcendentals=0),
        name="attend_backward",
    )(lo, count, swap, jnp.stack((st, en)), lse, delta, q, do, *pieces)


def key_chunks(st, en, QB, KB, rows):
    lo = st[::QB] // 16 * 16
    count = (en[QB - 1 :: QB] - lo + KB - 1) // KB
    return jnp.minimum(lo, rows - count * KB), count


STEP = 256
FREE = pl.CostEstimate(flops=0, bytes_accessed=0, transcendentals=0)


def once(shape):
    return pl.BlockSpec(shape, lambda i: (0,) * len(shape), pipeline_mode=pl.Buffered(1))


def width_of(n, limit):
    return max(w for w in range(128, min(n, limit) + 1, 128) if n % w == 0)


def dense(xs, weights, n, product, finish, outs, extras=(), name="dense", width=512):
    weight, weight_spec = weights

    def kernel(*refs):
        x_refs, refs = refs[: len(xs)], refs[len(xs) :]
        w_ref, refs = refs[0], refs[1:]
        extra_refs, out_refs = refs[: len(extras)], refs[len(extras) :]
        w = w_ref[...].reshape(w_ref.shape[-2:])
        base = 0
        for x_ref in x_refs:
            for row in range(0, x_ref.shape[0], STEP):
                rows = min(STEP, x_ref.shape[0] - row)
                finish(product(x_ref[row : row + rows, :], w), base + row, extra_refs, out_refs)
            base += x_ref.shape[0]

    return pl.pallas_call(
        kernel,
        grid=(n // width,),
        in_specs=[once(x.shape) for x in xs] + [weight_spec] + [spec for _, spec in extras],
        out_specs=tuple(spec for _, _, spec in outs),
        out_shape=tuple(jax.ShapeDtypeStruct(shape, kind) for shape, kind, _ in outs),
        compiler_params=pltpu.CompilerParams(vmem_limit_bytes=56 << 20),
        cost_estimate=FREE,
        name=name,
    )(*xs, weight, *[x for x, _ in extras])


def count_rows(xs):
    return sum(x.shape[0] for x in xs)


def project_rows(xs, weight, first, n, bias, scale, name):
    weight, layer = weight
    rows, depth = count_rows(xs), weight.shape[1]
    width = math.gcd(width_of(n, 640), first) if first else width_of(n, 640)

    def finish(result, row, extra, out):
        out[0][row : row + result.shape[0], :] = ((result + extra[0][...]) * scale).astype(BF)

    return dense(
        xs,
        (weight, pl.BlockSpec((1, depth, width), lambda i: (layer, 0, i + first // width))),
        n,
        lambda x, w: dot_on(x, w, 1, 0),
        finish,
        [((rows, n), BF, pl.BlockSpec((rows, width), lambda i: (0, i)))],
        [(bias[None, :], pl.BlockSpec((1, width), lambda i: (0, i)))],
        name,
        width,
    )[0]


def widen_rows(xs, weight, bias):
    fc_all, layer = weight
    rows, depth, n = count_rows(xs), fc_all.shape[1], fc_all.shape[2]
    width = width_of(n, 512)

    def finish(result, row, extra, out):
        active, slope = gelu_both(result + extra[0][...])
        out[0][row : row + result.shape[0], :] = active
        out[1][row : row + result.shape[0], :] = slope

    spec = pl.BlockSpec((rows, width), lambda i: (0, i))
    return dense(
        xs,
        (fc_all, pl.BlockSpec((1, depth, width), lambda i: (layer, 0, i))),
        n,
        lambda x, w: dot_on(x, w, 1, 0),
        finish,
        [((rows, n), BF, spec)] * 2,
        [(bias[None, :], pl.BlockSpec((1, width), lambda i: (0, i)))],
        "widen",
        width,
    )


def slope_rows(xs, weight, slope):
    fc_all, layer = weight
    rows, depth, n = count_rows(xs), fc_all.shape[1], fc_all.shape[2]
    width = width_of(n, 512)

    def finish(result, row, extra, out):
        grad = (result * extra[0][row : row + result.shape[0], :].astype(F32)).astype(BF)
        out[0][row : row + result.shape[0], :] = grad
        total = jnp.sum(grad.astype(F32), axis=0, keepdims=True)
        out[1][...] = total if row == 0 else out[1][...] + total

    spec = pl.BlockSpec((rows, width), lambda i: (0, i))
    return dense(
        xs,
        (fc_all, pl.BlockSpec((1, depth, width), lambda i: (layer, 0, i))),
        n,
        lambda x, w: dot_on(x, w, 1, 0),
        finish,
        [((rows, n), BF, spec), ((1, n), F32, pl.BlockSpec((1, width), lambda i: (0, i)))],
        [(slope, spec)],
        "grad_hidden",
        width,
    )


def back_rows(xs, weight, columns, name):
    weight, layer = weight
    rows = xs[0].shape[0]
    n = weight.shape[-2]
    width = width_of(n, 256)
    half = rows // 2 if lax.axis_size("tensor") == 2 else 0
    depth = weight.shape[-1]

    def kernel(*refs):
        x_refs, w_ref, out_refs = refs[: len(xs)], refs[len(xs)], refs[len(xs) + 1 :]
        w = w_ref[...].reshape(w_ref.shape[-2:])
        for row in range(0, rows, STEP):
            result = sum(
                dot_on(x_ref[row : row + STEP, :], w[:, c : c + x_ref.shape[1]], 1, 1)
                for x_ref, c in zip(x_refs, columns)
            )
            if row < half:
                out_refs[0][row : row + STEP, :] = result
            else:
                out_refs[-1][row - half : row - half + STEP, :] = result.astype(BF)

    w_spec = pl.BlockSpec((1, width, depth), lambda i: (layer, i, 0))
    kinds = [(half, F32)] if half else []
    kinds.append((rows - half, BF))
    return pl.pallas_call(
        kernel,
        grid=(n // width,),
        in_specs=[once(x.shape) for x in xs] + [w_spec],
        out_specs=tuple(pl.BlockSpec((r, width), lambda i: (0, i)) for r, _ in kinds),
        out_shape=tuple(jax.ShapeDtypeStruct((r, n), kind) for r, kind in kinds),
        compiler_params=pltpu.CompilerParams(vmem_limit_bytes=56 << 20),
        cost_estimate=FREE,
        name=name,
    )(*xs, weight)


def weight_terms(parts, n, kind, start=None, place=None, name="weight_terms"):
    depth = parts[0][1][0][0].shape[1]
    height = width_of(depth, 256)
    xs, ys = [], []
    plan = []
    for column, pairs in parts:
        for x, y, row in pairs:
            if not any(x is known for known in xs):
                xs.append(x)
            if not any(y is known for known in ys):
                ys.append(y)
        plan.append(
            (
                column,
                [
                    (
                        next(k for k, known in enumerate(xs) if known is x),
                        next(k for k, known in enumerate(ys) if known is y),
                        row,
                    )
                    for x, y, row in pairs
                ],
            )
        )
    more = []
    if start is not None:
        more.append(start)
    if place is not None and place[1] is not None:
        more.append(place[1])

    def kernel(*refs):
        x_refs, refs = refs[: len(xs)], refs[len(xs) :]
        y_refs, refs = refs[: len(ys)], refs[len(ys) :]
        out_ref = refs[-1]

        def store(a, b, value):
            if place is None:
                out_ref[:, a:b] = value.astype(kind)
            else:
                out_ref[0, :, a:b] = value.astype(kind)

        done = []
        for column, pairs in plan:
            span = y_refs[pairs[0][1]].shape[1]
            width = width_of(span, 640)
            for c in range(0, span, width):
                total = None if start is None else refs[0][:, column + c : column + c + width]
                for x, y, row in pairs:
                    count = x_refs[x].shape[0]
                    part = dot_on(x_refs[x][...], y_refs[y][row : row + count, c : c + width], 0, 0)
                    total = part if total is None else total + part
                store(column + c, column + c + width, total)
            done.append((column, column + span))
        edge = 0
        for a, b in sorted(done) + [(n, n)]:
            if a > edge:
                rest = jnp.zeros((height, a - edge), F32) if start is None else refs[0][:, edge:a]
                store(edge, a, rest)
            edge = b

    x_spec = [pl.BlockSpec((x.shape[0], height), lambda i: (0, i)) for x in xs]
    more_spec = []
    if start is not None:
        more_spec.append(pl.BlockSpec((height, n), lambda i: (i, 0)))
    aliases = {}
    if place is None:
        shape, spec = (depth, n), pl.BlockSpec((height, n), lambda i: (i, 0))
    else:
        slot = place[0]
        shape, spec = (2, depth, n), pl.BlockSpec((1, height, n), lambda i: (slot, i, 0))
        if place[1] is not None:
            more_spec.append(ANY)
            aliases = {len(xs) + len(ys) + len(more) - 1: 0}
    return pl.pallas_call(
        kernel,
        grid=(depth // height,),
        in_specs=x_spec + [once(y.shape) for y in ys] + more_spec,
        out_specs=spec,
        out_shape=jax.ShapeDtypeStruct(shape, kind),
        input_output_aliases=aliases,
        compiler_params=pltpu.CompilerParams(vmem_limit_bytes=60 << 20),
        cost_estimate=FREE,
        name=name,
    )(*xs, *ys, *more)


def over_dp(x, by, start=0, step=1):
    length = lax.axis_size("dp")
    pairs = [(i, i + by) for i in range(start, length, step) if 0 <= i + by < length]
    return lax.ppermute(x, "dp", pairs)


def near_rows(kv, swap):
    half = kv.shape[0] // 2

    def head(x):
        return lax.dynamic_slice_in_dim(x, swap * half, EDGE)

    def tail(x):
        return lax.dynamic_slice_in_dim(x, (1 - swap) * half, EDGE)

    left, right = over_dp(kv, 1), over_dp(kv, -1)
    far_left, far_right = over_dp(tail(kv), 2, 0, 2), over_dp(head(kv), -2, 1, 2)
    return (
        far_left,
        over_dp(tail(left), 1, 0, 2),
        left,
        kv,
        right,
        far_right,
        over_dp(head(right), -1, 1, 2),
    )


def to_half(whole, part, second):
    half = whole.shape[0] // 2
    zero = jnp.zeros((), F32)
    part = part.astype(F32)
    wide = jnp.concatenate((jnp.where(second == 0, part, zero), jnp.where(second == 1, part, zero)))
    return whole.astype(F32) + wide


def return_rows(grads):
    g_l2, g_l1, own, g_r1, g_r2 = grads
    return own, over_dp(g_l1, -1), over_dp(g_r1, 1), over_dp(g_l2, -2), over_dp(g_r2, 2)


def add_returned(parts, swap):
    own, from_right, from_left, for_tail, for_head = parts
    total = own.astype(F32) + from_right.astype(F32) + from_left.astype(F32)
    return to_half(to_half(total, for_tail, 1 - swap), for_head, swap).astype(BF)


def sum_everywhere(x, axis):
    length = lax.axis_size(axis)
    bit = 1
    while bit < length:
        x = x + lax.ppermute(x, axis, [(i, i ^ bit) for i in range(length)])
        bit *= 2
    return x


class Order:
    def __init__(self):
        self.last = None

    def after(self, x, *more):
        if self.last is not None:
            more += (self.last,)
        return lax.optimization_barrier((x, *more))[0] if more else x

    def done(self, x):
        self.last = x
        return x


def partner(x):
    return lax.ppermute(x, "tensor", [(0, 1), (1, 0)])


def collect(x):
    if lax.axis_size("tensor") != 2:
        return [lax.all_gather(x, "tensor", axis=0, tiled=True)]
    return [x, partner(x)]


def share(parts):
    if len(parts) == 1:
        return lax.psum_scatter(parts[0], "tensor", scatter_dimension=0, tiled=True), jnp.zeros((), BF)
    return parts[0], partner(parts[1])


def norm_parts(x):
    centred = x - jnp.mean(x, axis=-1, keepdims=True)
    scale = lax.rsqrt(jnp.mean(centred * centred, axis=-1, keepdims=True) + EPSILON)
    return centred * scale, scale


def norm_back(grad, z, scale, gain):
    e = grad * gain
    mean_e = jnp.mean(e, axis=-1, keepdims=True)
    mean_ez = jnp.mean(e * z, axis=-1, keepdims=True)
    return scale * (e - mean_e - z * mean_ez)


def gelu_both(u):
    below = 0.5 * (1.0 + lax.erf(u * math.sqrt(0.5)))
    density = jnp.exp(-0.5 * u * u) * (1.0 / math.sqrt(2.0 * math.pi))
    return (u * below).astype(BF), (below + u * density).astype(BF)


def per_device(
    frames, cotangent, segment_ids, w_qkv, w_out, w_fc1, w_fc2, bias_qv, bias_fc1, norm_vectors
):
    dp_place = lax.axis_index("dp")
    paired = lax.axis_size("tensor") == 2
    swap = lax.axis_index("tensor").astype(jnp.int32) if paired else jnp.int32(0)
    own = frames.shape[1]
    FR = own * lax.axis_size("tensor")
    half = FR // 2
    rows = 2 * EDGE + 3 * FR
    local = w_qkv.shape[2]
    heads = local // HD
    W = -(-local // 128) * 128
    fill = W - local
    vectors = norm_vectors.astype(F32)

    def widened(x):
        return jnp.pad(x, [(0, 0)] * (x.ndim - 1) + [(0, fill)]) if fill else x

    attention = jnp.concatenate(
        (widened(w_qkv).reshape(w_qkv.shape[0], 3 * W), widened(w_out)), axis=1
    )
    if attention.shape == w_fc1.shape:
        every = lax.all_gather(jnp.stack((attention, w_fc1, w_fc2)), "dp", axis=1, tiled=True)
        att, fc1, fc2 = (every, 0), (every, 1), (every, 2)
    else:
        att = lax.all_gather(attention[None], "dp", axis=1, tiled=True), 0
        every = lax.all_gather(jnp.stack((w_fc1, w_fc2)), "dp", axis=1, tiled=True)
        fc1, fc2 = (every, 0), (every, 1)
    bias_q = widened(bias_qv[0].astype(F32))
    bias_kv = jnp.concatenate((jnp.zeros((W,), F32), widened(bias_qv[1].astype(F32))))
    chosen = (jnp.arange(W)[:, None] // HD == jnp.arange(heads)[None, :]).astype(F32)
    order = Order()

    class Batch:
        pass

    batches = []
    for b in range(MB):
        m = Batch()
        batches.append(m)
        m.z1, m.r1 = norm_parts(frames[b].astype(F32))
        m.h1_own = (m.z1 * vectors[0] + vectors[1]).astype(BF)
        ids = segment_ids[b]
        reach = FR + EDGE
        padded = jnp.concatenate(
            (jnp.full((reach,), -1, jnp.int32), ids, jnp.full((reach,), 1 << 30, jnp.int32))
        )
        near = lax.dynamic_slice_in_dim(padded, dp_place * FR, rows)
        mine = jnp.concatenate(
            (
                lax.dynamic_slice_in_dim(ids, dp_place * FR + swap * half, half),
                lax.dynamic_slice_in_dim(ids, dp_place * FR + (1 - swap) * half, half),
            )
        )
        m.ranges = (
            jnp.sum((near[None, :] < mine[:, None]).astype(jnp.int32), axis=1),
            jnp.sum((near[None, :] <= mine[:, None]).astype(jnp.int32), axis=1),
        )
    m0, m1 = batches
    place = jnp.stack((swap, dp_place.astype(jnp.int32) % 2))
    for m in batches:
        m.h1 = collect(m.h1_own)

    def gated(xs, *wait):
        *rest, x = xs
        return [*rest, order.after(x, *wait)]

    def keys_values(m):
        m.kv = order.done(project_rows(gated(m.h1), att, W, 2 * W, bias_kv, 1.0, "keys_values"))

    def queries(m):
        m.q = order.done(project_rows(gated(m.h1), att, 0, W, bias_q, LOG2E * SCALE, "queries"))

    def attend(m, *wait):
        m.mixed, m.lse = attend_forward(order.after(m.q, *wait), m.pieces, m.ranges, place, heads)
        order.done(m.mixed)
        parts = back_rows([m.mixed], att, [3 * W], "attended")
        m.attended, m.attended_far = share(parts)
        order.done(parts[0])

    def second_norm(m):
        near, far = m.attended, order.after(m.attended_far)
        m.middle = frames[m.b].astype(F32) + near.astype(F32) + far.astype(F32) + vectors[4]
        m.z2, m.r2 = norm_parts(m.middle)
        h2 = order.done((m.z2 * vectors[2] + vectors[3]).astype(BF))
        m.h2 = collect(h2)

    def widen(m):
        m.active, m.slope = widen_rows(gated(m.h2), fc1, bias_fc1.astype(F32))
        order.done(m.slope)

    def grad_hidden(m):
        m.grad_u, m.grad_u_sum = slope_rows(gated(m.grad_f), fc2, m.slope)
        order.done(m.grad_u)

    def grad_normed(m):
        parts = back_rows(gated([m.grad_u]), fc1, [0], "grad_normed")
        m.grad_h2, m.grad_h2_far = share(parts)
        order.done(parts[0])

    def narrow(m):
        m.fed_parts = back_rows(gated([m.active]), fc2, [0], "narrow")
        order.done(m.fed_parts[0])

    def send_narrow(m):
        *rest, last = m.fed_parts
        m.fed, m.fed_far = share([*rest, order.after(last)])

    def grad_second_norm(m):
        m.grad_rows = cotangent[m.b].astype(F32)
        m.grad_h2 = m.grad_h2.astype(F32) + order.after(m.grad_h2_far).astype(F32)
        m.grad_middle = m.grad_rows + norm_back(m.grad_h2, m.z2, m.r2, vectors[2])
        a = order.done(m.grad_middle.astype(BF))
        m.grad_a = collect(a)

    no_bias = jnp.zeros((W,), F32)

    def attend_back(m):
        m.grad_mixed = project_rows(
            gated(m.grad_a), att, 3 * W, W, no_bias, 1.0, "grad_mixed"
        )
        delta = lax.dot_general(
            chosen,
            m.grad_mixed.astype(F32) * m.mixed.astype(F32),
            (((0,), (1,)), ((), ())),
            precision=lax.Precision.HIGHEST,
        )
        m.grad_q, *grads = attend_backward(
            m.q, m.grad_mixed, m.pieces, m.ranges, m.lse, delta, place, heads
        )
        order.done(m.grad_q)
        m.returned = return_rows(grads)

    def add_up(m, *wait):
        m.grad_kv = order.done(add_returned([order.after(x, *wait) for x in m.returned], swap))

    def grad_projected(m):
        grad_kv = order.after(m.grad_kv)
        parts = back_rows([m.grad_q, grad_kv], att, [0, W], "grad_projected")
        m.grad_h1, m.grad_h1_far = share(parts)
        order.done(parts[0])

    def rows_of(xs, y):
        pairs, row = [], 0
        for x in xs:
            pairs.append((x, y, row))
            row += x.shape[0]
        return pairs

    def finish(m):
        grad_h1 = m.grad_h1.astype(F32) + order.after(m.grad_h1_far).astype(F32)
        m.inputs_grad = m.grad_middle + norm_back(grad_h1, m.z1, m.r1, vectors[0])
        order.done(m.inputs_grad)
        m.norm_sums = jnp.stack(
            (
                jnp.sum(grad_h1 * m.z1, axis=0),
                jnp.sum(grad_h1, axis=0),
                jnp.sum(m.grad_h2 * m.z2, axis=0),
                jnp.sum(m.grad_h2, axis=0),
                jnp.sum(m.grad_middle, axis=0),
                jnp.sum(m.grad_rows, axis=0),
            )
        )

    def owned(terms, axis):
        return lax.psum_scatter(terms.astype(BF), "dp", scatter_dimension=axis, tiled=True).astype(F32)

    m0.b, m1.b = 0, 1
    keys_values(m0)
    keys_values(m1)
    queries(m0)
    queries(m1)
    m0.pieces = near_rows(m0.kv, swap)
    first_arrived = [m0.pieces[k] for k in (0, 2, 4, 5)]
    m1.pieces = near_rows(lax.optimization_barrier((m1.kv, m1.q, *first_arrived))[0], swap)
    for m in batches:
        m.grad_f = collect(lax.optimization_barrier((cotangent[m.b], m1.h1[-1]))[0])

    def term(x, y, *wait, **how):
        pairs = rows_of(gated(x, *wait), y)
        return order.done(weight_terms([(0, pairs)], w_fc1.shape[1], **how))

    attend(m0, m0.grad_f[-1], m1.grad_f[-1])
    second_norm(m0)
    attend(m1)
    widen(m0)
    grad_hidden(m0)
    grad_normed(m0)
    second_norm(m1)
    narrow(m0)
    fc2_term = term(m0.grad_f, m0.active, kind=F32)
    grad_second_norm(m0)
    fc1_term = term(m0.h2, m0.grad_u, kind=F32)
    widen(m1)
    grad_hidden(m1)
    grad_normed(m1)
    fc_terms = term(
        m1.grad_f, m1.active, m0.grad_a[-1], kind=BF, start=fc2_term, place=(1, None)
    )
    grad_second_norm(m1)
    fc_terms = term(m1.h2, m1.grad_u, kind=BF, start=fc1_term, place=(0, fc_terms))
    own_fc1, own_fc2 = owned(fc_terms, 1)
    attend_back(m0)
    send_narrow(m0)
    attend_back(m1)
    narrow(m1)
    send_narrow(m1)
    terms = weight_terms(
        [
            (0, rows_of(gated(m0.h1), m0.grad_q) + rows_of(m1.h1, m1.grad_q)),
            (3 * W, rows_of(m0.grad_a, m0.mixed) + rows_of(m1.grad_a, m1.mixed)),
        ],
        4 * W,
        F32,
    )
    order.done(terms)
    add_up(m1, m0.fed_far, m1.fed_far, *m0.returned)
    add_up(m0)
    kv_pairs = rows_of(m0.h1, m0.grad_kv) + rows_of(m1.h1, m1.grad_kv)
    terms = order.done(weight_terms([(W, kv_pairs)], 4 * W, BF, start=terms))
    own_attention = owned(lax.optimization_barrier((terms, own_fc1))[0], 0)
    grad_projected(m0)
    grad_projected(m1)
    finish(m0)
    outputs = [
        (m.middle + m.fed.astype(F32) + order.after(m.fed_far).astype(F32) + vectors[5]).astype(BF)
        for m in batches
    ]
    finish(m1)
    own_qkv = own_attention[:, : 3 * W].reshape(own_attention.shape[0], 3, W)[:, :, :local]
    own_out = own_attention[:, 3 * W :][:, :local]

    bias_parts = (
        sum(jnp.sum(m.grad_q, axis=0, dtype=F32) for m in batches)[:local],
        sum(jnp.sum(m.grad_kv[:, W:], axis=0, dtype=F32) for m in batches)[:local],
        sum(m.grad_u_sum[0] for m in batches),
    )
    norm_sums = m0.norm_sums + m1.norm_sums
    small = sum_everywhere(jnp.concatenate(bias_parts + (norm_sums.reshape(-1),)), "dp")
    bias_qv_total = small[: 2 * local].reshape(2, local)
    bias_fc1_total = small[2 * local : 2 * local + w_fc1.shape[1]]
    norm_total = sum_everywhere(small[2 * local + w_fc1.shape[1] :], "tensor").reshape(norm_sums.shape)
    return (
        jnp.stack(outputs),
        jnp.stack([m.inputs_grad for m in batches]),
        own_qkv,
        own_out,
        own_fc1,
        own_fc2,
        bias_qv_total,
        bias_fc1_total,
        norm_total,
    )


def solution(mesh):
    in_specs = (
        P(None, ("dp", "tensor"), None),
        P(None, ("dp", "tensor"), None),
        P(),
        P("dp", None, "tensor"),
        P("dp", "tensor"),
        P("dp", "tensor"),
        P("dp", "tensor"),
        P(None, "tensor"),
        P("tensor"),
        P(),
    )
    out_specs = (
        P(None, ("dp", "tensor"), None),
        P(None, ("dp", "tensor"), None),
        P("dp", None, "tensor"),
        P("dp", "tensor"),
        P("dp", "tensor"),
        P("dp", "tensor"),
        P(None, "tensor"),
        P("tensor"),
        P(),
    )
    return jax.shard_map(
        per_device, mesh=mesh, in_specs=in_specs, out_specs=out_specs, check_vma=False
    )
```

time: 1320 us -> 1030 us (0.78)
  matrix products: 260 us -> 7.12 us
  Pallas kernels: 185 us -> 436 us
  blocking collectives: 195 us -> 0 us
  waiting for transfers between devices: 367 us -> 233 us
  starting transfers between devices: 206 us -> 229 us
  other arithmetic: 53.8 us -> 71.9 us
    pallas_call x0 -> x24, Pallas kernels: none -> 261 us  [the longest x10 90.5 us: dense(): pl.pallas_call(kernel, grid=(n // width,), in_specs=[once(x.shape) for x...]
    dot_general x42 -> x2, matrix products: 260 us -> 7.12 us  [attend_back(): lax.dot_general(chosen, m.grad_mixed.astype(F32) * m.mixed.astype(F32), (...]
    psum x2 -> x0, blocking collectives: 195 us -> none  [the longest x1 157 us: per_device(): lax.psum((jnp.stack((bias_q_sum, bias_v_sum))[:, :local], bias_fc1_sum),...]
    ppermute x16, waiting for transfers between devices: 164 us -> 68 us  [partner(): return lax.ppermute(x, 'tensor', [(0, 1), (1, 0)])]
    ppermute x16 -> x20, waiting for transfers between devices: 184 us -> 104 us  [over_dp(): return lax.ppermute(x, 'dp', pairs)]
    ppermute x0 -> x5, starting transfers between devices: none -> 60.6 us  [sum_everywhere(): x = x + lax.ppermute(x, axis, [(i, i ^ bit) for i in range(length)])]
    ppermute x16 -> x20, starting transfers between devices: 185 us -> 149 us  [over_dp(): return lax.ppermute(x, 'dp', pairs)]
    all_gather x4 -> x1, waiting for transfers between devices: 17.7 us -> 40.2 us  [per_device(): lax.all_gather(jnp.stack((attention, w_fc1, w_fc2)), 'dp', axis=1, tiled=...]
  transfers between devices with their start and end apart: 40 -> 44, of which waited for: 15 -> 17; matrix products, arithmetic and copies ran while one was open for 24% -> 9% of each run, Pallas kernels for 14% -> 41%
where the time goes in v2:
time: 1030 us; the launch traced here: 1020 us
  Pallas kernels  436 us (42%)
  waiting for transfers between devices  233 us (23%)
  starting transfers between devices  229 us (22%)
  other arithmetic  71.9 us (7%)
  local copies, waits for them, and re-layouts  32 us (3%)
  between operations  15.1 us (1%)
    ppermute x20, starting transfers between devices, over_dp(): return lax.ppermute(x, 'dp', pairs)  149 us
    ppermute x20, waiting for transfers between devices, over_dp(): return lax.ppermute(x, 'dp', pairs)  104 us
    pallas_call x2, Pallas kernels, attend_backward(): pl.pallas_call(functools.partial(backward_kernel, heads, W, QB, KB), out_...  100 us
    pallas_call x10, Pallas kernels, dense(): pl.pallas_call(kernel, grid=(n // width,), in_specs=[once(x.shape) for x...  90.5 us
    pallas_call x6, Pallas kernels, weight_terms(): pl.pallas_call(kernel, grid=(depth // height,), in_specs=x_spec + [once(y...  89.1 us
    pallas_call x8, Pallas kernels, back_rows(): pl.pallas_call(kernel, grid=(n // width,), in_specs=[once(x.shape) for x...  81.7 us
    pallas_call x2, Pallas kernels, attend_forward(): pl.pallas_call(functools.partial(forward_kernel, heads, W, QB, KB), out_s...  74.1 us
    ppermute x16, waiting for transfers between devices, partner(): return lax.ppermute(x, 'tensor', [(0, 1), (1, 0)])  68 us
  transfers between devices with their start and end apart: 44, of which 17 were waited for; matrix products, arithmetic and copies ran while one was open for 9% of the time, Pallas kernels for 41%

profile of v2, /device:TPU:0, one launch (start us, length us, event | category | flops | bytes accessed | tf_op | source)
XLA Modules:
  0.0 1023.7 jit_solution(17474968600020351148)
XLA Ops:
  24.3 24.5 %collective-permute-done.1.refs_1_.refs_3_ = bf16[512,1280]{1,0:T(8,128)(2,1)S(1)} collective-permute-done((bf16[512,1280]{1,0:T(8,128)(2,1)}, bf16[512,1280]{1,0:T(8,128)(2,1)S(1)}, u32[]{:S(2)}, u32[]{:S(2)}) %collective-permute-start.1) | collective-permute-done | bytes 1310752 | tf_op jit(solution)/shard_map/ppermute | solution.py:547
  50.9 26.0 %collective-permute-done.refs_1_ = bf16[512,1280]{1,0:T(8,128)(2,1)S(1)} collective-permute-done((bf16[512,1280]{1,0:T(8,128)(2,1)}, bf16[512,1280]{1,0:T(8,128)(2,1)S(1)}, u32[]{:S(2)}, u32[]{:S(2)}) %collective-permute-start) | collective-permute-done | bytes 1310752 | tf_op jit(solution)/shard_map/ppermute | solution.py:547
  76.9 40.2 %all-gather.2.cloned.1.call-done.refs_2_.refs_1_ = bf16[3,1280,2560]{2,1,0:T(8,128)(2,1)} async-done(((bf16[3,80,2560]{2,1,0:T(8,128)(2,1)}), bf16[3,1280,2560]{2,1,0:T(8,128)(2,1)}) %all-gather.2.cloned.1.call-update) | async-done | bytes 19660816 | tf_op jit(solution)/shard_map/all_gather | solution.py:604
  163.2 37.5 %collective-permute-done.4.refs_0_ = bf16[512,1280]{1,0:T(8,128)(2,1)} collective-permute-done((bf16[512,1280]{1,0:T(8,128)(2,1)}, bf16[512,1280]{1,0:T(8,128)(2,1)}, u32[]{:S(2)}, u32[]{:S(2)}) %collective-permute-start.4) | collective-permute-done | bytes 1310752 | tf_op jit(solution)/shard_map/ppermute | solution.py:479
  204.4 45.7 %collective-permute-start.6 = (bf16[512,1280]{1,0:T(8,128)(2,1)}, bf16[512,1280]{1,0:T(8,128)(2,1)}, u32[]{:S(2)}, u32[]{:S(2)}) collective-permute-start(bf16[512,1280]{1,0:T(8,128)(2,1)} %constant_dynamic-slice_fusion.8), channel_id=1, source_target_pairs={{0,2},{4,6},{8,10},{12,14},{16,18},{20,22},{24,26},{28,30},{1,3},{... | collective-permute-start | bytes 3932168 | tf_op jit(solution)/shard_map/ppermute | solution.py:479
  259.0 37.1 %attend_forward.2 = (bf16[1024,640]{1,0:T(8,128)(2,1)}, f32[8,1024]{1,0:T(8,128)}) custom-call(s32[4]{0:T(128)} %get-tuple-element.248.lo_ref, s32[4]{0:T(128)} %get-tuple-element.249.count_ref, s32[2]{0:T(128)} %pad_add_fusion.4.place_ref.swap_ref, s32[2,1024]{1,0:T(2,128)} %pad_add_fusion.se_ref, bf16[1024,640]{1,0:T(8,128)(2,1)} %queries.2.q_ref, ...), custom_call_target="tpu_custom_call" | custom-call | tf_op jit(solution)/shard_map/attend_forward/pallas_call | solution.py:131
  311.1 13.4 %collective-permute-start.12 = (bf16[512,1280]{1,0:T(8,128)(2,1)S(1)}, bf16[512,1280]{1,0:T(8,128)(2,1)}, u32[]{:S(2)}, u32[]{:S(2)}) collective-permute-start(bf16[512,1280]{1,0:T(8,128)(2,1)S(1)} %get-tuple-element.257), channel_id=1, source_target_pairs={{0,4},{4,8},{8,12},{12,16},{16,20},{20,24},{24,28},{1,5},{5,9},{9,... | collective-permute-start | bytes 3932168 | tf_op jit(solution)/shard_map/ppermute | solution.py:479
  341.4 37.0 %attend_forward.3 = (bf16[1024,640]{1,0:T(8,128)(2,1)}, f32[8,1024]{1,0:T(8,128)}) custom-call(s32[4]{0:T(128)} %get-tuple-element.250.lo_ref, s32[4]{0:T(128)} %get-tuple-element.251.count_ref, s32[2]{0:T(128)} %pad_add_fusion.4.place_ref.swap_ref, s32[2,1024]{1,0:T(2,128)} %pad_add_fusion.1.se_ref, bf16[1024,640]{1,0:T(8,128)(2,1)} %queries.3.q_ref, ...), custom_call_target="tpu_custom_call" | custom-call | tf_op jit(solution)/shard_map/attend_forward/pallas_call | solution.py:131
  387.0 14.0 %widen.2 = (bf16[1024,2560]{1,0:T(8,128)(2,1)}, bf16[1024,2560]{1,0:T(8,128)(2,1)}) custom-call(bf16[512,1280]{1,0:T(8,128)(2,1)} %copy-done.25, bf16[512,1280]{1,0:T(8,128)(2,1)} %collective-permute-done.11.refs_1_, bf16[3,1280,2560]{2,1,0:T(8,128)(2,1)} %all-gather.2.cloned.1.call-done.refs_2_.refs_1_, f32[1,2560]{1,0:T(1,128)} %reshape.160.refs_3_), custom_call_target="tpu_custom_call" | custom-call | tf_op jit(solution)/shard_map/widen/pallas_call | solution.py:268
  401.1 12.4 %grad_hidden.2 = (bf16[1024,2560]{1,0:T(8,128)(2,1)}, f32[1,2560]{1,0:T(1,128)}) custom-call(bf16[512,1280]{1,0:T(8,128)(2,1)} %get-tuple-element.97.refs_0_, bf16[512,1280]{1,0:T(8,128)(2,1)} %collective-permute-done.2.refs_1_, bf16[3,1280,2560]{2,1,0:T(8,128)(2,1)} %all-gather.2.cloned.1.call-done.refs_2_.refs_1_, ...), custom_call_target="tpu_custom_call" | custom-call | tf_op jit(solution)/shard_map/grad_hidden/pallas_call | solution.py:268
  413.4 11.5 %grad_normed.2 = (f32[512,1280]{1,0:T(8,128)}, bf16[512,1280]{1,0:T(8,128)(2,1)}) custom-call(bf16[1024,2560]{1,0:T(8,128)(2,1)} %get-tuple-element.115.refs_0_.refs_2_, bf16[3,1280,2560]{2,1,0:T(8,128)(2,1)} %all-gather.2.cloned.1.call-done.refs_2_.refs_1_), custom_call_target="tpu_custom_call" | custom-call | tf_op jit(solution)/shard_map/grad_normed/pallas_call | solution.py:378
  431.7 11.4 %narrow.2 = (f32[512,1280]{1,0:T(8,128)}, bf16[512,1280]{1,0:T(8,128)(2,1)}) custom-call(bf16[1024,2560]{1,0:T(8,128)(2,1)} %get-tuple-element.118.refs_0_.refs_2_, bf16[3,1280,2560]{2,1,0:T(8,128)(2,1)} %all-gather.2.cloned.1.call-done.refs_2_.refs_1_), custom_call_target="tpu_custom_call" | custom-call | tf_op jit(solution)/shard_map/narrow/pallas_call | solution.py:378
  443.1 13.7 %weight_terms.6.refs_3_ = f32[1280,2560]{1,0:T(8,128)} custom-call(bf16[512,1280]{1,0:T(8,128)(2,1)} %get-tuple-element.97.refs_0_, bf16[512,1280]{1,0:T(8,128)(2,1)} %collective-permute-done.2.refs_1_, bf16[1024,2560]{1,0:T(8,128)(2,1)} %get-tuple-element.118.refs_0_.refs_2_), custom_call_target="tpu_custom_call" | custom-call | tf_op jit(solution)/shard_map/weight_terms/pallas_call | solution.py:463
  465.0 13.4 %weight_terms.7.refs_3_ = f32[1280,2560]{1,0:T(8,128)} custom-call(bf16[512,1280]{1,0:T(8,128)(2,1)} %copy-done.25, bf16[512,1280]{1,0:T(8,128)(2,1)} %collective-permute-done.11.refs_1_, bf16[1024,2560]{1,0:T(8,128)(2,1)} %get-tuple-element.115.refs_0_.refs_2_), custom_call_target="tpu_custom_call" | custom-call | tf_op jit(solution)/shard_map/weight_terms/pallas_call | solution.py:463
  478.7 14.0 %widen.3 = (bf16[1024,2560]{1,0:T(8,128)(2,1)}, bf16[1024,2560]{1,0:T(8,128)(2,1)}) custom-call(bf16[512,1280]{1,0:T(8,128)(2,1)} %add_convert_fusion.2.refs_0_, bf16[512,1280]{1,0:T(8,128)(2,1)} %collective-permute-done.21.refs_1_, bf16[3,1280,2560]{2,1,0:T(8,128)(2,1)} %all-gather.2.cloned.1.call-done.refs_2_.refs_1_, f32[1,2560]{1,0:T(1,128)} %reshape.160.refs_3_), custom_call_target="tpu_custom_call" | custom-call | tf_op jit(solution)/shard_map/widen/pallas_call | solution.py:268
  492.7 12.4 %grad_hidden.3 = (bf16[1024,2560]{1,0:T(8,128)(2,1)}, f32[1,2560]{1,0:T(1,128)}) custom-call(bf16[512,1280]{1,0:T(8,128)(2,1)} %get-tuple-element.98.refs_0_, bf16[512,1280]{1,0:T(8,128)(2,1)} %collective-permute-done.3.refs_1_, bf16[3,1280,2560]{2,1,0:T(8,128)(2,1)} %all-gather.2.cloned.1.call-done.refs_2_.refs_1_, ...), custom_call_target="tpu_custom_call" | custom-call | tf_op jit(solution)/shard_map/grad_hidden/pallas_call | solution.py:268
  505.1 11.4 %grad_normed.3 = (f32[512,1280]{1,0:T(8,128)}, bf16[512,1280]{1,0:T(8,128)(2,1)}) custom-call(bf16[1024,2560]{1,0:T(8,128)(2,1)} %get-tuple-element.130.refs_0_.refs_2_, bf16[3,1280,2560]{2,1,0:T(8,128)(2,1)} %all-gather.2.cloned.1.call-done.refs_2_.refs_1_), custom_call_target="tpu_custom_call" | custom-call | tf_op jit(solution)/shard_map/grad_normed/pallas_call | solution.py:378
  518.0 15.5 %weight_terms.8.refs_4_ = bf16[2,1280,2560]{2,1,0:T(8,128)(2,1)} custom-call(bf16[512,1280]{1,0:T(8,128)(2,1)} %get-tuple-element.98.refs_0_, bf16[512,1280]{1,0:T(8,128)(2,1)} %collective-permute-done.3.refs_1_, bf16[1024,2560]{1,0:T(8,128)(2,1)} %get-tuple-element.145.refs_2_.refs_0_, f32[1280,2560]{1,0:T(8,128)} %weight_terms.6.refs_3_), custom_call_target="tpu_custom_call" | custom-call | tf_op jit(solution)/shard_map/weight_terms/pallas_call | solution.py:463
  544.1 15.4 %weight_terms.9 = bf16[2,1280,2560]{2,1,0:T(8,128)(2,1)} custom-call(bf16[512,1280]{1,0:T(8,128)(2,1)} %add_convert_fusion.2.refs_0_, bf16[512,1280]{1,0:T(8,128)(2,1)} %collective-permute-done.21.refs_1_, bf16[1024,2560]{1,0:T(8,128)(2,1)} %get-tuple-element.130.refs_0_.refs_2_, f32[1280,2560]{1,0:T(8,128)} %weight_terms.7.refs_3_, ...), custom_call_target="tpu_custom_call", output_to_operand_aliasing={{}: (4, {})} | custom-call | tf_op jit(solution)/shard_map/weight_terms/pallas_call | solution.py:463
  570.9 50.3 %attend_backward.2 = (bf16[1024,640]{1,0:T(8,128)(2,1)}, bf16[512,1280]{1,0:T(8,128)(2,1)}, bf16[1024,1280]{1,0:T(8,128)(2,1)}, bf16[1024,1280]{1,0:T(8,128)(2,1...) custom-call(s32[4]{0:T(128)} %get-tuple-element.248.lo_ref, s32[4]{0:T(128)} %get-tuple-element.249.count_ref, ...), custom_call_target="tpu_custom_call" | custom-call | tf_op jit(solution)/shard_map/attend_backward/pallas_call | solution.py:217
  622.7 30.2 %collective-permute-start.29 = (bf16[512,1280]{1,0:T(8,128)(2,1)}, bf16[512,1280]{1,0:T(8,128)(2,1)}, u32[]{:S(2)}, u32[]{:S(2)}) collective-permute-start(bf16[512,1280]{1,0:T(8,128)(2,1)} %get-tuple-element.152), channel_id=1, source_target_pairs={{0,4},{2,6},{4,8},{6,10},{8,12},{10,14},{12,16},{14,18},{16,20},{1... | collective-permute-start | bytes 3932168 | tf_op jit(solution)/shard_map/ppermute | solution.py:479
  668.3 49.9 %attend_backward.3 = (bf16[1024,640]{1,0:T(8,128)(2,1)}, bf16[512,1280]{1,0:T(8,128)(2,1)}, bf16[1024,1280]{1,0:T(8,128)(2,1)}, bf16[1024,1280]{1,0:T(8,128)(2,1...) custom-call(s32[4]{0:T(128)} %get-tuple-element.250.lo_ref, s32[4]{0:T(128)} %get-tuple-element.251.count_ref, ...), custom_call_target="tpu_custom_call" | custom-call | tf_op jit(solution)/shard_map/attend_backward/pallas_call | solution.py:217
  718.2 11.6 %narrow.3 = (f32[512,1280]{1,0:T(8,128)}, bf16[512,1280]{1,0:T(8,128)(2,1)}) custom-call(bf16[1024,2560]{1,0:T(8,128)(2,1)} %get-tuple-element.145.refs_2_.refs_0_, bf16[3,1280,2560]{2,1,0:T(8,128)(2,1)} %all-gather.2.cloned.1.call-done.refs_2_.refs_1_), custom_call_target="tpu_custom_call" | custom-call | tf_op jit(solution)/shard_map/narrow/pallas_call | solution.py:378
  731.5 13.9 %collective-permute-start.33 = (bf16[512,1280]{1,0:T(8,128)(2,1)S(1)}, bf16[512,1280]{1,0:T(8,128)(2,1)}, u32[]{:S(2)}, u32[]{:S(2)}) collective-permute-start(bf16[512,1280]{1,0:T(8,128)(2,1)S(1)} %copy-done.58), channel_id=1, source_target_pairs={{0,4},{2,6},{4,8},{6,10},{8,12},{10,14},{12,16},{14,18},{16,20},{1... | collective-permute-start | bytes 3932168 | tf_op jit(solution)/shard_map/ppermute | solution.py:479
  753.9 11.1 %collective-permute-start.31 = (bf16[1024,1280]{1,0:T(8,128)(2,1)}, bf16[1024,1280]{1,0:T(8,128)(2,1)S(1)}, u32[]{:S(2)}, u32[]{:S(2)}) collective-permute-start(bf16[1024,1280]{1,0:T(8,128)(2,1)} %get-tuple-element.157), channel_id=1, source_target_pairs={{0,2},{2,4},{4,6},{6,8},{8,10},{10,12},{12,14},{14,16},{16,18},{18... | collective-permute-start | bytes 7864328 | tf_op jit(solution)/shard_map/ppermute | solution.py:479
  765.0 48.7 %collective-permute-done.33 = bf16[512,1280]{1,0:T(8,128)(2,1)} collective-permute-done((bf16[512,1280]{1,0:T(8,128)(2,1)S(1)}, bf16[512,1280]{1,0:T(8,128)(2,1)}, u32[]{:S(2)}, u32[]{:S(2)}) %collective-permute-start.33) | collective-permute-done | bytes 1310752 | tf_op jit(solution)/shard_map/ppermute | solution.py:479
  815.4 15.5 %weight_terms.10.refs_6_ = f32[1280,2560]{1,0:T(8,128)} custom-call(bf16[512,1280]{1,0:T(8,128)(2,1)} %get-tuple-element.252.refs_0_, bf16[512,1280]{1,0:T(8,128)(2,1)} %copy-done.16, bf16[512,1280]{1,0:T(8,128)(2,1)} %get-tuple-element.253.refs_0_.refs_2_, bf16[512,1280]{1,0:T(8,128)(2,1)} %copy-done.15, bf16[512,1280]{1,0:T(8,128)(2,1)} %copy-done.23, ...), custom_call_target="tpu_custom_call" | custom-call | tf_op jit(solution)/shard_map/weight_terms/pallas_call | solution.py:463
  834.4 11.6 %collective-permute-done.30 = bf16[1024,1280]{1,0:T(8,128)(2,1)} collective-permute-done((bf16[1024,1280]{1,0:T(8,128)(2,1)}, bf16[1024,1280]{1,0:T(8,128)(2,1)}, u32[]{:S(2)}, u32[]{:S(2)}) %collective-permute-start.30) | collective-permute-done | bytes 2621472 | tf_op jit(solution)/shard_map/ppermute | solution.py:479
  858.3 15.6 %weight_terms.11 = bf16[1280,2560]{1,0:T(8,128)(2,1)} custom-call(bf16[512,1280]{1,0:T(8,128)(2,1)} %get-tuple-element.252.refs_0_, bf16[512,1280]{1,0:T(8,128)(2,1)} %copy-done.16, bf16[512,1280]{1,0:T(8,128)(2,1)} %get-tuple-element.253.refs_0_.refs_2_, bf16[512,1280]{1,0:T(8,128)(2,1)} %copy-done.15, bf16[1024,1280]{1,0:T(8,128)(2,1)} %fusion.3.refs_4_.refs_1_, ...), custom_call_target="tpu_custom_call" | custom-call | tf_op jit(solution)/shard_map/weight_terms/pallas_call | solution.py:463
  888.3 10.7 %grad_projected.3 = (f32[512,1280]{1,0:T(8,128)}, bf16[512,1280]{1,0:T(8,128)(2,1)}) custom-call(bf16[1024,640]{1,0:T(8,128)(2,1)} %get-tuple-element.144.refs_9_.refs_0_, bf16[1024,1280]{1,0:T(8,128)(2,1)} %fusion.1.refs_5_.refs_1_, bf16[3,1280,2560]{2,1,0:T(8,128)(2,1)} %all-gather.2.cloned.1.call-done.refs_2_.refs_1_), custom_call_target="tpu_custom_call" | custom-call | tf_op jit(solution)/shard_map/grad_projected/pallas_call | solution.py:378
  920.2 49.1 %collective-permute-start.36 = (f32[11520]{0:T(1024)S(1)}, f32[11520]{0:T(1024)S(1)}, u32[]{:S(2)}, u32[]{:S(2)}) collective-permute-start(f32[11520]{0:T(1024)S(1)} %pad_maximum_fusion.3), channel_id=1, source_target_pairs={{0,2},{2,0},{4,6},{6,4},{8,10},{10,8},{12,14},{14,12},{16,18},{18,... | collective-permute-start | bytes 138248 | tf_op jit(solution)/shard_map/ppermute | solution.py:527
  1000.5 13.0 %reduce-scatter.5.cloned.1.call-done = bf16[80,2560]{1,0:T(8,128)(2,1)} async-done(((bf16[1280,2560]{1,0:T(8,128)(2,1)}), bf16[80,2560]{1,0:T(8,128)(2,1)}) %reduce-scatter.5.cloned.1.call-update) | async-done | bytes 409616 | tf_op jit(solution)/shard_map/reduce_scatter | solution.py:747
  (325 shorter events, 270.7 us)
Async XLA Ops:
  7.2 109.9 %all-gather.2.cloned.1.call-start = ((), (), s32[]{:S(2)}) async-start(), calls=%async_computation.2 | async-start | bytes 20889600 | tf_op jit(solution)/shard_map/all_gather | solution.py:604
  11.6 862.3 %reduce-scatter.3.cloned.1.call-start = ((), (), s32[]{:S(2)}) async-start(), calls=%async_computation.3 | async-start | bytes 13926400 | tf_op jit(solution)/shard_map/reduce_scatter | solution.py:747
  16.0 32.8 %collective-permute-start.1 = (bf16[512,1280]{1,0:T(8,128)(2,1)}, bf16[512,1280]{1,0:T(8,128)(2,1)S(1)}, u32[]{:S(2)}, u32[]{:S(2)}) collective-permute-start(bf16[512,1280]{1,0:T(8,128)(2,1)} %get-tuple-element.253.refs_0_.refs_2_), channel_id=1, source_target_pairs={{0,1},{1,0},{2,3},{3,2},{4,5},{5,4},{6,7},{7,6},{8,9},{9,8},{10,11... | collective-permute-start | bytes 3932168 | tf_op jit(solution)/shard_map/ppermute | solution.py:547
  19.0 57.9 %collective-permute-start = (bf16[512,1280]{1,0:T(8,128)(2,1)}, bf16[512,1280]{1,0:T(8,128)(2,1)S(1)}, u32[]{:S(2)}, u32[]{:S(2)}) collective-permute-start(bf16[512,1280]{1,0:T(8,128)(2,1)} %get-tuple-element.252.refs_0_), channel_id=1, source_target_pairs={{0,1},{1,0},{2,3},{3,2},{4,5},{5,4},{6,7},{7,6},{8,9},{9,8},{10,11... | collective-permute-start | bytes 3932168 | tf_op jit(solution)/shard_map/ppermute | solution.py:547
  48.8 201.4 %collective-permute-start.2 = (bf16[512,1280]{1,0:T(8,128)(2,1)}, bf16[512,1280]{1,0:T(8,128)(2,1)}, u32[]{:S(2)}, u32[]{:S(2)}) collective-permute-start(bf16[512,1280]{1,0:T(8,128)(2,1)} %get-tuple-element.97.refs_0_), channel_id=1, source_target_pairs={{0,1},{1,0},{2,3},{3,2},{4,5},{5,4},{6,7},{7,6},{8,9},{9,8},{10,11... | collective-permute-start | bytes 3932168 | tf_op jit(solution)/shard_map/ppermute | solution.py:547
  124.9 33.0 %collective-permute-start.7 = (bf16[1024,1280]{1,0:T(8,128)(2,1)}, bf16[1024,1280]{1,0:T(8,128)(2,1)}, u32[]{:S(2)}, u32[]{:S(2)}) collective-permute-start(bf16[1024,1280]{1,0:T(8,128)(2,1)} %keys_values.2.refs_3_), channel_id=1, source_target_pairs={{2,0},{4,2},{6,4},{8,6},{10,8},{12,10},{14,12},{16,14},{18,16},{20... | collective-permute-start | bytes 7864328 | tf_op jit(solution)/shard_map/ppermute | solution.py:479
  126.3 74.4 %collective-permute-start.5 = (bf16[1024,1280]{1,0:T(8,128)(2,1)}, bf16[1024,1280]{1,0:T(8,128)(2,1)}, u32[]{:S(2)}, u32[]{:S(2)}) collective-permute-start(bf16[1024,1280]{1,0:T(8,128)(2,1)} %keys_values.2.refs_3_), channel_id=1, source_target_pairs={{0,2},{2,4},{4,6},{6,8},{8,10},{10,12},{12,14},{14,16},{16,18},{18... | collective-permute-start | bytes 7864328 | tf_op jit(solution)/shard_map/ppermute | solution.py:479
  136.0 64.6 %collective-permute-start.4 = (bf16[512,1280]{1,0:T(8,128)(2,1)}, bf16[512,1280]{1,0:T(8,128)(2,1)}, u32[]{:S(2)}, u32[]{:S(2)}) collective-permute-start(bf16[512,1280]{1,0:T(8,128)(2,1)} %get-tuple-element.259), channel_id=1, source_target_pairs={{0,4},{4,8},{8,12},{12,16},{16,20},{20,24},{24,28},{1,5},{5,9},{9,... | collective-permute-start | bytes 3932168 | tf_op jit(solution)/shard_map/ppermute | solution.py:479
  157.9 101.1 %collective-permute-start.3 = (bf16[512,1280]{1,0:T(8,128)(2,1)}, bf16[512,1280]{1,0:T(8,128)(2,1)}, u32[]{:S(2)}, u32[]{:S(2)}) collective-permute-start(bf16[512,1280]{1,0:T(8,128)(2,1)} %get-tuple-element.98.refs_0_), channel_id=1, source_target_pairs={{0,1},{1,0},{2,3},{3,2},{4,5},{5,4},{6,7},{7,6},{8,9},{9,8},{10,11... | collective-permute-start | bytes 3932168 | tf_op jit(solution)/shard_map/ppermute | solution.py:547
  161.9 97.1 %collective-permute-start.9 = (bf16[512,1280]{1,0:T(8,128)(2,1)}, bf16[512,1280]{1,0:T(8,128)(2,1)}, u32[]{:S(2)}, u32[]{:S(2)}) collective-permute-start(bf16[512,1280]{1,0:T(8,128)(2,1)} %constant_dynamic-slice_fusion.6), channel_id=1, source_target_pairs={{2,0},{6,4},{10,8},{14,12},{18,16},{22,20},{26,24},{30,28},{3,1},{... | collective-permute-start | bytes 3932168 | tf_op jit(solution)/shard_map/ppermute | solution.py:479
  200.7 123.9 %collective-permute-start.15 = (bf16[1024,1280]{1,0:T(8,128)(2,1)S(1)}, bf16[1024,1280]{1,0:T(8,128)(2,1)}, u32[]{:S(2)}, u32[]{:S(2)}) collective-permute-start(bf16[1024,1280]{1,0:T(8,128)(2,1)S(1)} %copy-done.8), channel_id=1, source_target_pairs={{2,0},{4,2},{6,4},{8,6},{10,8},{12,10},{14,12},{16,14},{18,16},{20... | collective-permute-start | bytes 7864328 | tf_op jit(solution)/shard_map/ppermute | solution.py:479
  204.4 54.6 %collective-permute-start.6 = (bf16[512,1280]{1,0:T(8,128)(2,1)}, bf16[512,1280]{1,0:T(8,128)(2,1)}, u32[]{:S(2)}, u32[]{:S(2)}) collective-permute-start(bf16[512,1280]{1,0:T(8,128)(2,1)} %constant_dynamic-slice_fusion.8), channel_id=1, source_target_pairs={{0,2},{4,6},{8,10},{12,14},{16,18},{20,22},{24,26},{28,30},{1,3},{... | collective-permute-start | bytes 3932168 | tf_op jit(solution)/shard_map/ppermute | solution.py:479
  250.2 77.1 %collective-permute-start.13 = (bf16[1024,1280]{1,0:T(8,128)(2,1)S(1)}, bf16[1024,1280]{1,0:T(8,128)(2,1)}, u32[]{:S(2)}, u32[]{:S(2)}) collective-permute-start(bf16[1024,1280]{1,0:T(8,128)(2,1)S(1)} %copy-done.8), channel_id=1, source_target_pairs={{0,2},{2,4},{4,6},{6,8},{8,10},{10,12},{12,14},{14,16},{16,18},{18... | collective-permute-start | bytes 7864328 | tf_op jit(solution)/shard_map/ppermute | solution.py:479
  303.6 29.4 %collective-permute-start.10 = (bf16[512,1280]{1,0:T(8,128)(2,1)}, bf16[512,1280]{1,0:T(8,128)(2,1)}, u32[]{:S(2)}, u32[]{:S(2)}) collective-permute-start(bf16[512,1280]{1,0:T(8,128)(2,1)} %get-tuple-element.103), channel_id=1, source_target_pairs={{0,1},{1,0},{2,3},{3,2},{4,5},{5,4},{6,7},{7,6},{8,9},{9,8},{10,11... | collective-permute-start | bytes 3932168 | tf_op jit(solution)/shard_map/ppermute | solution.py:547
  311.1 29.2 %collective-permute-start.12 = (bf16[512,1280]{1,0:T(8,128)(2,1)S(1)}, bf16[512,1280]{1,0:T(8,128)(2,1)}, u32[]{:S(2)}, u32[]{:S(2)}) collective-permute-start(bf16[512,1280]{1,0:T(8,128)(2,1)S(1)} %get-tuple-element.257), channel_id=1, source_target_pairs={{0,4},{4,8},{8,12},{12,16},{16,20},{20,24},{24,28},{1,5},{5,9},{9,... | collective-permute-start | bytes 3932168 | tf_op jit(solution)/shard_map/ppermute | solution.py:479
  335.9 51.1 %collective-permute-start.11 = (bf16[512,1280]{1,0:T(8,128)(2,1)S(1)}, bf16[512,1280]{1,0:T(8,128)(2,1)}, u32[]{:S(2)}, u32[]{:S(2)}) collective-permute-start(bf16[512,1280]{1,0:T(8,128)(2,1)S(1)} %add_convert_fusion.3.refs_0_), channel_id=1, source_target_pairs={{0,1},{1,0},{2,3},{3,2},{4,5},{5,4},{6,7},{7,6},{8,9},{9,8},{10,11... | collective-permute-start | bytes 3932168 | tf_op jit(solution)/shard_map/ppermute | solution.py:547
  385.9 40.5 %collective-permute-start.18 = (bf16[512,1280]{1,0:T(8,128)(2,1)}, bf16[512,1280]{1,0:T(8,128)(2,1)}, u32[]{:S(2)}, u32[]{:S(2)}) collective-permute-start(bf16[512,1280]{1,0:T(8,128)(2,1)} %get-tuple-element.111), channel_id=1, source_target_pairs={{0,1},{1,0},{2,3},{3,2},{4,5},{5,4},{6,7},{7,6},{8,9},{9,8},{10,11... | collective-permute-start | bytes 3932168 | tf_op jit(solution)/shard_map/ppermute | solution.py:547
  424.9 31.9 %collective-permute-start.19 = (bf16[512,1280]{1,0:T(8,128)(2,1)}, bf16[512,1280]{1,0:T(8,128)(2,1)S(1)}, u32[]{:S(2)}, u32[]{:S(2)}) collective-permute-start(bf16[512,1280]{1,0:T(8,128)(2,1)} %get-tuple-element.122), channel_id=1, source_target_pairs={{0,1},{1,0},{2,3},{3,2},{4,5},{5,4},{6,7},{7,6},{8,9},{9,8},{10,11... | collective-permute-start | bytes 3932168 | tf_op jit(solution)/shard_map/ppermute | solution.py:547
  431.1 47.5 %collective-permute-start.21 = (bf16[512,1280]{1,0:T(8,128)(2,1)}, bf16[512,1280]{1,0:T(8,128)(2,1)}, u32[]{:S(2)}, u32[]{:S(2)}) collective-permute-start(bf16[512,1280]{1,0:T(8,128)(2,1)} %add_convert_fusion.2.refs_0_), channel_id=1, source_target_pairs={{0,1},{1,0},{2,3},{3,2},{4,5},{5,4},{6,7},{7,6},{8,9},{9,8},{10,11... | collective-permute-start | bytes 3932168 | tf_op jit(solution)/shard_map/ppermute | solution.py:547
  463.4 54.6 %collective-permute-start.20 = (bf16[512,1280]{1,0:T(8,128)(2,1)S(1)}, bf16[512,1280]{1,0:T(8,128)(2,1)S(1)}, u32[]{:S(2)}, u32[]{:S(2)}) collective-permute-start(bf16[512,1280]{1,0:T(8,128)(2,1)S(1)} %convert_element_type.179.refs_0_.refs_4_), channel_id=1, source_target_pairs={{0,1},{1,0},{2,3},{3,2},{4,5},{5,4},{6,7},{7,6},{8,9},{9,8},{10,11... | collective-permute-start | bytes 3932168 | tf_op jit(solution)/shard_map/ppermute | solution.py:547
  559.5 454.1 %reduce-scatter.5.cloned.1.call-start = ((), (), s32[]{:S(2)}) async-start(), calls=%async_computation.4 | async-start | bytes 6963200 | tf_op jit(solution)/shard_map/reduce_scatter | solution.py:747
  559.5 94.6 %collective-permute-start.24 = (bf16[512,1280]{1,0:T(8,128)(2,1)S(1)}, bf16[512,1280]{1,0:T(8,128)(2,1)S(1)}, u32[]{:S(2)}, u32[]{:S(2)}) collective-permute-start(bf16[512,1280]{1,0:T(8,128)(2,1)S(1)} %convert_element_type.182.refs_0_.refs_6_), channel_id=1, source_target_pairs={{0,1},{1,0},{2,3},{3,2},{4,5},{5,4},{6,7},{7,6},{8,9},{9,8},{10,11... | collective-permute-start | bytes 3932168 | tf_op jit(solution)/shard_map/ppermute | solution.py:547
  621.3 108.5 %collective-permute-start.23 = (bf16[512,1280]{1,0:T(8,128)(2,1)}, bf16[512,1280]{1,0:T(8,128)(2,1)}, u32[]{:S(2)}, u32[]{:S(2)}) collective-permute-start(bf16[512,1280]{1,0:T(8,128)(2,1)} %get-tuple-element.139), channel_id=1, source_target_pairs={{0,1},{1,0},{2,3},{3,2},{4,5},{5,4},{6,7},{7,6},{8,9},{9,8},{10,11... | collective-permute-start | bytes 3932168 | tf_op jit(solution)/shard_map/ppermute | solution.py:547
  621.4 110.1 %collective-permute-start.28 = (bf16[512,1280]{1,0:T(8,128)(2,1)}, bf16[512,1280]{1,0:T(8,128)(2,1)}, u32[]{:S(2)}, u32[]{:S(2)}) collective-permute-start(bf16[512,1280]{1,0:T(8,128)(2,1)} %get-tuple-element.151), channel_id=1, source_target_pairs={{4,0},{6,2},{8,4},{10,6},{12,8},{14,10},{16,12},{18,14},{20,16},{2... | collective-permute-start | bytes 3932168 | tf_op jit(solution)/shard_map/ppermute | solution.py:479
  622.7 126.2 %collective-permute-start.29 = (bf16[512,1280]{1,0:T(8,128)(2,1)}, bf16[512,1280]{1,0:T(8,128)(2,1)}, u32[]{:S(2)}, u32[]{:S(2)}) collective-permute-start(bf16[512,1280]{1,0:T(8,128)(2,1)} %get-tuple-element.152), channel_id=1, source_target_pairs={{0,4},{2,6},{4,8},{6,10},{8,12},{10,14},{12,16},{14,18},{16,20},{1... | collective-permute-start | bytes 3932168 | tf_op jit(solution)/shard_map/ppermute | solution.py:479
  652.9 178.1 %collective-permute-start.26 = (bf16[1024,1280]{1,0:T(8,128)(2,1)}, bf16[1024,1280]{1,0:T(8,128)(2,1)}, u32[]{:S(2)}, u32[]{:S(2)}) collective-permute-start(bf16[1024,1280]{1,0:T(8,128)(2,1)} %get-tuple-element.149), channel_id=1, source_target_pairs={{2,0},{4,2},{6,4},{8,6},{10,8},{12,10},{14,12},{16,14},{18,16},{20... | collective-permute-start | bytes 7864328 | tf_op jit(solution)/shard_map/ppermute | solution.py:479
  654.2 176.7 %collective-permute-start.27 = (bf16[1024,1280]{1,0:T(8,128)(2,1)}, bf16[1024,1280]{1,0:T(8,128)(2,1)}, u32[]{:S(2)}, u32[]{:S(2)}) collective-permute-start(bf16[1024,1280]{1,0:T(8,128)(2,1)} %get-tuple-element.150), channel_id=1, source_target_pairs={{0,2},{2,4},{4,6},{6,8},{8,10},{10,12},{12,14},{14,16},{16,18},{18... | collective-permute-start | bytes 7864328 | tf_op jit(solution)/shard_map/ppermute | solution.py:479
  731.5 82.2 %collective-permute-start.33 = (bf16[512,1280]{1,0:T(8,128)(2,1)S(1)}, bf16[512,1280]{1,0:T(8,128)(2,1)}, u32[]{:S(2)}, u32[]{:S(2)}) collective-permute-start(bf16[512,1280]{1,0:T(8,128)(2,1)S(1)} %copy-done.58), channel_id=1, source_target_pairs={{0,4},{2,6},{4,8},{6,10},{8,12},{10,14},{12,16},{14,18},{16,20},{1... | collective-permute-start | bytes 3932168 | tf_op jit(solution)/shard_map/ppermute | solution.py:479
  748.8 82.1 %collective-permute-start.32 = (bf16[512,1280]{1,0:T(8,128)(2,1)}, bf16[512,1280]{1,0:T(8,128)(2,1)}, u32[]{:S(2)}, u32[]{:S(2)}) collective-permute-start(bf16[512,1280]{1,0:T(8,128)(2,1)} %get-tuple-element.159), channel_id=1, source_target_pairs={{4,0},{6,2},{8,4},{10,6},{12,8},{14,10},{16,12},{18,14},{20,16},{2... | collective-permute-start | bytes 3932168 | tf_op jit(solution)/shard_map/ppermute | solution.py:479
  753.9 80.5 %collective-permute-start.31 = (bf16[1024,1280]{1,0:T(8,128)(2,1)}, bf16[1024,1280]{1,0:T(8,128)(2,1)S(1)}, u32[]{:S(2)}, u32[]{:S(2)}) collective-permute-start(bf16[1024,1280]{1,0:T(8,128)(2,1)} %get-tuple-element.157), channel_id=1, source_target_pairs={{0,2},{2,4},{4,6},{6,8},{8,10},{10,12},{12,14},{14,16},{16,18},{18... | collective-permute-start | bytes 7864328 | tf_op jit(solution)/shard_map/ppermute | solution.py:479
  813.7 32.3 %collective-permute-start.30 = (bf16[1024,1280]{1,0:T(8,128)(2,1)}, bf16[1024,1280]{1,0:T(8,128)(2,1)}, u32[]{:S(2)}, u32[]{:S(2)}) collective-permute-start(bf16[1024,1280]{1,0:T(8,128)(2,1)} %get-tuple-element.155), channel_id=1, source_target_pairs={{2,0},{4,2},{6,4},{8,6},{10,8},{12,10},{14,12},{16,14},{18,16},{20... | collective-permute-start | bytes 7864328 | tf_op jit(solution)/shard_map/ppermute | solution.py:479
  920.2 54.3 %collective-permute-start.36 = (f32[11520]{0:T(1024)S(1)}, f32[11520]{0:T(1024)S(1)}, u32[]{:S(2)}, u32[]{:S(2)}) collective-permute-start(f32[11520]{0:T(1024)S(1)} %pad_maximum_fusion.3), channel_id=1, source_target_pairs={{0,2},{2,0},{4,6},{6,4},{8,10},{10,8},{12,14},{14,12},{16,18},{18,... | collective-permute-start | bytes 138248 | tf_op jit(solution)/shard_map/ppermute | solution.py:527
  (71 other events, 1068.4 us)
Sparse Core Ops, SparseCore 0:
  11.8 105.3 all-gather.1
  559.6 256.9 reduce-scatter.2
  876.6 136.8 reduce-scatter.4

commit v3 on v2

--- a/solution.py
+++ b/solution.py
@@ -41,7 +41,21 @@
     return jnp.where(in_head(1, width, offset), 1.0, 0.0).astype(BF)
 
 
-def window_parts(refs, swap, FR):
+def window_parts(refs, place, FR):
+    swap, core = place[0], place[1]
+    half = FR // 2
+    left, right, last = EDGE, EDGE + 2 * FR, EDGE + 3 * FR
+    inside, across = right + core * (left - right), left + core * (right - left)
+    parts = []
+    for ref, base in zip(refs[:3], (inside, across, EDGE + FR)):
+        parts.append((ref, 0, base + swap * half, half))
+        parts.append((ref, half, base + (1 - swap) * half, half))
+    parts.append((refs[3], 0, core * last, EDGE))
+    parts.append((refs[4], 0, (1 - core) * last, EDGE))
+    return parts
+
+
+def piece_parts(refs, swap, FR):
     half = FR // 2
     both = (swap * half, (1 - swap) * half)
     bases = [[base + add for add in both] for base in (EDGE, EDGE + FR, EDGE + 2 * FR)]
@@ -57,7 +71,7 @@
     swap, core = place[0], place[1]
     left_direct, left_relayed, *near, right_direct, right_relayed = refs
     copies = []
-    for number, (ref, row, at, rows) in enumerate(window_parts([left_direct, *near, right_direct], swap, FR)):
+    for number, (ref, row, at, rows) in enumerate(piece_parts([left_direct, *near, right_direct], swap, FR)):
         to = window.at[pl.ds(pl.multiple_of(at, EDGE), rows)]
         copies.append(pltpu.make_async_copy(ref.at[pl.ds(row, rows)], to, sems.at[number]))
         if ref is left_direct or ref is right_direct:
@@ -123,7 +137,7 @@
 ANY = pl.BlockSpec(memory_space=pl.ANY)
 
 
-def attend_forward(q, pieces, ranges, swap, heads, QB=256, KB=768):
+def attend_forward(q, pieces, ranges, swap, heads, QB=256, KB=1536):
     st, en = ranges
     FR, W = q.shape
     rows = 3 * FR + 2 * EDGE
@@ -155,7 +169,6 @@
     *refs, window, grads, dq_s, sems = refs
     number = len(refs) - 6
     pieces, dq_ref, outs = refs[:number], refs[number], refs[number + 1 :]
-    swap = swap_ref[0]
     fetch_window(pieces, swap_ref, q_ref.shape[0], window, sems)
     spans = head_spans(heads)
     grads[...] = jnp.zeros(grads.shape, F32)
@@ -196,7 +209,7 @@
         return carry
 
     lax.fori_loop(0, q_ref.shape[0] // QB, query_block, 0)
-    for ref, row, at, rows in window_parts(outs, swap, q_ref.shape[0]):
+    for ref, row, at, rows in window_parts(outs, swap_ref, q_ref.shape[0]):
 
         def store(j, carry, ref=ref, row=row, at=at):
             to = pl.multiple_of(row + j * 128, 128)
@@ -213,7 +226,7 @@
     FR, W = q.shape
     rows = 3 * FR + 2 * EDGE
     lo, count = key_chunks(st, en, QB, KB, rows)
-    grads = [(piece, 2 * W) for piece in (EDGE, FR, FR, FR, EDGE)]
+    grads = [(piece, 2 * W) for piece in (FR, FR, FR, EDGE, EDGE)]
     return pl.pallas_call(
         functools.partial(backward_kernel, heads, W, QB, KB),
         out_shape=(jax.ShapeDtypeStruct((FR, W), BF),)
@@ -271,7 +284,7 @@
         in_specs=[once(x.shape) for x in xs] + [weight_spec] + [spec for _, spec in extras],
         out_specs=tuple(spec for _, _, spec in outs),
         out_shape=tuple(jax.ShapeDtypeStruct(shape, kind) for shape, kind, _ in outs),
-        compiler_params=pltpu.CompilerParams(vmem_limit_bytes=56 << 20),
+        compiler_params=pltpu.CompilerParams(vmem_limit_bytes=26 << 20),
         cost_estimate=FREE,
         name=name,
     )(*xs, weight, *[x for x, _ in extras])
@@ -381,13 +394,13 @@
         in_specs=[once(x.shape) for x in xs] + [w_spec],
         out_specs=tuple(pl.BlockSpec((r, width), lambda i: (0, i)) for r, _ in kinds),
         out_shape=tuple(jax.ShapeDtypeStruct((r, n), kind) for r, kind in kinds),
-        compiler_params=pltpu.CompilerParams(vmem_limit_bytes=56 << 20),
+        compiler_params=pltpu.CompilerParams(vmem_limit_bytes=26 << 20),
         cost_estimate=FREE,
         name=name,
     )(*xs, weight)
 
 
-def weight_terms(parts, n, kind, start=None, place=None, name="weight_terms"):
+def weight_terms(parts, n, kind, start=None, place=None, room=26):
     depth = parts[0][1][0][0].shape[1]
     height = width_of(depth, 256)
     xs, ys = [], []
@@ -467,10 +480,20 @@
         out_specs=spec,
         out_shape=jax.ShapeDtypeStruct(shape, kind),
         input_output_aliases=aliases,
-        compiler_params=pltpu.CompilerParams(vmem_limit_bytes=60 << 20),
+        compiler_params=pltpu.CompilerParams(vmem_limit_bytes=room << 20),
         cost_estimate=FREE,
-        name=name,
+        name="weight_terms",
     )(*xs, *ys, *more)
+
+
+def across(x):
+    length = lax.axis_size("dp")
+    pairs = [(i, i - 1 + 2 * (i % 2)) for i in range(length)]
+    return lax.ppermute(x, "dp", [(i, j) for i, j in pairs if 0 <= j < length])
+
+
+def inside(x):
+    return lax.ppermute(x, "dp", [(i, i ^ 1) for i in range(lax.axis_size("dp"))])
 
 
 def over_dp(x, by, start=0, step=1):
@@ -501,23 +524,58 @@
     )
 
 
-def to_half(whole, part, second):
-    half = whole.shape[0] // 2
-    zero = jnp.zeros((), F32)
-    part = part.astype(F32)
-    wide = jnp.concatenate((jnp.where(second == 0, part, zero), jnp.where(second == 1, part, zero)))
-    return whole.astype(F32) + wide
-
-
-def return_rows(grads):
-    g_l2, g_l1, own, g_r1, g_r2 = grads
-    return own, over_dp(g_l1, -1), over_dp(g_r1, 1), over_dp(g_l2, -2), over_dp(g_r2, 2)
-
-
-def add_returned(parts, swap):
-    own, from_right, from_left, for_tail, for_head = parts
-    total = own.astype(F32) + from_right.astype(F32) + from_left.astype(F32)
-    return to_half(to_half(total, for_tail, 1 - swap), for_head, swap).astype(BF)
+BLOCK = 256
+
+
+def add_far(near, far, second):
+    rows, width = far.shape
+    steps = rows // BLOCK
+
+    def kernel(second_ref, near_ref, far_ref, out_ref):
+        out_ref[...] = (near_ref[...].astype(F32) + far_ref[...].astype(F32)).astype(BF)
+
+    here = pl.BlockSpec((BLOCK, width), lambda i, s: (s[0] * steps + i, 0))
+    return pl.pallas_call(
+        kernel,
+        grid_spec=pltpu.PrefetchScalarGridSpec(
+            num_scalar_prefetch=1,
+            grid=(steps,),
+            in_specs=[here, pl.BlockSpec((BLOCK, width), lambda i, s: (i, 0))],
+            out_specs=here,
+        ),
+        out_shape=jax.ShapeDtypeStruct(near.shape, BF),
+        input_output_aliases={1: 0},
+        cost_estimate=FREE,
+        name="add_far",
+    )(second[None], near, far)
+
+
+def return_rows(grads, place):
+    swap, core = place[0], place[1]
+    near_inside, near_across, own, far_across, far_inside = grads
+    head, tail = swap, 1 - swap
+    near_across = add_far(near_across, inside(far_inside), jnp.where(core == 0, tail, head))
+    from_across = across(near_across)
+    near_inside = add_far(near_inside, across(far_across), jnp.where(core == 0, head, tail))
+    return (own, from_across, inside(near_inside)), near_across
+
+
+def add_returned(parts):
+    rows, width = parts[0].shape
+
+    def kernel(*refs):
+        refs[-1][...] = sum(ref[...].astype(F32) for ref in refs[:-1]).astype(BF)
+
+    block = pl.BlockSpec((BLOCK, width), lambda i: (i, 0))
+    return pl.pallas_call(
+        kernel,
+        grid=(rows // BLOCK,),
+        in_specs=[block] * len(parts),
+        out_specs=block,
+        out_shape=jax.ShapeDtypeStruct((rows, width), BF),
+        cost_estimate=FREE,
+        name="add_returned",
+    )(*parts)
 
 
 def sum_everywhere(x, axis):
@@ -600,13 +658,7 @@
     attention = jnp.concatenate(
         (widened(w_qkv).reshape(w_qkv.shape[0], 3 * W), widened(w_out)), axis=1
     )
-    if attention.shape == w_fc1.shape:
-        every = lax.all_gather(jnp.stack((attention, w_fc1, w_fc2)), "dp", axis=1, tiled=True)
-        att, fc1, fc2 = (every, 0), (every, 1), (every, 2)
-    else:
-        att = lax.all_gather(attention[None], "dp", axis=1, tiled=True), 0
-        every = lax.all_gather(jnp.stack((w_fc1, w_fc2)), "dp", axis=1, tiled=True)
-        fc1, fc2 = (every, 0), (every, 1)
+    att = lax.all_gather(attention[None], "dp", axis=1, tiled=True), 0
     bias_q = widened(bias_qv[0].astype(F32))
     bias_kv = jnp.concatenate((jnp.zeros((W,), F32), widened(bias_qv[1].astype(F32))))
     chosen = (jnp.arange(W)[:, None] // HD == jnp.arange(heads)[None, :]).astype(F32)
@@ -646,8 +698,8 @@
         *rest, x = xs
         return [*rest, order.after(x, *wait)]
 
-    def keys_values(m):
-        m.kv = order.done(project_rows(gated(m.h1), att, W, 2 * W, bias_kv, 1.0, "keys_values"))
+    def keys_values(m, *wait):
+        m.kv = order.done(project_rows(gated(m.h1, *wait), att, W, 2 * W, bias_kv, 1.0, "keys_values"))
 
     def queries(m):
         m.q = order.done(project_rows(gated(m.h1), att, 0, W, bias_q, LOG2E * SCALE, "queries"))
@@ -679,8 +731,8 @@
         m.grad_h2, m.grad_h2_far = share(parts)
         order.done(parts[0])
 
-    def narrow(m):
-        m.fed_parts = back_rows(gated([m.active]), fc2, [0], "narrow")
+    def narrow(m, *wait):
+        m.fed_parts = back_rows(gated([m.active], *wait), fc2, [0], "narrow")
         order.done(m.fed_parts[0])
 
     def send_narrow(m):
@@ -696,7 +748,7 @@
 
     no_bias = jnp.zeros((W,), F32)
 
-    def attend_back(m):
+    def attend_back(m, *wait):
         m.grad_mixed = project_rows(
             gated(m.grad_a), att, 3 * W, W, no_bias, 1.0, "grad_mixed"
         )
@@ -707,13 +759,13 @@
             precision=lax.Precision.HIGHEST,
         )
         m.grad_q, *grads = attend_backward(
-            m.q, m.grad_mixed, m.pieces, m.ranges, m.lse, delta, place, heads
+            lax.optimization_barrier((m.q, *wait))[0], m.grad_mixed, m.pieces, m.ranges, m.lse, delta, place, heads
         )
         order.done(m.grad_q)
-        m.returned = return_rows(grads)
+        m.returned, m.ready = return_rows(grads, place)
 
     def add_up(m, *wait):
-        m.grad_kv = order.done(add_returned([order.after(x, *wait) for x in m.returned], swap))
+        m.grad_kv = order.done(add_returned([order.after(x, *wait) for x in m.returned]))
 
     def grad_projected(m):
         grad_kv = order.after(m.grad_kv)
@@ -747,12 +799,15 @@
         return lax.psum_scatter(terms.astype(BF), "dp", scatter_dimension=axis, tiled=True).astype(F32)
 
     m0.b, m1.b = 0, 1
-    keys_values(m0)
+    keys_values(m0, m1.h1[-1])
     keys_values(m1)
     queries(m0)
     queries(m1)
     m0.pieces = near_rows(m0.kv, swap)
     first_arrived = [m0.pieces[k] for k in (0, 2, 4, 5)]
+    w_fc = lax.optimization_barrier((jnp.stack((w_fc1, w_fc2)), *first_arrived))[0]
+    fc_all = lax.all_gather(w_fc, "dp", axis=1, tiled=True)
+    fc1, fc2 = (fc_all, 0), (fc_all, 1)
     m1.pieces = near_rows(lax.optimization_barrier((m1.kv, m1.q, *first_arrived))[0], swap)
     for m in batches:
         m.grad_f = collect(lax.optimization_barrier((cotangent[m.b], m1.h1[-1]))[0])
@@ -781,27 +836,27 @@
     grad_second_norm(m1)
     fc_terms = term(m1.h2, m1.grad_u, kind=BF, start=fc1_term, place=(0, fc_terms))
     own_fc1, own_fc2 = owned(fc_terms, 1)
-    attend_back(m0)
+    attend_back(m0, m1.grad_a[-1])
     send_narrow(m0)
-    attend_back(m1)
-    narrow(m1)
+    attend_back(m1, m0.ready)
+    narrow(m1, m0.fed_far)
     send_narrow(m1)
     terms = weight_terms(
         [
-            (0, rows_of(gated(m0.h1), m0.grad_q) + rows_of(m1.h1, m1.grad_q)),
+            (0, rows_of(gated(m0.h1, m1.ready), m0.grad_q) + rows_of(m1.h1, m1.grad_q)),
             (3 * W, rows_of(m0.grad_a, m0.mixed) + rows_of(m1.grad_a, m1.mixed)),
         ],
         4 * W,
         F32,
     )
     order.done(terms)
-    add_up(m1, m0.fed_far, m1.fed_far, *m0.returned)
     add_up(m0)
-    kv_pairs = rows_of(m0.h1, m0.grad_kv) + rows_of(m1.h1, m1.grad_kv)
+    grad_projected(m0)
+    add_up(m1, m1.fed_far)
+    kv_pairs = rows_of(m0.h1, m0.grad_kv) + rows_of(gated(m1.h1), m1.grad_kv)
     terms = order.done(weight_terms([(W, kv_pairs)], 4 * W, BF, start=terms))
+    grad_projected(m1)
     own_attention = owned(lax.optimization_barrier((terms, own_fc1))[0], 0)
-    grad_projected(m0)
-    grad_projected(m1)
     finish(m0)
     outputs = [
         (m.middle + m.fed.astype(F32) + order.after(m.fed_far).astype(F32) + vectors[5]).astype(BF)

time: 1030 us -> 1000 us (0.971)
  local copies, waits for them, and re-layouts: 32 us -> 121 us
  Pallas kernels: 436 us -> 377 us
  waiting for transfers between devices: 233 us -> 186 us
    unnamed x118 -> x234, local copies, waits for them, and re-layouts: 5.78 us -> 97 us
    ppermute x20 -> x12, starting transfers between devices: 149 us -> 71.9 us  [over_dp(): return lax.ppermute(x, 'dp', pairs)]
    ppermute x0 -> x8, starting transfers between devices: none -> 53.6 us  [the longest x4 46.8 us: inside(): lax.ppermute(x, 'dp', [(i, i ^ 1) for i in range(lax.axis_size('dp'))])]
    all_gather x1 -> x2, waiting for transfers between devices: 40.2 us -> 0.17 us  [the longest x1 0.15 us: per_device(): att = (lax.all_gather(attention[None], 'dp', axis=1, tiled=True), 0)]
    ppermute x20 -> x12, waiting for transfers between devices: 104 us -> 71.6 us  [over_dp(): return lax.ppermute(x, 'dp', pairs)]
    pallas_call x8, Pallas kernels: 81.7 us -> 55.1 us  [back_rows(): pl.pallas_call(kernel, grid=(n // width,), in_specs=[once(x.shape) for x...]
    pallas_call x6, Pallas kernels: 89.1 us -> 66.1 us  [weight_terms(): pl.pallas_call(kernel, grid=(depth // height,), in_specs=x_spec + [once(y...]
    pallas_call x10, Pallas kernels: 90.5 us -> 67.5 us  [dense(): pl.pallas_call(kernel, grid=(n // width,), in_specs=[once(x.shape) for x...]
  transfers between devices with their start and end apart: 44 -> 45, of which waited for: 17 -> 14; matrix products, arithmetic and copies ran while one was open for 9% -> 8% of each run, Pallas kernels for 41% -> 36%
where the time goes in v3:
time: 1000 us; the launch traced here: 993 us
  Pallas kernels  377 us (38%)
  starting transfers between devices  225 us (22%)
  waiting for transfers between devices  186 us (19%)
  local copies, waits for them, and re-layouts  121 us (12%)
  other arithmetic  63.5 us (6%)
  between operations  15.7 us (2%)
    pallas_call x2, Pallas kernels, attend_backward(): pl.pallas_call(functools.partial(backward_kernel, heads, W, QB, KB), out_...  101 us
    unnamed x234, local copies, waits for them, and re-layouts  97 us
    ppermute x16, waiting for transfers between devices, partner(): return lax.ppermute(x, 'tensor', [(0, 1), (1, 0)])  82 us
    ppermute x5, starting transfers between devices, sum_everywhere(): x = x + lax.ppermute(x, axis, [(i, i ^ bit) for i in range(length)])  81.4 us
    ppermute x12, starting transfers between devices, over_dp(): return lax.ppermute(x, 'dp', pairs)  71.9 us
    ppermute x12, waiting for transfers between devices, over_dp(): return lax.ppermute(x, 'dp', pairs)  71.6 us
    pallas_call x10, Pallas kernels, dense(): pl.pallas_call(kernel, grid=(n // width,), in_specs=[once(x.shape) for x...  67.5 us
    pallas_call x6, Pallas kernels, weight_terms(): pl.pallas_call(kernel, grid=(depth // height,), in_specs=x_spec + [once(y...  66.1 us
  transfers between devices with their start and end apart: 45, of which 14 were waited for; matrix products, arithmetic and copies ran while one was open for 8% of the time, Pallas kernels for 36%

profile of v3, /device:TPU:0, one launch (start us, length us, event | category | flops | bytes accessed | tf_op | source)
XLA Modules:
  0.0 992.9 jit_solution(18201263319702046350)
XLA Ops:
  21.0 27.4 %collective-permute-done.refs_1_ = bf16[512,1280]{1,0:T(8,128)(2,1)S(1)} collective-permute-done((bf16[512,1280]{1,0:T(8,128)(2,1)S(1)}, bf16[512,1280]{1,0:T(8,128)(2,1)S(1)}, u32[]{:S(2)}, u32[]{:S(2)}) %collective-permute-start) | collective-permute-done | bytes 1310752 | tf_op jit(solution)/shard_map/ppermute | solution.py:605
  49.6 26.2 %collective-permute-done.1.refs_1_.refs_3_ = bf16[512,1280]{1,0:T(8,128)(2,1)S(1)} collective-permute-done((bf16[512,1280]{1,0:T(8,128)(2,1)S(1)}, bf16[512,1280]{1,0:T(8,128)(2,1)S(1)}, u32[]{:S(2)}, u32[]{:S(2)}) %collective-permute-start.1) | collective-permute-done | bytes 1310752 | tf_op jit(solution)/shard_map/ppermute | solution.py:605
  100.8 61.3 %collective-permute-done.4.refs_0_ = bf16[512,1280]{1,0:T(8,128)(2,1)} collective-permute-done((bf16[512,1280]{1,0:T(8,128)(2,1)}, bf16[512,1280]{1,0:T(8,128)(2,1)}, u32[]{:S(2)}, u32[]{:S(2)}) %collective-permute-start.4) | collective-permute-done | bytes 1310752 | tf_op jit(solution)/shard_map/ppermute | solution.py:502
  182.8 17.4 %collective-permute-start.13 = (bf16[1024,1280]{1,0:T(8,128)(2,1)}, bf16[1024,1280]{1,0:T(8,128)(2,1)}, u32[]{:S(2)}, u32[]{:S(2)}) collective-permute-start(bf16[1024,1280]{1,0:T(8,128)(2,1)} %keys_values.3.refs_3_), channel_id=1, source_target_pairs={{0,2},{2,4},{4,6},{6,8},{8,10},{10,12},{12,14},{14,16},{16,18},{18... | collective-permute-start | bytes 7864328 | tf_op jit(solution)/shard_map/ppermute | solution.py:502
  223.4 32.5 %attend_forward.2 = (bf16[1024,640]{1,0:T(8,128)(2,1)}, f32[8,1024]{1,0:T(8,128)}) custom-call(s32[4]{0:T(128)} %get-tuple-element.256.lo_ref, s32[4]{0:T(128)} %get-tuple-element.257.count_ref, s32[2]{0:T(128)} %pad_add_fusion.4.place_ref.swap_ref, s32[2,1024]{1,0:T(2,128)} %pad_add_fusion.se_ref, bf16[1024,640]{1,0:T(8,128)(2,1)} %copy-done.59, ...), custom_call_target="tpu_custom_call" | custom-call | tf_op jit(solution)/shard_map/attend_forward/pallas_call | solution.py:145
  266.9 10.2 %collective-permute-start.12 = (bf16[512,1280]{1,0:T(8,128)(2,1)S(1)}, bf16[512,1280]{1,0:T(8,128)(2,1)}, u32[]{:S(2)}, u32[]{:S(2)}) collective-permute-start(bf16[512,1280]{1,0:T(8,128)(2,1)S(1)} %get-tuple-element.265), channel_id=1, source_target_pairs={{0,4},{4,8},{8,12},{12,16},{16,20},{20,24},{24,28},{1,5},{5,9},{9,... | collective-permute-start | bytes 3932168 | tf_op jit(solution)/shard_map/ppermute | solution.py:502
  281.2 20.7 %collective-permute-start.14 = (bf16[512,1280]{1,0:T(8,128)(2,1)S(1)}, bf16[512,1280]{1,0:T(8,128)(2,1)}, u32[]{:S(2)}, u32[]{:S(2)}) collective-permute-start(bf16[512,1280]{1,0:T(8,128)(2,1)S(1)} %constant_dynamic-slice_fusion.2), channel_id=1, source_target_pairs={{0,2},{4,6},{8,10},{12,14},{16,18},{20,22},{24,26},{28,30},{1,3},{... | collective-permute-start | bytes 3932168 | tf_op jit(solution)/shard_map/ppermute | solution.py:502
  306.9 10.3 %collective-permute-done.12.refs_0_ = bf16[512,1280]{1,0:T(8,128)(2,1)} collective-permute-done((bf16[512,1280]{1,0:T(8,128)(2,1)S(1)}, bf16[512,1280]{1,0:T(8,128)(2,1)}, u32[]{:S(2)}, u32[]{:S(2)}) %collective-permute-start.12) | collective-permute-done | bytes 1310752 | tf_op jit(solution)/shard_map/ppermute | solution.py:502
  317.1 32.1 %attend_forward.3 = (bf16[1024,640]{1,0:T(8,128)(2,1)}, f32[8,1024]{1,0:T(8,128)}) custom-call(s32[4]{0:T(128)} %get-tuple-element.258.lo_ref, s32[4]{0:T(128)} %get-tuple-element.259.count_ref, s32[2]{0:T(128)} %pad_add_fusion.4.place_ref.swap_ref, s32[2,1024]{1,0:T(2,128)} %pad_add_fusion.1.se_ref, bf16[1024,640]{1,0:T(8,128)(2,1)} %copy-done.58, ...), custom_call_target="tpu_custom_call" | custom-call | tf_op jit(solution)/shard_map/attend_forward/pallas_call | solution.py:145
  362.3 13.3 %widen.2 = (bf16[1024,2560]{1,0:T(8,128)(2,1)S(1)}, bf16[1024,2560]{1,0:T(8,128)(2,1)S(1)}) custom-call(bf16[512,1280]{1,0:T(8,128)(2,1)} %add_convert_fusion.3.refs_0_, bf16[512,1280]{1,0:T(8,128)(2,1)} %collective-permute-done.11.refs_1_, bf16[2,1280,2560]{2,1,0:T(8,128)(2,1)S(1)} %copy-done, f32[1,2560]{1,0:T(1,128)S(1)} %reshape.160.refs_3_), custom_call_target="tpu_custom_call" | custom-call | tf_op jit(solution)/shard_map/widen/pallas_call | solution.py:281
  378.0 10.9 %grad_hidden.2 = (bf16[1024,2560]{1,0:T(8,128)(2,1)S(1)}, f32[1,2560]{1,0:T(1,128)S(1)}) custom-call(bf16[512,1280]{1,0:T(8,128)(2,1)} %get-tuple-element.99.refs_0_, bf16[512,1280]{1,0:T(8,128)(2,1)} %collective-permute-done.2.refs_1_, bf16[2,1280,2560]{2,1,0:T(8,128)(2,1)S(1)} %copy-done.1, bf16[1024,2560]{1,0:T(8,128)(2,1)S(1)} %get-tuple-element.115.refs_3_), custom_call_target="tpu_custom_call" | custom-call | tf_op jit(solution)/shard_map/grad_hidden/pallas_call | solution.py:281
  388.9 8.7 grad_normed.2
  403.5 8.2 narrow.2
  416.7 10.2 %weight_terms.6.refs_3_ = f32[1280,2560]{1,0:T(8,128)S(1)} custom-call(bf16[512,1280]{1,0:T(8,128)(2,1)} %get-tuple-element.99.refs_0_, bf16[512,1280]{1,0:T(8,128)(2,1)} %collective-permute-done.2.refs_1_, bf16[1024,2560]{1,0:T(8,128)(2,1)S(1)} %copy-done.38), custom_call_target="tpu_custom_call" | custom-call | tf_op jit(solution)/shard_map/weight_terms/pallas_call | solution.py:476
  441.8 10.2 %weight_terms.7.refs_3_ = f32[1280,2560]{1,0:T(8,128)S(1)} custom-call(bf16[512,1280]{1,0:T(8,128)(2,1)} %add_convert_fusion.3.refs_0_, bf16[512,1280]{1,0:T(8,128)(2,1)} %collective-permute-done.11.refs_1_, bf16[1024,2560]{1,0:T(8,128)(2,1)S(1)} %get-tuple-element.118.refs_0_.refs_2_), custom_call_target="tpu_custom_call" | custom-call | tf_op jit(solution)/shard_map/weight_terms/pallas_call | solution.py:476
  457.7 13.2 %widen.3 = (bf16[1024,2560]{1,0:T(8,128)(2,1)S(1)}, bf16[1024,2560]{1,0:T(8,128)(2,1)S(1)}) custom-call(bf16[512,1280]{1,0:T(8,128)(2,1)} %add_convert_fusion.2.refs_0_, bf16[512,1280]{1,0:T(8,128)(2,1)} %collective-permute-done.21.refs_1_, bf16[2,1280,2560]{2,1,0:T(8,128)(2,1)S(1)} %copy-done.1, f32[1,2560]{1,0:T(1,128)S(1)} %reshape.160.refs_3_), custom_call_target="tpu_custom_call" | custom-call | tf_op jit(solution)/shard_map/widen/pallas_call | solution.py:281
  477.5 10.4 %grad_hidden.3 = (bf16[1024,2560]{1,0:T(8,128)(2,1)S(1)}, f32[1,2560]{1,0:T(1,128)S(1)}) custom-call(bf16[512,1280]{1,0:T(8,128)(2,1)S(1)} %copy-done.49, bf16[512,1280]{1,0:T(8,128)(2,1)} %collective-permute-done.3.refs_1_, bf16[2,1280,2560]{2,1,0:T(8,128)(2,1)S(1)} %copy-done.1, bf16[1024,2560]{1,0:T(8,128)(2,1)S(1)} %copy-done.71), custom_call_target="tpu_custom_call" | custom-call | tf_op jit(solution)/shard_map/grad_hidden/pallas_call | solution.py:281
  487.9 8.0 grad_normed.3
  496.6 12.2 %weight_terms.8.refs_4_ = bf16[2,1280,2560]{2,1,0:T(8,128)(2,1)S(1)} custom-call(bf16[512,1280]{1,0:T(8,128)(2,1)S(1)} %copy-done.49, bf16[512,1280]{1,0:T(8,128)(2,1)} %collective-permute-done.3.refs_1_, bf16[1024,2560]{1,0:T(8,128)(2,1)S(1)} %get-tuple-element.153.refs_2_.refs_0_, f32[1280,2560]{1,0:T(8,128)} %copy-done.13), custom_call_target="tpu_custom_call" | custom-call | tf_op jit(solution)/shard_map/weight_terms/pallas_call | solution.py:476
  508.9 10.1 %collective-permute-done.22 = bf16[512,1280]{1,0:T(8,128)(2,1)S(1)} collective-permute-done((bf16[512,1280]{1,0:T(8,128)(2,1)S(1)}, bf16[512,1280]{1,0:T(8,128)(2,1)S(1)}, u32[]{:S(2)}, u32[]{:S(2)}) %collective-permute-start.22) | collective-permute-done | bytes 1310752 | tf_op jit(solution)/shard_map/ppermute | solution.py:605
  523.1 11.8 %weight_terms.9 = bf16[2,1280,2560]{2,1,0:T(8,128)(2,1)S(1)} custom-call(bf16[512,1280]{1,0:T(8,128)(2,1)} %add_convert_fusion.2.refs_0_, bf16[512,1280]{1,0:T(8,128)(2,1)} %collective-permute-done.21.refs_1_, bf16[1024,2560]{1,0:T(8,128)(2,1)S(1)} %get-tuple-element.133.refs_0_.refs_2_, f32[1280,2560]{1,0:T(8,128)} %copy-done.12, ...), custom_call_target="tpu_custom_call", output_to_operand_aliasing={{}: (4, {})} | custom-call | tf_op jit(solution)/shard_map/weight_terms/pallas_call | solution.py:476
  549.6 12.1 %collective-permute-done.23.refs_1_.refs_7_ = bf16[512,1280]{1,0:T(8,128)(2,1)S(1)} collective-permute-done((bf16[512,1280]{1,0:T(8,128)(2,1)S(1)}, bf16[512,1280]{1,0:T(8,128)(2,1)S(1)}, u32[]{:S(2)}, u32[]{:S(2)}) %collective-permute-start.23) | collective-permute-done | bytes 1310752 | tf_op jit(solution)/shard_map/ppermute | solution.py:605
  562.9 51.8 %attend_backward.2 = (bf16[1024,640]{1,0:T(8,128)(2,1)}, bf16[1024,1280]{1,0:T(8,128)(2,1)}, bf16[1024,1280]{1,0:T(8,128)(2,1)}, bf16[1024,1280]{1,0:T(8,128)(2,...) custom-call(s32[4]{0:T(128)} %get-tuple-element.249.lo_ref, s32[4]{0:T(128)} %get-tuple-element.250.count_ref, ...), custom_call_target="tpu_custom_call" | custom-call | tf_op jit(solution)/shard_map/attend_backward/pallas_call | solution.py:230
  627.3 49.7 %attend_backward.3 = (bf16[1024,640]{1,0:T(8,128)(2,1)}, bf16[1024,1280]{1,0:T(8,128)(2,1)}, bf16[1024,1280]{1,0:T(8,128)(2,1)}, bf16[1024,1280]{1,0:T(8,128)(2,...) custom-call(s32[4]{0:T(128)} %get-tuple-element.246.lo_ref, s32[4]{0:T(128)} %get-tuple-element.247.count_ref, ...), custom_call_target="tpu_custom_call" | custom-call | tf_op jit(solution)/shard_map/attend_backward/pallas_call | solution.py:230
  678.7 21.5 %collective-permute-start.26 = (bf16[512,1280]{1,0:T(8,128)(2,1)}, bf16[512,1280]{1,0:T(8,128)(2,1)}, u32[]{:S(2)}, u32[]{:S(2)}) collective-permute-start(bf16[512,1280]{1,0:T(8,128)(2,1)} %get-tuple-element.151), channel_id=1, source_target_pairs={{0,2},{2,0},{4,6},{6,4},{8,10},{10,8},{12,14},{14,12},{16,18},{18,... | collective-permute-start | bytes 3932168 | tf_op jit(solution)/shard_map/ppermute | solution.py:496
  710.3 25.1 %collective-permute-start.34 = (bf16[1024,1280]{1,0:T(8,128)(2,1)}, bf16[1024,1280]{1,0:T(8,128)(2,1)}, u32[]{:S(2)}, u32[]{:S(2)}) collective-permute-start(bf16[1024,1280]{1,0:T(8,128)(2,1)} %add_far.7), channel_id=1, source_target_pairs={{0,2},{2,0},{4,6},{6,4},{8,10},{10,8},{12,14},{14,12},{16,18},{18,... | collective-permute-start | bytes 7864328 | tf_op jit(solution)/shard_map/ppermute | solution.py:496
  748.7 8.9 narrow.3
  758.2 10.1 %weight_terms.10.refs_6_ = f32[1280,2560]{1,0:T(8,128)S(1)} custom-call(bf16[512,1280]{1,0:T(8,128)(2,1)S(1)} %copy-done.18, bf16[512,1280]{1,0:T(8,128)(2,1)S(1)} %copy-done.31, bf16[512,1280]{1,0:T(8,128)(2,1)S(1)} %copy-done.21, bf16[512,1280]{1,0:T(8,128)(2,1)S(1)} %copy-done.35, bf16[512,1280]{1,0:T(8,128)(2,1)S(1)} %copy-done.46, ...), custom_call_target="tpu_custom_call" | custom-call | tf_op jit(solution)/shard_map/weight_terms/pallas_call | solution.py:476
  805.2 11.6 %weight_terms.11 = bf16[1280,2560]{1,0:T(8,128)(2,1)S(1)} custom-call(bf16[512,1280]{1,0:T(8,128)(2,1)S(1)} %copy-done.18, bf16[512,1280]{1,0:T(8,128)(2,1)S(1)} %copy-done.32, bf16[512,1280]{1,0:T(8,128)(2,1)S(1)} %copy-done.21, bf16[512,1280]{1,0:T(8,128)(2,1)S(1)} %copy-done.36, bf16[1024,1280]{1,0:T(8,128)(2,1)S(1)} %copy-done.25, ...), custom_call_target="tpu_custom_call" | custom-call | tf_op jit(solution)/shard_map/weight_terms/pallas_call | solution.py:476
  858.3 56.4 %collective-permute-start.36 = (f32[11520]{0:T(1024)S(1)}, f32[11520]{0:T(1024)S(1)}, u32[]{:S(2)}, u32[]{:S(2)}) collective-permute-start(f32[11520]{0:T(1024)S(1)} %pad_maximum_fusion.4), channel_id=1, source_target_pairs={{0,2},{2,0},{4,6},{6,4},{8,10},{10,8},{12,14},{14,12},{16,18},{18,... | collective-permute-start | bytes 138248 | tf_op jit(solution)/shard_map/ppermute | solution.py:585
  918.3 22.6 %collective-permute-start.37 = (f32[11520]{0:T(1024)S(1)}, f32[11520]{0:T(1024)S(1)}, u32[]{:S(2)}, u32[]{:S(2)}) collective-permute-start(f32[11520]{0:T(1024)S(1)} %fusion.74), channel_id=1, source_target_pairs={{0,4},{2,6},{4,0},{6,2},{8,12},{10,14},{12,8},{14,10},{16,20},{18,... | collective-permute-start | bytes 138248 | tf_op jit(solution)/shard_map/ppermute | solution.py:585
  964.9 17.5 %reduce-scatter.5.cloned.1.call-done = bf16[80,2560]{1,0:T(8,128)(2,1)} async-done(((bf16[1280,2560]{1,0:T(8,128)(2,1)}), bf16[80,2560]{1,0:T(8,128)(2,1)}) %reduce-scatter.5.cloned.1.call-update) | async-done | bytes 409616 | tf_op jit(solution)/shard_map/reduce_scatter | solution.py:799
  (448 shorter events, 324.8 us)
Async XLA Ops:
  7.2 69.8 %all-gather.6.cloned.1.call-start = ((), (), s32[]{:S(2)}) async-start(), calls=%async_computation.5 | async-start | bytes 6963200 | tf_op jit(solution)/shard_map/all_gather | solution.py:661
  10.1 347.5 %all-gather.4.cloned.1.call-start = ((), (), s32[]{:S(2)}) async-start(), calls=%async_computation.2 | async-start | bytes 13926400 | tf_op jit(solution)/shard_map/all_gather | solution.py:809
  15.8 32.6 %collective-permute-start = (bf16[512,1280]{1,0:T(8,128)(2,1)S(1)}, bf16[512,1280]{1,0:T(8,128)(2,1)S(1)}, u32[]{:S(2)}, u32[]{:S(2)}) collective-permute-start(bf16[512,1280]{1,0:T(8,128)(2,1)S(1)} %get-tuple-element.260.refs_0_), channel_id=1, source_target_pairs={{0,1},{1,0},{2,3},{3,2},{4,5},{5,4},{6,7},{7,6},{8,9},{9,8},{10,11... | collective-permute-start | bytes 3932168 | tf_op jit(solution)/shard_map/ppermute | solution.py:605
  19.9 55.8 %collective-permute-start.1 = (bf16[512,1280]{1,0:T(8,128)(2,1)S(1)}, bf16[512,1280]{1,0:T(8,128)(2,1)S(1)}, u32[]{:S(2)}, u32[]{:S(2)}) collective-permute-start(bf16[512,1280]{1,0:T(8,128)(2,1)S(1)} %get-tuple-element.261.refs_0_.refs_2_), channel_id=1, source_target_pairs={{0,1},{1,0},{2,3},{3,2},{4,5},{5,4},{6,7},{7,6},{8,9},{9,8},{10,11... | collective-permute-start | bytes 3932168 | tf_op jit(solution)/shard_map/ppermute | solution.py:605
  87.5 74.7 %collective-permute-start.7 = (bf16[1024,1280]{1,0:T(8,128)(2,1)S(1)}, bf16[1024,1280]{1,0:T(8,128)(2,1)}, u32[]{:S(2)}, u32[]{:S(2)}) collective-permute-start(bf16[1024,1280]{1,0:T(8,128)(2,1)S(1)} %keys_values.2.refs_3_), channel_id=1, source_target_pairs={{2,0},{4,2},{6,4},{8,6},{10,8},{12,10},{14,12},{16,14},{18,16},{20... | collective-permute-start | bytes 7864328 | tf_op jit(solution)/shard_map/ppermute | solution.py:502
  88.8 73.4 %collective-permute-start.5 = (bf16[1024,1280]{1,0:T(8,128)(2,1)S(1)}, bf16[1024,1280]{1,0:T(8,128)(2,1)}, u32[]{:S(2)}, u32[]{:S(2)}) collective-permute-start(bf16[1024,1280]{1,0:T(8,128)(2,1)S(1)} %keys_values.2.refs_3_), channel_id=1, source_target_pairs={{0,2},{2,4},{4,6},{6,8},{8,10},{10,12},{12,14},{14,16},{16,18},{18... | collective-permute-start | bytes 7864328 | tf_op jit(solution)/shard_map/ppermute | solution.py:502
  96.8 65.4 %collective-permute-start.4 = (bf16[512,1280]{1,0:T(8,128)(2,1)}, bf16[512,1280]{1,0:T(8,128)(2,1)}, u32[]{:S(2)}, u32[]{:S(2)}) collective-permute-start(bf16[512,1280]{1,0:T(8,128)(2,1)} %get-tuple-element.267), channel_id=1, source_target_pairs={{0,4},{4,8},{8,12},{12,16},{16,20},{20,24},{24,28},{1,5},{5,9},{9,... | collective-permute-start | bytes 3932168 | tf_op jit(solution)/shard_map/ppermute | solution.py:502
  162.2 657.2 %reduce-scatter.3.cloned.1.call-start = ((), (), s32[]{:S(2)}) async-start(), calls=%async_computation.3 | async-start | bytes 13926400 | tf_op jit(solution)/shard_map/reduce_scatter | solution.py:799
  165.8 41.0 %collective-permute-start.2 = (bf16[512,1280]{1,0:T(8,128)(2,1)}, bf16[512,1280]{1,0:T(8,128)(2,1)}, u32[]{:S(2)}, u32[]{:S(2)}) collective-permute-start(bf16[512,1280]{1,0:T(8,128)(2,1)} %get-tuple-element.99.refs_0_), channel_id=1, source_target_pairs={{0,1},{1,0},{2,3},{3,2},{4,5},{5,4},{6,7},{7,6},{8,9},{9,8},{10,11... | collective-permute-start | bytes 3932168 | tf_op jit(solution)/shard_map/ppermute | solution.py:605
  167.6 55.9 %collective-permute-start.3 = (bf16[512,1280]{1,0:T(8,128)(2,1)}, bf16[512,1280]{1,0:T(8,128)(2,1)}, u32[]{:S(2)}, u32[]{:S(2)}) collective-permute-start(bf16[512,1280]{1,0:T(8,128)(2,1)} %get-tuple-element.100.refs_0_), channel_id=1, source_target_pairs={{0,1},{1,0},{2,3},{3,2},{4,5},{5,4},{6,7},{7,6},{8,9},{9,8},{10,11... | collective-permute-start | bytes 3932168 | tf_op jit(solution)/shard_map/ppermute | solution.py:605
  181.5 95.6 %collective-permute-start.15 = (bf16[1024,1280]{1,0:T(8,128)(2,1)}, bf16[1024,1280]{1,0:T(8,128)(2,1)}, u32[]{:S(2)}, u32[]{:S(2)}) collective-permute-start(bf16[1024,1280]{1,0:T(8,128)(2,1)} %keys_values.3.refs_3_), channel_id=1, source_target_pairs={{2,0},{4,2},{6,4},{8,6},{10,8},{12,10},{14,12},{16,14},{18,16},{20... | collective-permute-start | bytes 7864328 | tf_op jit(solution)/shard_map/ppermute | solution.py:502
  182.8 97.0 %collective-permute-start.13 = (bf16[1024,1280]{1,0:T(8,128)(2,1)}, bf16[1024,1280]{1,0:T(8,128)(2,1)}, u32[]{:S(2)}, u32[]{:S(2)}) collective-permute-start(bf16[1024,1280]{1,0:T(8,128)(2,1)} %keys_values.3.refs_3_), channel_id=1, source_target_pairs={{0,2},{2,4},{4,6},{6,8},{8,10},{10,12},{12,14},{14,16},{16,18},{18... | collective-permute-start | bytes 7864328 | tf_op jit(solution)/shard_map/ppermute | solution.py:502
  260.6 41.4 %collective-permute-start.10 = (bf16[512,1280]{1,0:T(8,128)(2,1)S(1)}, bf16[512,1280]{1,0:T(8,128)(2,1)S(1)}, u32[]{:S(2)}, u32[]{:S(2)}) collective-permute-start(bf16[512,1280]{1,0:T(8,128)(2,1)S(1)} %get-tuple-element.105), channel_id=1, source_target_pairs={{0,1},{1,0},{2,3},{3,2},{4,5},{5,4},{6,7},{7,6},{8,9},{9,8},{10,11... | collective-permute-start | bytes 3932168 | tf_op jit(solution)/shard_map/ppermute | solution.py:605
  265.2 41.7 %collective-permute-start.16 = (bf16[512,1280]{1,0:T(8,128)(2,1)S(1)}, bf16[512,1280]{1,0:T(8,128)(2,1)}, u32[]{:S(2)}, u32[]{:S(2)}) collective-permute-start(bf16[512,1280]{1,0:T(8,128)(2,1)S(1)} %get-tuple-element.264), channel_id=1, source_target_pairs={{6,2},{10,6},{14,10},{18,14},{22,18},{26,22},{30,26},{7,3},{11,7},... | collective-permute-start | bytes 3932168 | tf_op jit(solution)/shard_map/ppermute | solution.py:502
  266.9 50.2 %collective-permute-start.12 = (bf16[512,1280]{1,0:T(8,128)(2,1)S(1)}, bf16[512,1280]{1,0:T(8,128)(2,1)}, u32[]{:S(2)}, u32[]{:S(2)}) collective-permute-start(bf16[512,1280]{1,0:T(8,128)(2,1)S(1)} %get-tuple-element.265), channel_id=1, source_target_pairs={{0,4},{4,8},{8,12},{12,16},{16,20},{20,24},{24,28},{1,5},{5,9},{9,... | collective-permute-start | bytes 3932168 | tf_op jit(solution)/shard_map/ppermute | solution.py:502
  278.5 38.6 %collective-permute-start.17 = (bf16[512,1280]{1,0:T(8,128)(2,1)S(1)}, bf16[512,1280]{1,0:T(8,128)(2,1)}, u32[]{:S(2)}, u32[]{:S(2)}) collective-permute-start(bf16[512,1280]{1,0:T(8,128)(2,1)S(1)} %constant_dynamic-slice_fusion), channel_id=1, source_target_pairs={{2,0},{6,4},{10,8},{14,12},{18,16},{22,20},{26,24},{30,28},{3,1},{... | collective-permute-start | bytes 3932168 | tf_op jit(solution)/shard_map/ppermute | solution.py:502
  281.2 35.9 %collective-permute-start.14 = (bf16[512,1280]{1,0:T(8,128)(2,1)S(1)}, bf16[512,1280]{1,0:T(8,128)(2,1)}, u32[]{:S(2)}, u32[]{:S(2)}) collective-permute-start(bf16[512,1280]{1,0:T(8,128)(2,1)S(1)} %constant_dynamic-slice_fusion.2), channel_id=1, source_target_pairs={{0,2},{4,6},{8,10},{12,14},{16,18},{20,22},{24,26},{28,30},{1,3},{... | collective-permute-start | bytes 3932168 | tf_op jit(solution)/shard_map/ppermute | solution.py:502
  304.6 53.0 %collective-permute-start.11 = (bf16[512,1280]{1,0:T(8,128)(2,1)}, bf16[512,1280]{1,0:T(8,128)(2,1)}, u32[]{:S(2)}, u32[]{:S(2)}) collective-permute-start(bf16[512,1280]{1,0:T(8,128)(2,1)} %add_convert_fusion.3.refs_0_), channel_id=1, source_target_pairs={{0,1},{1,0},{2,3},{3,2},{4,5},{5,4},{6,7},{7,6},{8,9},{9,8},{10,11... | collective-permute-start | bytes 3932168 | tf_op jit(solution)/shard_map/ppermute | solution.py:605
  356.1 41.5 %collective-permute-start.18 = (bf16[512,1280]{1,0:T(8,128)(2,1)}, bf16[512,1280]{1,0:T(8,128)(2,1)}, u32[]{:S(2)}, u32[]{:S(2)}) collective-permute-start(bf16[512,1280]{1,0:T(8,128)(2,1)} %get-tuple-element.114), channel_id=1, source_target_pairs={{0,1},{1,0},{2,3},{3,2},{4,5},{5,4},{6,7},{7,6},{8,9},{9,8},{10,11... | collective-permute-start | bytes 3932168 | tf_op jit(solution)/shard_map/ppermute | solution.py:605
  397.5 34.2 %collective-permute-start.19 = (bf16[512,1280]{1,0:T(8,128)(2,1)}, bf16[512,1280]{1,0:T(8,128)(2,1)}, u32[]{:S(2)}, u32[]{:S(2)}) collective-permute-start(bf16[512,1280]{1,0:T(8,128)(2,1)} %get-tuple-element.125), channel_id=1, source_target_pairs={{0,1},{1,0},{2,3},{3,2},{4,5},{5,4},{6,7},{7,6},{8,9},{9,8},{10,11... | collective-permute-start | bytes 3932168 | tf_op jit(solution)/shard_map/ppermute | solution.py:605
  402.4 55.3 %collective-permute-start.21 = (bf16[512,1280]{1,0:T(8,128)(2,1)}, bf16[512,1280]{1,0:T(8,128)(2,1)}, u32[]{:S(2)}, u32[]{:S(2)}) collective-permute-start(bf16[512,1280]{1,0:T(8,128)(2,1)} %add_convert_fusion.2.refs_0_), channel_id=1, source_target_pairs={{0,1},{1,0},{2,3},{3,2},{4,5},{5,4},{6,7},{7,6},{8,9},{9,8},{10,11... | collective-permute-start | bytes 3932168 | tf_op jit(solution)/shard_map/ppermute | solution.py:605
  440.9 55.7 %collective-permute-start.20 = (bf16[512,1280]{1,0:T(8,128)(2,1)S(1)}, bf16[512,1280]{1,0:T(8,128)(2,1)S(1)}, u32[]{:S(2)}, u32[]{:S(2)}) collective-permute-start(bf16[512,1280]{1,0:T(8,128)(2,1)S(1)} %convert_element_type.143.refs_0_.refs_4_), channel_id=1, source_target_pairs={{0,1},{1,0},{2,3},{3,2},{4,5},{5,4},{6,7},{7,6},{8,9},{9,8},{10,11... | collective-permute-start | bytes 3932168 | tf_op jit(solution)/shard_map/ppermute | solution.py:605
  539.7 442.8 %reduce-scatter.5.cloned.1.call-start = ((), (), s32[]{:S(2)}) async-start(), calls=%async_computation.4 | async-start | bytes 6963200 | tf_op jit(solution)/shard_map/reduce_scatter | solution.py:799
  621.3 78.9 %collective-permute-start.28 = (bf16[512,1280]{1,0:T(8,128)(2,1)}, bf16[512,1280]{1,0:T(8,128)(2,1)S(1)}, u32[]{:S(2)}, u32[]{:S(2)}) collective-permute-start(bf16[512,1280]{1,0:T(8,128)(2,1)} %get-tuple-element.159), channel_id=1, source_target_pairs={{2,4},{4,2},{6,8},{8,6},{10,12},{12,10},{14,16},{16,14},{18,20},{2... | collective-permute-start | bytes 3932168 | tf_op jit(solution)/shard_map/ppermute | solution.py:492
  678.7 56.7 %collective-permute-start.26 = (bf16[512,1280]{1,0:T(8,128)(2,1)}, bf16[512,1280]{1,0:T(8,128)(2,1)}, u32[]{:S(2)}, u32[]{:S(2)}) collective-permute-start(bf16[512,1280]{1,0:T(8,128)(2,1)} %get-tuple-element.151), channel_id=1, source_target_pairs={{0,2},{2,0},{4,6},{6,4},{8,10},{10,8},{12,14},{14,12},{16,18},{18,... | collective-permute-start | bytes 3932168 | tf_op jit(solution)/shard_map/ppermute | solution.py:496
  704.0 69.0 %collective-permute-start.29 = (bf16[1024,1280]{1,0:T(8,128)(2,1)}, bf16[1024,1280]{1,0:T(8,128)(2,1)}, u32[]{:S(2)}, u32[]{:S(2)}) collective-permute-start(bf16[1024,1280]{1,0:T(8,128)(2,1)} %add_far.6), channel_id=1, source_target_pairs={{0,2},{2,0},{4,6},{6,4},{8,10},{10,8},{12,14},{14,12},{16,18},{18,... | collective-permute-start | bytes 7864328 | tf_op jit(solution)/shard_map/ppermute | solution.py:496
  704.1 36.1 %collective-permute-start.24 = (bf16[512,1280]{1,0:T(8,128)(2,1)S(1)}, bf16[512,1280]{1,0:T(8,128)(2,1)S(1)}, u32[]{:S(2)}, u32[]{:S(2)}) collective-permute-start(bf16[512,1280]{1,0:T(8,128)(2,1)S(1)} %copy-done.77), channel_id=1, source_target_pairs={{0,1},{1,0},{2,3},{3,2},{4,5},{5,4},{6,7},{7,6},{8,9},{9,8},{10,11... | collective-permute-start | bytes 3932168 | tf_op jit(solution)/shard_map/ppermute | solution.py:605
  705.5 67.6 %collective-permute-start.27 = (bf16[1024,1280]{1,0:T(8,128)(2,1)}, bf16[1024,1280]{1,0:T(8,128)(2,1)}, u32[]{:S(2)}, u32[]{:S(2)}) collective-permute-start(bf16[1024,1280]{1,0:T(8,128)(2,1)} %add_far.4), channel_id=1, source_target_pairs={{2,4},{4,2},{6,8},{8,6},{10,12},{12,10},{14,16},{16,14},{18,20},{2... | collective-permute-start | bytes 7864328 | tf_op jit(solution)/shard_map/ppermute | solution.py:492
  710.3 83.3 %collective-permute-start.34 = (bf16[1024,1280]{1,0:T(8,128)(2,1)}, bf16[1024,1280]{1,0:T(8,128)(2,1)}, u32[]{:S(2)}, u32[]{:S(2)}) collective-permute-start(bf16[1024,1280]{1,0:T(8,128)(2,1)} %add_far.7), channel_id=1, source_target_pairs={{0,2},{2,0},{4,6},{6,4},{8,10},{10,8},{12,14},{14,12},{16,18},{18,... | collective-permute-start | bytes 7864328 | tf_op jit(solution)/shard_map/ppermute | solution.py:496
  738.1 55.5 %collective-permute-start.32 = (bf16[1024,1280]{1,0:T(8,128)(2,1)}, bf16[1024,1280]{1,0:T(8,128)(2,1)}, u32[]{:S(2)}, u32[]{:S(2)}) collective-permute-start(bf16[1024,1280]{1,0:T(8,128)(2,1)} %add_far.5), channel_id=1, source_target_pairs={{2,4},{4,2},{6,8},{8,6},{10,12},{12,10},{14,16},{16,14},{18,20},{2... | collective-permute-start | bytes 7864328 | tf_op jit(solution)/shard_map/ppermute | solution.py:492
  757.6 36.0 %collective-permute-start.31 = (bf16[512,1280]{1,0:T(8,128)(2,1)}, bf16[512,1280]{1,0:T(8,128)(2,1)}, u32[]{:S(2)}, u32[]{:S(2)}) collective-permute-start(bf16[512,1280]{1,0:T(8,128)(2,1)} %get-tuple-element.166), channel_id=1, source_target_pairs={{0,1},{1,0},{2,3},{3,2},{4,5},{5,4},{6,7},{7,6},{8,9},{9,8},{10,11... | collective-permute-start | bytes 3932168 | tf_op jit(solution)/shard_map/ppermute | solution.py:605
  858.3 60.0 %collective-permute-start.36 = (f32[11520]{0:T(1024)S(1)}, f32[11520]{0:T(1024)S(1)}, u32[]{:S(2)}, u32[]{:S(2)}) collective-permute-start(f32[11520]{0:T(1024)S(1)} %pad_maximum_fusion.4), channel_id=1, source_target_pairs={{0,2},{2,0},{4,6},{6,4},{8,10},{10,8},{12,14},{14,12},{16,18},{18,... | collective-permute-start | bytes 138248 | tf_op jit(solution)/shard_map/ppermute | solution.py:585
  (130 other events, 1244.4 us)
Sparse Core Ops, SparseCore 0:
  10.9 66.0 all-gather.5
  162.3 174.2 all-gather.3
  539.8 175.6 reduce-scatter.2
  822.2 160.2 reduce-scatter.4

commit v4 on v3

--- a/solution.py
+++ b/solution.py
@@ -284,7 +284,7 @@
         in_specs=[once(x.shape) for x in xs] + [weight_spec] + [spec for _, spec in extras],
         out_specs=tuple(spec for _, _, spec in outs),
         out_shape=tuple(jax.ShapeDtypeStruct(shape, kind) for shape, kind, _ in outs),
-        compiler_params=pltpu.CompilerParams(vmem_limit_bytes=26 << 20),
+        compiler_params=pltpu.CompilerParams(vmem_limit_bytes=50 << 20),
         cost_estimate=FREE,
         name=name,
     )(*xs, weight, *[x for x, _ in extras])
@@ -394,13 +394,13 @@
         in_specs=[once(x.shape) for x in xs] + [w_spec],
         out_specs=tuple(pl.BlockSpec((r, width), lambda i: (0, i)) for r, _ in kinds),
         out_shape=tuple(jax.ShapeDtypeStruct((r, n), kind) for r, kind in kinds),
-        compiler_params=pltpu.CompilerParams(vmem_limit_bytes=26 << 20),
+        compiler_params=pltpu.CompilerParams(vmem_limit_bytes=50 << 20),
         cost_estimate=FREE,
         name=name,
     )(*xs, weight)
 
 
-def weight_terms(parts, n, kind, start=None, place=None, room=26):
+def weight_terms(parts, n, kind, start=None, place=None, room=52):
     depth = parts[0][1][0][0].shape[1]
     height = width_of(depth, 256)
     xs, ys = [], []
@@ -623,11 +623,44 @@
     return centred * scale, scale
 
 
-def norm_back(grad, z, scale, gain):
-    e = grad * gain
-    mean_e = jnp.mean(e, axis=-1, keepdims=True)
-    mean_ez = jnp.mean(e * z, axis=-1, keepdims=True)
-    return scale * (e - mean_e - z * mean_ez)
+def norm_back_rows(near, far, x, gain, base):
+    rows, width = near.shape
+    step = math.gcd(rows, 128)
+    far = jnp.broadcast_to(far, near.shape)
+
+    def kernel(near_ref, far_ref, x_ref, gain_ref, base_ref, out_ref, low_ref, sums_ref):
+        grad = near_ref[...].astype(F32) + far_ref[...].astype(F32)
+        z, scale = norm_parts(x_ref[...].astype(F32))
+        e = grad * gain_ref[...]
+        mean_e = jnp.mean(e, axis=-1, keepdims=True)
+        mean_ez = jnp.mean(e * z, axis=-1, keepdims=True)
+        before = base_ref[...].astype(F32)
+        result = before + scale * (e - mean_e - z * mean_ez)
+        out_ref[...] = result
+        low_ref[...] = result.astype(BF)
+
+        @pl.when(pl.program_id(0) == 0)
+        def _():
+            sums_ref[...] = jnp.zeros(sums_ref.shape, F32)
+
+        for row, part in enumerate((grad * z, grad, result, before)):
+            sums_ref[row : row + 1, :] += jnp.sum(part, axis=0, keepdims=True)
+
+    block = pl.BlockSpec((step, width), lambda i: (i, 0))
+    return pl.pallas_call(
+        kernel,
+        grid=(rows // step,),
+        in_specs=[block, block, block, pl.BlockSpec((1, width), lambda i: (0, 0)), block],
+        out_specs=(block, block, pl.BlockSpec((8, width), lambda i: (0, 0))),
+        out_shape=(
+            jax.ShapeDtypeStruct((rows, width), F32),
+            jax.ShapeDtypeStruct((rows, width), BF),
+            jax.ShapeDtypeStruct((8, width), F32),
+        ),
+        compiler_params=pltpu.CompilerParams(vmem_limit_bytes=26 << 20),
+        cost_estimate=FREE,
+        name="norm_back",
+    )(near, far, x, gain[None, :], base)
 
 
 def gelu_both(u):
@@ -740,11 +773,10 @@
         m.fed, m.fed_far = share([*rest, order.after(last)])
 
     def grad_second_norm(m):
-        m.grad_rows = cotangent[m.b].astype(F32)
-        m.grad_h2 = m.grad_h2.astype(F32) + order.after(m.grad_h2_far).astype(F32)
-        m.grad_middle = m.grad_rows + norm_back(m.grad_h2, m.z2, m.r2, vectors[2])
-        a = order.done(m.grad_middle.astype(BF))
-        m.grad_a = collect(a)
+        m.grad_middle, a, m.sums_two = norm_back_rows(
+            m.grad_h2, order.after(m.grad_h2_far), m.middle, vectors[2], cotangent[m.b]
+        )
+        m.grad_a = collect(order.done(a))
 
     no_bias = jnp.zeros((W,), F32)
 
@@ -759,10 +791,14 @@
             precision=lax.Precision.HIGHEST,
         )
         m.grad_q, *grads = attend_backward(
-            lax.optimization_barrier((m.q, *wait))[0], m.grad_mixed, m.pieces, m.ranges, m.lse, delta, place, heads
+            lax.optimization_barrier((m.q, *wait))[0] if wait else m.q, m.grad_mixed, m.pieces, m.ranges, m.lse, delta, place, heads
         )
         order.done(m.grad_q)
-        m.returned, m.ready = return_rows(grads, place)
+        m.grads = grads
+
+    def send_back(m):
+        near_inside, near_across, *rest = m.grads
+        m.returned, m.ready = return_rows([near_inside, order.after(near_across), *rest], place)
 
     def add_up(m, *wait):
         m.grad_kv = order.done(add_returned([order.after(x, *wait) for x in m.returned]))
@@ -781,19 +817,11 @@
         return pairs
 
     def finish(m):
-        grad_h1 = m.grad_h1.astype(F32) + order.after(m.grad_h1_far).astype(F32)
-        m.inputs_grad = m.grad_middle + norm_back(grad_h1, m.z1, m.r1, vectors[0])
-        order.done(m.inputs_grad)
-        m.norm_sums = jnp.stack(
-            (
-                jnp.sum(grad_h1 * m.z1, axis=0),
-                jnp.sum(grad_h1, axis=0),
-                jnp.sum(m.grad_h2 * m.z2, axis=0),
-                jnp.sum(m.grad_h2, axis=0),
-                jnp.sum(m.grad_middle, axis=0),
-                jnp.sum(m.grad_rows, axis=0),
-            )
+        m.inputs_grad, low, sums_one = norm_back_rows(
+            m.grad_h1, order.after(m.grad_h1_far), frames[m.b], vectors[0], m.grad_middle
         )
+        order.done(low)
+        m.norm_sums = jnp.concatenate((sums_one[:2], m.sums_two[:4]))
 
     def owned(terms, axis):
         return lax.psum_scatter(terms.astype(BF), "dp", scatter_dimension=axis, tiled=True).astype(F32)
@@ -836,25 +864,27 @@
     grad_second_norm(m1)
     fc_terms = term(m1.h2, m1.grad_u, kind=BF, start=fc1_term, place=(0, fc_terms))
     own_fc1, own_fc2 = owned(fc_terms, 1)
-    attend_back(m0, m1.grad_a[-1])
+    attend_back(m0)
+    send_back(m0)
     send_narrow(m0)
     attend_back(m1, m0.ready)
     narrow(m1, m0.fed_far)
     send_narrow(m1)
     terms = weight_terms(
         [
-            (0, rows_of(gated(m0.h1, m1.ready), m0.grad_q) + rows_of(m1.h1, m1.grad_q)),
+            (0, rows_of(gated(m0.h1), m0.grad_q) + rows_of(m1.h1, m1.grad_q)),
             (3 * W, rows_of(m0.grad_a, m0.mixed) + rows_of(m1.grad_a, m1.mixed)),
         ],
         4 * W,
         F32,
     )
     order.done(terms)
-    add_up(m0)
+    send_back(m1)
+    add_up(m0, m1.ready)
     grad_projected(m0)
     add_up(m1, m1.fed_far)
     kv_pairs = rows_of(m0.h1, m0.grad_kv) + rows_of(gated(m1.h1), m1.grad_kv)
-    terms = order.done(weight_terms([(W, kv_pairs)], 4 * W, BF, start=terms))
+    terms = order.done(weight_terms([(W, kv_pairs)], 4 * W, BF, start=terms, room=26))
     grad_projected(m1)
     own_attention = owned(lax.optimization_barrier((terms, own_fc1))[0], 0)
     finish(m0)

time: 1000 us -> 1000 us (level)
  Pallas kernels: 377 us -> 447 us
  local copies, waits for them, and re-layouts: 121 us -> 78.8 us
  other arithmetic: 63.5 us -> 35.7 us
    ppermute x5, starting transfers between devices: 81.4 us -> 30.7 us  [sum_everywhere(): x = x + lax.ppermute(x, axis, [(i, i ^ bit) for i in range(length)])]
    ppermute x4, starting transfers between devices: 46.8 us -> 94.7 us  [inside(): lax.ppermute(x, 'dp', [(i, i ^ 1) for i in range(lax.axis_size('dp'))])]
    unnamed x234 -> x154, local copies, waits for them, and re-layouts: 97 us -> 52.7 us
    pallas_call x8, Pallas kernels: 55.1 us -> 77.6 us  [back_rows(): pl.pallas_call(kernel, grid=(n // width,), in_specs=[once(x.shape) for x...]
    pallas_call x6, Pallas kernels: 66.1 us -> 84.9 us  [weight_terms(): pl.pallas_call(kernel, grid=(depth // height,), in_specs=x_spec + [once(y...]
    pallas_call x0 -> x4, Pallas kernels: none -> 16.1 us  [norm_back_rows(): pl.pallas_call(kernel, grid=(rows // step,), in_specs=[block, block, bloc...]
    pallas_call x10, Pallas kernels: 67.5 us -> 81.7 us  [dense(): pl.pallas_call(kernel, grid=(n // width,), in_specs=[once(x.shape) for x...]
    reduce_sum x6 -> x0, other arithmetic: 13.9 us -> none  [the longest x2 5.46 us: finish(): jnp.sum(m.grad_h2 * m.z2, axis=0)]
  transfers between devices with their start and end apart: 45 -> 45, of which waited for: 14 -> 13; matrix products, arithmetic and copies ran while one was open for 8% -> 6% of each run, Pallas kernels for 36% -> 42%
where the time goes in v4:
time: 1000 us; the launch traced here: 993 us
  Pallas kernels  447 us (45%)
  starting transfers between devices  233 us (23%)
  waiting for transfers between devices  179 us (18%)
  local copies, waits for them, and re-layouts  78.8 us (8%)
  other arithmetic  35.7 us (4%)
  between operations  15.1 us (2%)
    pallas_call x2, Pallas kernels, attend_backward(): pl.pallas_call(functools.partial(backward_kernel, heads, W, QB, KB), out_...  100 us
    ppermute x4, starting transfers between devices, inside(): lax.ppermute(x, 'dp', [(i, i ^ 1) for i in range(lax.axis_size('dp'))])  94.7 us
    ppermute x16, waiting for transfers between devices, partner(): return lax.ppermute(x, 'tensor', [(0, 1), (1, 0)])  86.9 us
    pallas_call x6, Pallas kernels, weight_terms(): pl.pallas_call(kernel, grid=(depth // height,), in_specs=x_spec + [once(y...  84.9 us
    pallas_call x10, Pallas kernels, dense(): pl.pallas_call(kernel, grid=(n // width,), in_specs=[once(x.shape) for x...  81.7 us
    ppermute x12, starting transfers between devices, over_dp(): return lax.ppermute(x, 'dp', pairs)  81.1 us
    pallas_call x8, Pallas kernels, back_rows(): pl.pallas_call(kernel, grid=(n // width,), in_specs=[once(x.shape) for x...  77.6 us
    pallas_call x2, Pallas kernels, attend_forward(): pl.pallas_call(functools.partial(forward_kernel, heads, W, QB, KB), out_s...  64.5 us
  transfers between devices with their start and end apart: 45, of which 13 were waited for; matrix products, arithmetic and copies ran while one was open for 6% of the time, Pallas kernels for 42%

profile of v4, /device:TPU:0, one launch (start us, length us, event | category | flops | bytes accessed | tf_op | source)
XLA Modules:
  0.0 992.9 jit_solution(13282780747648391484)
XLA Ops:
  18.8 29.5 %collective-permute-done.refs_1_ = bf16[512,1280]{1,0:T(8,128)(2,1)S(1)} collective-permute-done((bf16[512,1280]{1,0:T(8,128)(2,1)S(1)}, bf16[512,1280]{1,0:T(8,128)(2,1)S(1)}, u32[]{:S(2)}, u32[]{:S(2)}) %collective-permute-start) | collective-permute-done | bytes 1310752 | tf_op jit(solution)/shard_map/ppermute | solution.py:605
  49.4 26.2 %collective-permute-done.1.refs_1_.refs_3_ = bf16[512,1280]{1,0:T(8,128)(2,1)S(1)} collective-permute-done((bf16[512,1280]{1,0:T(8,128)(2,1)S(1)}, bf16[512,1280]{1,0:T(8,128)(2,1)S(1)}, u32[]{:S(2)}, u32[]{:S(2)}) %collective-permute-start.1) | collective-permute-done | bytes 1310752 | tf_op jit(solution)/shard_map/ppermute | solution.py:605
  101.3 63.0 %collective-permute-done.4.refs_0_ = bf16[512,1280]{1,0:T(8,128)(2,1)} collective-permute-done((bf16[512,1280]{1,0:T(8,128)(2,1)}, bf16[512,1280]{1,0:T(8,128)(2,1)}, u32[]{:S(2)}, u32[]{:S(2)}) %collective-permute-start.4) | collective-permute-done | bytes 1310752 | tf_op jit(solution)/shard_map/ppermute | solution.py:502
  187.1 10.8 %collective-permute-start.13 = (bf16[1024,1280]{1,0:T(8,128)(2,1)}, bf16[1024,1280]{1,0:T(8,128)(2,1)S(1)}, u32[]{:S(2)}, u32[]{:S(2)}) collective-permute-start(bf16[1024,1280]{1,0:T(8,128)(2,1)} %keys_values.3.refs_3_), channel_id=1, source_target_pairs={{0,2},{2,4},{4,6},{6,8},{8,10},{10,12},{12,14},{14,16},{16,18},{18... | collective-permute-start | bytes 7864328 | tf_op jit(solution)/shard_map/ppermute | solution.py:502
  222.0 32.2 %attend_forward.2 = (bf16[1024,640]{1,0:T(8,128)(2,1)}, f32[8,1024]{1,0:T(8,128)}) custom-call(s32[4]{0:T(128)} %get-tuple-element.256.lo_ref, s32[4]{0:T(128)} %get-tuple-element.257.count_ref, s32[2]{0:T(128)} %pad_add_fusion.4.place_ref.swap_ref, s32[2,1024]{1,0:T(2,128)} %pad_add_fusion.se_ref, bf16[1024,640]{1,0:T(8,128)(2,1)} %copy-done.30, ...), custom_call_target="tpu_custom_call" | custom-call | tf_op jit(solution)/shard_map/attend_forward/pallas_call | solution.py:145
  266.3 11.1 %collective-permute-start.12 = (bf16[512,1280]{1,0:T(8,128)(2,1)S(1)}, bf16[512,1280]{1,0:T(8,128)(2,1)S(1)}, u32[]{:S(2)}, u32[]{:S(2)}) collective-permute-start(bf16[512,1280]{1,0:T(8,128)(2,1)S(1)} %get-tuple-element.265), channel_id=1, source_target_pairs={{0,4},{4,8},{8,12},{12,16},{16,20},{20,24},{24,28},{1,5},{5,9},{9,... | collective-permute-start | bytes 3932168 | tf_op jit(solution)/shard_map/ppermute | solution.py:502
  278.5 35.8 %collective-permute-start.14 = (bf16[512,1280]{1,0:T(8,128)(2,1)S(1)}, bf16[512,1280]{1,0:T(8,128)(2,1)}, u32[]{:S(2)}, u32[]{:S(2)}) collective-permute-start(bf16[512,1280]{1,0:T(8,128)(2,1)S(1)} %constant_dynamic-slice_fusion.2), channel_id=1, source_target_pairs={{0,2},{4,6},{8,10},{12,14},{16,18},{20,22},{24,26},{28,30},{1,3},{... | collective-permute-start | bytes 3932168 | tf_op jit(solution)/shard_map/ppermute | solution.py:502
  322.7 32.3 %attend_forward.3 = (bf16[1024,640]{1,0:T(8,128)(2,1)}, f32[8,1024]{1,0:T(8,128)}) custom-call(s32[4]{0:T(128)} %get-tuple-element.258.lo_ref, s32[4]{0:T(128)} %get-tuple-element.259.count_ref, s32[2]{0:T(128)} %pad_add_fusion.4.place_ref.swap_ref, s32[2,1024]{1,0:T(2,128)} %pad_add_fusion.1.se_ref, bf16[1024,640]{1,0:T(8,128)(2,1)} %copy-done.29, ...), custom_call_target="tpu_custom_call" | custom-call | tf_op jit(solution)/shard_map/attend_forward/pallas_call | solution.py:145
  365.9 13.6 %widen.2 = (bf16[1024,2560]{1,0:T(8,128)(2,1)}, bf16[1024,2560]{1,0:T(8,128)(2,1)}) custom-call(bf16[512,1280]{1,0:T(8,128)(2,1)S(1)} %copy-done.32, bf16[512,1280]{1,0:T(8,128)(2,1)} %collective-permute-done.11.refs_1_, bf16[2,1280,2560]{2,1,0:T(8,128)(2,1)} %all-gather.4.cloned.1.call-done.refs_2_.refs_1_, f32[1,2560]{1,0:T(1,128)S(1)} %reshape.126.refs_3_), custom_call_target="tpu_custom_call" | custom-call | tf_op jit(solution)/shard_map/widen/pallas_call | solution.py:281
  379.5 12.4 %grad_hidden.2 = (bf16[1024,2560]{1,0:T(8,128)(2,1)}, f32[1,2560]{1,0:T(1,128)S(1)}) custom-call(bf16[512,1280]{1,0:T(8,128)(2,1)} %get-tuple-element.111.refs_0_.base_ref, bf16[512,1280]{1,0:T(8,128)(2,1)} %collective-permute-done.2.refs_1_, bf16[2,1280,2560]{2,1,0:T(8,128)(2,1)} %all-gather.4.cloned.1.call-done.refs_2_.refs_1_, ...), custom_call_target="tpu_custom_call" | custom-call | tf_op jit(solution)/shard_map/grad_hidden/pallas_call | solution.py:281
  392.0 11.7 %grad_normed.2 = (f32[512,1280]{1,0:T(8,128)S(1)}, bf16[512,1280]{1,0:T(8,128)(2,1)}) custom-call(bf16[1024,2560]{1,0:T(8,128)(2,1)} %get-tuple-element.130.refs_0_.refs_2_, bf16[2,1280,2560]{2,1,0:T(8,128)(2,1)} %all-gather.4.cloned.1.call-done.refs_2_.refs_1_), custom_call_target="tpu_custom_call" | custom-call | tf_op jit(solution)/shard_map/grad_normed/pallas_call | solution.py:391
  411.2 11.3 %narrow.2 = (f32[512,1280]{1,0:T(8,128)S(1)}, bf16[512,1280]{1,0:T(8,128)(2,1)S(1)}) custom-call(bf16[1024,2560]{1,0:T(8,128)(2,1)} %get-tuple-element.133.refs_0_.refs_2_, bf16[2,1280,2560]{2,1,0:T(8,128)(2,1)} %all-gather.4.cloned.1.call-done.refs_2_.refs_1_), custom_call_target="tpu_custom_call" | custom-call | tf_op jit(solution)/shard_map/narrow/pallas_call | solution.py:391
  424.0 13.8 %weight_terms.6.refs_3_ = f32[1280,2560]{1,0:T(8,128)} custom-call(bf16[512,1280]{1,0:T(8,128)(2,1)} %get-tuple-element.111.refs_0_.base_ref, bf16[512,1280]{1,0:T(8,128)(2,1)} %collective-permute-done.2.refs_1_, bf16[1024,2560]{1,0:T(8,128)(2,1)} %get-tuple-element.133.refs_0_.refs_2_), custom_call_target="tpu_custom_call" | custom-call | tf_op jit(solution)/shard_map/weight_terms/pallas_call | solution.py:476
  448.8 13.4 %weight_terms.7.refs_3_ = f32[1280,2560]{1,0:T(8,128)} custom-call(bf16[512,1280]{1,0:T(8,128)(2,1)S(1)} %copy-done.33, bf16[512,1280]{1,0:T(8,128)(2,1)} %collective-permute-done.11.refs_1_, bf16[1024,2560]{1,0:T(8,128)(2,1)} %get-tuple-element.130.refs_0_.refs_2_), custom_call_target="tpu_custom_call" | custom-call | tf_op jit(solution)/shard_map/weight_terms/pallas_call | solution.py:476
  462.3 14.2 %widen.3 = (bf16[1024,2560]{1,0:T(8,128)(2,1)}, bf16[1024,2560]{1,0:T(8,128)(2,1)}) custom-call(bf16[512,1280]{1,0:T(8,128)(2,1)} %add_convert_fusion.2.refs_0_, bf16[512,1280]{1,0:T(8,128)(2,1)} %collective-permute-done.21.refs_1_, bf16[2,1280,2560]{2,1,0:T(8,128)(2,1)} %all-gather.4.cloned.1.call-done.refs_2_.refs_1_, f32[1,2560]{1,0:T(1,128)S(1)} %reshape.126.refs_3_), custom_call_target="tpu_custom_call" | custom-call | tf_op jit(solution)/shard_map/widen/pallas_call | solution.py:281
  476.5 12.0 %grad_hidden.3 = (bf16[1024,2560]{1,0:T(8,128)(2,1)}, f32[1,2560]{1,0:T(1,128)S(1)}) custom-call(bf16[512,1280]{1,0:T(8,128)(2,1)S(1)} %copy-done.18, bf16[512,1280]{1,0:T(8,128)(2,1)} %collective-permute-done.3.refs_1_, bf16[2,1280,2560]{2,1,0:T(8,128)(2,1)} %all-gather.4.cloned.1.call-done.refs_2_.refs_1_, bf16[1024,2560]{1,0:T(8,128)(2,1)} %get-tuple-element.143.refs_3_), custom_call_target="tpu_custom_call" | custom-call | tf_op jit(solution)/shard_map/grad_hidden/pallas_call | solution.py:281
  488.5 11.5 %grad_normed.3 = (f32[512,1280]{1,0:T(8,128)S(1)}, bf16[512,1280]{1,0:T(8,128)(2,1)}) custom-call(bf16[1024,2560]{1,0:T(8,128)(2,1)} %get-tuple-element.146.refs_0_.refs_2_, bf16[2,1280,2560]{2,1,0:T(8,128)(2,1)} %all-gather.4.cloned.1.call-done.refs_2_.refs_1_), custom_call_target="tpu_custom_call" | custom-call | tf_op jit(solution)/shard_map/grad_normed/pallas_call | solution.py:391
  501.1 15.1 %weight_terms.8.refs_4_ = bf16[2,1280,2560]{2,1,0:T(8,128)(2,1)} custom-call(bf16[512,1280]{1,0:T(8,128)(2,1)S(1)} %copy-done.18, bf16[512,1280]{1,0:T(8,128)(2,1)} %collective-permute-done.3.refs_1_, bf16[1024,2560]{1,0:T(8,128)(2,1)} %get-tuple-element.166.refs_2_.refs_0_, f32[1280,2560]{1,0:T(8,128)} %weight_terms.6.refs_3_), custom_call_target="tpu_custom_call" | custom-call | tf_op jit(solution)/shard_map/weight_terms/pallas_call | solution.py:476
  531.7 15.1 %weight_terms.9 = bf16[2,1280,2560]{2,1,0:T(8,128)(2,1)} custom-call(bf16[512,1280]{1,0:T(8,128)(2,1)} %add_convert_fusion.2.refs_0_, bf16[512,1280]{1,0:T(8,128)(2,1)} %collective-permute-done.21.refs_1_, bf16[1024,2560]{1,0:T(8,128)(2,1)} %get-tuple-element.146.refs_0_.refs_2_, f32[1280,2560]{1,0:T(8,128)} %weight_terms.7.refs_3_, ...), custom_call_target="tpu_custom_call", output_to_operand_aliasing={{}: (4, {})} | custom-call | tf_op jit(solution)/shard_map/weight_terms/pallas_call | solution.py:476
  555.5 50.3 %attend_backward.2 = (bf16[1024,640]{1,0:T(8,128)(2,1)}, bf16[1024,1280]{1,0:T(8,128)(2,1)}, bf16[1024,1280]{1,0:T(8,128)(2,1)}, bf16[1024,1280]{1,0:T(8,128)(2,...) custom-call(s32[4]{0:T(128)} %get-tuple-element.249.lo_ref, s32[4]{0:T(128)} %get-tuple-element.250.count_ref, ...), custom_call_target="tpu_custom_call" | custom-call | tf_op jit(solution)/shard_map/attend_backward/pallas_call | solution.py:230
  605.8 20.0 %collective-permute-start.25 = (bf16[512,1280]{1,0:T(8,128)(2,1)}, bf16[512,1280]{1,0:T(8,128)(2,1)}, u32[]{:S(2)}, u32[]{:S(2)}) collective-permute-start(bf16[512,1280]{1,0:T(8,128)(2,1)} %get-tuple-element.162), channel_id=1, source_target_pairs={{0,2},{2,0},{4,6},{6,4},{8,10},{10,8},{12,14},{14,12},{16,18},{18,... | collective-permute-start | bytes 3932168 | tf_op jit(solution)/shard_map/ppermute | solution.py:496
  639.1 49.8 %attend_backward.3 = (bf16[1024,640]{1,0:T(8,128)(2,1)}, bf16[1024,1280]{1,0:T(8,128)(2,1)}, bf16[1024,1280]{1,0:T(8,128)(2,1)}, bf16[1024,1280]{1,0:T(8,128)(2,...) custom-call(s32[4]{0:T(128)} %get-tuple-element.246.lo_ref, s32[4]{0:T(128)} %get-tuple-element.247.count_ref, ...), custom_call_target="tpu_custom_call" | custom-call | tf_op jit(solution)/shard_map/attend_backward/pallas_call | solution.py:230
  688.9 25.9 %collective-permute-start.26 = (bf16[512,1280]{1,0:T(8,128)(2,1)}, bf16[512,1280]{1,0:T(8,128)(2,1)}, u32[]{:S(2)}, u32[]{:S(2)}) collective-permute-start(bf16[512,1280]{1,0:T(8,128)(2,1)} %get-tuple-element.170), channel_id=1, source_target_pairs={{0,2},{2,0},{4,6},{6,4},{8,10},{10,8},{12,14},{14,12},{16,18},{18,... | collective-permute-start | bytes 3932168 | tf_op jit(solution)/shard_map/ppermute | solution.py:496
  723.4 11.0 %narrow.3 = (f32[512,1280]{1,0:T(8,128)S(1)}, bf16[512,1280]{1,0:T(8,128)(2,1)S(1)}) custom-call(bf16[1024,2560]{1,0:T(8,128)(2,1)} %get-tuple-element.166.refs_2_.refs_0_, bf16[2,1280,2560]{2,1,0:T(8,128)(2,1)} %all-gather.4.cloned.1.call-done.refs_2_.refs_1_), custom_call_target="tpu_custom_call" | custom-call | tf_op jit(solution)/shard_map/narrow/pallas_call | solution.py:391
  735.6 16.0 %weight_terms.10.refs_6_ = f32[1280,2560]{1,0:T(8,128)} custom-call(bf16[512,1280]{1,0:T(8,128)(2,1)S(1)} %copy-done.2, bf16[512,1280]{1,0:T(8,128)(2,1)} %copy-done.11, bf16[512,1280]{1,0:T(8,128)(2,1)} %copy-done.4, bf16[512,1280]{1,0:T(8,128)(2,1)} %copy-done.15, bf16[512,1280]{1,0:T(8,128)(2,1)} %get-tuple-element.140.refs_0_.refs_4_, ...), custom_call_target="tpu_custom_call" | custom-call | tf_op jit(solution)/shard_map/weight_terms/pallas_call | solution.py:476
  759.1 47.0 %collective-permute-start.34 = (bf16[1024,1280]{1,0:T(8,128)(2,1)}, bf16[1024,1280]{1,0:T(8,128)(2,1)}, u32[]{:S(2)}, u32[]{:S(2)}) collective-permute-start(bf16[1024,1280]{1,0:T(8,128)(2,1)} %add_far.7), channel_id=1, source_target_pairs={{0,2},{2,0},{4,6},{6,4},{8,10},{10,8},{12,14},{14,12},{16,18},{18,... | collective-permute-start | bytes 7864328 | tf_op jit(solution)/shard_map/ppermute | solution.py:496
  823.4 13.7 %collective-permute-done.31 = bf16[512,1280]{1,0:T(8,128)(2,1)} collective-permute-done((bf16[512,1280]{1,0:T(8,128)(2,1)}, bf16[512,1280]{1,0:T(8,128)(2,1)}, u32[]{:S(2)}, u32[]{:S(2)}) %collective-permute-start.31) | collective-permute-done | bytes 1310752 | tf_op jit(solution)/shard_map/ppermute | solution.py:605
  851.3 11.6 %weight_terms.11 = bf16[1280,2560]{1,0:T(8,128)(2,1)S(1)} custom-call(bf16[512,1280]{1,0:T(8,128)(2,1)S(1)} %copy-done.3, bf16[512,1280]{1,0:T(8,128)(2,1)S(1)} %copy-done.14, bf16[512,1280]{1,0:T(8,128)(2,1)S(1)} %copy-done.5, bf16[512,1280]{1,0:T(8,128)(2,1)S(1)} %copy-done.17, bf16[1024,1280]{1,0:T(8,128)(2,1)S(1)} %copy-done.6, ...), custom_call_target="tpu_custom_call" | custom-call | tf_op jit(solution)/shard_map/weight_terms/pallas_call | solution.py:476
  870.0 9.6 grad_projected.3
  895.5 11.1 %collective-permute-done.35.far_ref = bf16[512,1280]{1,0:T(8,128)(2,1)S(1)} collective-permute-done((bf16[512,1280]{1,0:T(8,128)(2,1)}, bf16[512,1280]{1,0:T(8,128)(2,1)S(1)}, u32[]{:S(2)}, u32[]{:S(2)}) %collective-permute-start.35) | collective-permute-done | bytes 1310752 | tf_op jit(solution)/shard_map/ppermute | solution.py:605
  911.8 21.9 %collective-permute-start.36 = (f32[11520]{0:T(1024)S(1)}, f32[11520]{0:T(1024)S(1)}, u32[]{:S(2)}, u32[]{:S(2)}) collective-permute-start(f32[11520]{0:T(1024)S(1)} %pad_maximum_fusion.4), channel_id=1, source_target_pairs={{0,2},{2,0},{4,6},{6,4},{8,10},{10,8},{12,14},{14,12},{16,18},{18,... | collective-permute-start | bytes 138248 | tf_op jit(solution)/shard_map/ppermute | solution.py:585
  963.3 19.2 %reduce-scatter.5.cloned.1.call-done = bf16[80,2560]{1,0:T(8,128)(2,1)} async-done(((bf16[1280,2560]{1,0:T(8,128)(2,1)}), bf16[80,2560]{1,0:T(8,128)(2,1)}) %reduce-scatter.5.cloned.1.call-update) | async-done | bytes 409616 | tf_op jit(solution)/shard_map/reduce_scatter | solution.py:827
  (345 shorter events, 285.9 us)
Async XLA Ops:
  7.2 69.8 %all-gather.6.cloned.1.call-start = ((), (), s32[]{:S(2)}) async-start(), calls=%async_computation.5 | async-start | bytes 6963200 | tf_op jit(solution)/shard_map/all_gather | solution.py:694
  10.1 354.5 %all-gather.4.cloned.1.call-start = ((), (), s32[]{:S(2)}) async-start(), calls=%async_computation.2 | async-start | bytes 13926400 | tf_op jit(solution)/shard_map/all_gather | solution.py:837
  15.7 32.6 %collective-permute-start = (bf16[512,1280]{1,0:T(8,128)(2,1)S(1)}, bf16[512,1280]{1,0:T(8,128)(2,1)S(1)}, u32[]{:S(2)}, u32[]{:S(2)}) collective-permute-start(bf16[512,1280]{1,0:T(8,128)(2,1)S(1)} %get-tuple-element.260.refs_0_), channel_id=1, source_target_pairs={{0,1},{1,0},{2,3},{3,2},{4,5},{5,4},{6,7},{7,6},{8,9},{9,8},{10,11... | collective-permute-start | bytes 3932168 | tf_op jit(solution)/shard_map/ppermute | solution.py:605
  18.7 56.9 %collective-permute-start.1 = (bf16[512,1280]{1,0:T(8,128)(2,1)S(1)}, bf16[512,1280]{1,0:T(8,128)(2,1)S(1)}, u32[]{:S(2)}, u32[]{:S(2)}) collective-permute-start(bf16[512,1280]{1,0:T(8,128)(2,1)S(1)} %get-tuple-element.261.refs_0_.refs_2_), channel_id=1, source_target_pairs={{0,1},{1,0},{2,3},{3,2},{4,5},{5,4},{6,7},{7,6},{8,9},{9,8},{10,11... | collective-permute-start | bytes 3932168 | tf_op jit(solution)/shard_map/ppermute | solution.py:605
  85.2 79.1 %collective-permute-start.5 = (bf16[1024,1280]{1,0:T(8,128)(2,1)}, bf16[1024,1280]{1,0:T(8,128)(2,1)}, u32[]{:S(2)}, u32[]{:S(2)}) collective-permute-start(bf16[1024,1280]{1,0:T(8,128)(2,1)} %keys_values.2.refs_3_), channel_id=1, source_target_pairs={{0,2},{2,4},{4,6},{6,8},{8,10},{10,12},{12,14},{14,16},{16,18},{18... | collective-permute-start | bytes 7864328 | tf_op jit(solution)/shard_map/ppermute | solution.py:502
  88.9 75.5 %collective-permute-start.7 = (bf16[1024,1280]{1,0:T(8,128)(2,1)}, bf16[1024,1280]{1,0:T(8,128)(2,1)}, u32[]{:S(2)}, u32[]{:S(2)}) collective-permute-start(bf16[1024,1280]{1,0:T(8,128)(2,1)} %keys_values.2.refs_3_), channel_id=1, source_target_pairs={{2,0},{4,2},{6,4},{8,6},{10,8},{12,10},{14,12},{16,14},{18,16},{20... | collective-permute-start | bytes 7864328 | tf_op jit(solution)/shard_map/ppermute | solution.py:502
  93.6 70.7 %collective-permute-start.4 = (bf16[512,1280]{1,0:T(8,128)(2,1)}, bf16[512,1280]{1,0:T(8,128)(2,1)}, u32[]{:S(2)}, u32[]{:S(2)}) collective-permute-start(bf16[512,1280]{1,0:T(8,128)(2,1)} %get-tuple-element.267), channel_id=1, source_target_pairs={{0,4},{4,8},{8,12},{12,16},{16,20},{20,24},{24,28},{1,5},{5,9},{9,... | collective-permute-start | bytes 3932168 | tf_op jit(solution)/shard_map/ppermute | solution.py:502
  98.6 65.7 %collective-permute-start.8 = (bf16[512,1280]{1,0:T(8,128)(2,1)}, bf16[512,1280]{1,0:T(8,128)(2,1)}, u32[]{:S(2)}, u32[]{:S(2)}) collective-permute-start(bf16[512,1280]{1,0:T(8,128)(2,1)} %get-tuple-element.266), channel_id=1, source_target_pairs={{6,2},{10,6},{14,10},{18,14},{22,18},{26,22},{30,26},{7,3},{11,7},... | collective-permute-start | bytes 3932168 | tf_op jit(solution)/shard_map/ppermute | solution.py:502
  164.4 701.2 %reduce-scatter.3.cloned.1.call-start = ((), (), s32[]{:S(2)}) async-start(), calls=%async_computation.3 | async-start | bytes 13926400 | tf_op jit(solution)/shard_map/reduce_scatter | solution.py:827
  167.9 42.9 %collective-permute-start.2 = (bf16[512,1280]{1,0:T(8,128)(2,1)}, bf16[512,1280]{1,0:T(8,128)(2,1)}, u32[]{:S(2)}, u32[]{:S(2)}) collective-permute-start(bf16[512,1280]{1,0:T(8,128)(2,1)} %get-tuple-element.111.refs_0_.base_ref), channel_id=1, source_target_pairs={{0,1},{1,0},{2,3},{3,2},{4,5},{5,4},{6,7},{7,6},{8,9},{9,8},{10,11... | collective-permute-start | bytes 3932168 | tf_op jit(solution)/shard_map/ppermute | solution.py:605
  169.7 52.3 %collective-permute-start.3 = (bf16[512,1280]{1,0:T(8,128)(2,1)}, bf16[512,1280]{1,0:T(8,128)(2,1)}, u32[]{:S(2)}, u32[]{:S(2)}) collective-permute-start(bf16[512,1280]{1,0:T(8,128)(2,1)} %get-tuple-element.112.refs_0_.base_ref), channel_id=1, source_target_pairs={{0,1},{1,0},{2,3},{3,2},{4,5},{5,4},{6,7},{7,6},{8,9},{9,8},{10,11... | collective-permute-start | bytes 3932168 | tf_op jit(solution)/shard_map/ppermute | solution.py:605
  187.1 91.3 %collective-permute-start.13 = (bf16[1024,1280]{1,0:T(8,128)(2,1)}, bf16[1024,1280]{1,0:T(8,128)(2,1)S(1)}, u32[]{:S(2)}, u32[]{:S(2)}) collective-permute-start(bf16[1024,1280]{1,0:T(8,128)(2,1)} %keys_values.3.refs_3_), channel_id=1, source_target_pairs={{0,2},{2,4},{4,6},{6,8},{8,10},{10,12},{12,14},{14,16},{16,18},{18... | collective-permute-start | bytes 7864328 | tf_op jit(solution)/shard_map/ppermute | solution.py:502
  198.0 116.3 %collective-permute-start.15 = (bf16[1024,1280]{1,0:T(8,128)(2,1)}, bf16[1024,1280]{1,0:T(8,128)(2,1)}, u32[]{:S(2)}, u32[]{:S(2)}) collective-permute-start(bf16[1024,1280]{1,0:T(8,128)(2,1)} %keys_values.3.refs_3_), channel_id=1, source_target_pairs={{2,0},{4,2},{6,4},{8,6},{10,8},{12,10},{14,12},{16,14},{18,16},{20... | collective-permute-start | bytes 7864328 | tf_op jit(solution)/shard_map/ppermute | solution.py:502
  261.9 55.0 %collective-permute-start.10 = (bf16[512,1280]{1,0:T(8,128)(2,1)S(1)}, bf16[512,1280]{1,0:T(8,128)(2,1)S(1)}, u32[]{:S(2)}, u32[]{:S(2)}) collective-permute-start(bf16[512,1280]{1,0:T(8,128)(2,1)S(1)} %get-tuple-element.117), channel_id=1, source_target_pairs={{0,1},{1,0},{2,3},{3,2},{4,5},{5,4},{6,7},{7,6},{8,9},{9,8},{10,11... | collective-permute-start | bytes 3932168 | tf_op jit(solution)/shard_map/ppermute | solution.py:605
  266.3 54.9 %collective-permute-start.12 = (bf16[512,1280]{1,0:T(8,128)(2,1)S(1)}, bf16[512,1280]{1,0:T(8,128)(2,1)S(1)}, u32[]{:S(2)}, u32[]{:S(2)}) collective-permute-start(bf16[512,1280]{1,0:T(8,128)(2,1)S(1)} %get-tuple-element.265), channel_id=1, source_target_pairs={{0,4},{4,8},{8,12},{12,16},{16,20},{20,24},{24,28},{1,5},{5,9},{9,... | collective-permute-start | bytes 3932168 | tf_op jit(solution)/shard_map/ppermute | solution.py:502
  277.5 43.7 %collective-permute-start.16 = (bf16[512,1280]{1,0:T(8,128)(2,1)S(1)}, bf16[512,1280]{1,0:T(8,128)(2,1)S(1)}, u32[]{:S(2)}, u32[]{:S(2)}) collective-permute-start(bf16[512,1280]{1,0:T(8,128)(2,1)S(1)} %get-tuple-element.264), channel_id=1, source_target_pairs={{6,2},{10,6},{14,10},{18,14},{22,18},{26,22},{30,26},{7,3},{11,7},... | collective-permute-start | bytes 3932168 | tf_op jit(solution)/shard_map/ppermute | solution.py:502
  278.5 42.7 %collective-permute-start.14 = (bf16[512,1280]{1,0:T(8,128)(2,1)S(1)}, bf16[512,1280]{1,0:T(8,128)(2,1)}, u32[]{:S(2)}, u32[]{:S(2)}) collective-permute-start(bf16[512,1280]{1,0:T(8,128)(2,1)S(1)} %constant_dynamic-slice_fusion.2), channel_id=1, source_target_pairs={{0,2},{4,6},{8,10},{12,14},{16,18},{20,22},{24,26},{28,30},{1,3},{... | collective-permute-start | bytes 3932168 | tf_op jit(solution)/shard_map/ppermute | solution.py:502
  318.5 46.0 %collective-permute-start.11 = (bf16[512,1280]{1,0:T(8,128)(2,1)S(1)}, bf16[512,1280]{1,0:T(8,128)(2,1)}, u32[]{:S(2)}, u32[]{:S(2)}) collective-permute-start(bf16[512,1280]{1,0:T(8,128)(2,1)S(1)} %add_convert_fusion.3.refs_0_), channel_id=1, source_target_pairs={{0,1},{1,0},{2,3},{3,2},{4,5},{5,4},{6,7},{7,6},{8,9},{9,8},{10,11... | collective-permute-start | bytes 3932168 | tf_op jit(solution)/shard_map/ppermute | solution.py:605
  363.4 41.8 %collective-permute-start.18 = (bf16[512,1280]{1,0:T(8,128)(2,1)}, bf16[512,1280]{1,0:T(8,128)(2,1)}, u32[]{:S(2)}, u32[]{:S(2)}) collective-permute-start(bf16[512,1280]{1,0:T(8,128)(2,1)} %get-tuple-element.126), channel_id=1, source_target_pairs={{0,1},{1,0},{2,3},{3,2},{4,5},{5,4},{6,7},{7,6},{8,9},{9,8},{10,11... | collective-permute-start | bytes 3932168 | tf_op jit(solution)/shard_map/ppermute | solution.py:605
  410.0 52.3 %collective-permute-start.21 = (bf16[512,1280]{1,0:T(8,128)(2,1)}, bf16[512,1280]{1,0:T(8,128)(2,1)}, u32[]{:S(2)}, u32[]{:S(2)}) collective-permute-start(bf16[512,1280]{1,0:T(8,128)(2,1)} %add_convert_fusion.2.refs_0_), channel_id=1, source_target_pairs={{0,1},{1,0},{2,3},{3,2},{4,5},{5,4},{6,7},{7,6},{8,9},{9,8},{10,11... | collective-permute-start | bytes 3932168 | tf_op jit(solution)/shard_map/ppermute | solution.py:605
  446.6 54.5 %collective-permute-start.20 = (bf16[512,1280]{1,0:T(8,128)(2,1)}, bf16[512,1280]{1,0:T(8,128)(2,1)S(1)}, u32[]{:S(2)}, u32[]{:S(2)}) collective-permute-start(bf16[512,1280]{1,0:T(8,128)(2,1)} %get-tuple-element.140.refs_0_.refs_4_), channel_id=1, source_target_pairs={{0,1},{1,0},{2,3},{3,2},{4,5},{5,4},{6,7},{7,6},{8,9},{9,8},{10,11... | collective-permute-start | bytes 3932168 | tf_op jit(solution)/shard_map/ppermute | solution.py:605
  546.9 435.6 %reduce-scatter.5.cloned.1.call-start = ((), (), s32[]{:S(2)}) async-start(), calls=%async_computation.4 | async-start | bytes 6963200 | tf_op jit(solution)/shard_map/reduce_scatter | solution.py:827
  546.9 81.8 %collective-permute-start.24 = (bf16[512,1280]{1,0:T(8,128)(2,1)}, bf16[512,1280]{1,0:T(8,128)(2,1)}, u32[]{:S(2)}, u32[]{:S(2)}) collective-permute-start(bf16[512,1280]{1,0:T(8,128)(2,1)} %copy-done.36), channel_id=1, source_target_pairs={{0,1},{1,0},{2,3},{3,2},{4,5},{5,4},{6,7},{7,6},{8,9},{9,8},{10,11... | collective-permute-start | bytes 3932168 | tf_op jit(solution)/shard_map/ppermute | solution.py:605
  625.7 97.7 %collective-permute-start.23 = (bf16[512,1280]{1,0:T(8,128)(2,1)}, bf16[512,1280]{1,0:T(8,128)(2,1)}, u32[]{:S(2)}, u32[]{:S(2)}) collective-permute-start(bf16[512,1280]{1,0:T(8,128)(2,1)} %copy-done.58), channel_id=1, source_target_pairs={{0,1},{1,0},{2,3},{3,2},{4,5},{5,4},{6,7},{7,6},{8,9},{9,8},{10,11... | collective-permute-start | bytes 3932168 | tf_op jit(solution)/shard_map/ppermute | solution.py:605
  626.6 92.3 %collective-permute-start.28 = (bf16[512,1280]{1,0:T(8,128)(2,1)}, bf16[512,1280]{1,0:T(8,128)(2,1)}, u32[]{:S(2)}, u32[]{:S(2)}) collective-permute-start(bf16[512,1280]{1,0:T(8,128)(2,1)} %get-tuple-element.174), channel_id=1, source_target_pairs={{2,4},{4,2},{6,8},{8,6},{10,12},{12,10},{14,16},{16,14},{18,20},{2... | collective-permute-start | bytes 3932168 | tf_op jit(solution)/shard_map/ppermute | solution.py:492
  688.9 62.6 %collective-permute-start.26 = (bf16[512,1280]{1,0:T(8,128)(2,1)}, bf16[512,1280]{1,0:T(8,128)(2,1)}, u32[]{:S(2)}, u32[]{:S(2)}) collective-permute-start(bf16[512,1280]{1,0:T(8,128)(2,1)} %get-tuple-element.170), channel_id=1, source_target_pairs={{0,2},{2,0},{4,6},{6,4},{8,10},{10,8},{12,14},{14,12},{16,18},{18,... | collective-permute-start | bytes 3932168 | tf_op jit(solution)/shard_map/ppermute | solution.py:496
  714.8 41.6 %collective-permute-start.33 = (bf16[512,1280]{1,0:T(8,128)(2,1)}, bf16[512,1280]{1,0:T(8,128)(2,1)}, u32[]{:S(2)}, u32[]{:S(2)}) collective-permute-start(bf16[512,1280]{1,0:T(8,128)(2,1)} %get-tuple-element.185), channel_id=1, source_target_pairs={{2,4},{4,2},{6,8},{8,6},{10,12},{12,10},{14,16},{16,14},{18,20},{2... | collective-permute-start | bytes 3932168 | tf_op jit(solution)/shard_map/ppermute | solution.py:492
  716.6 90.0 %collective-permute-start.27 = (bf16[1024,1280]{1,0:T(8,128)(2,1)}, bf16[1024,1280]{1,0:T(8,128)(2,1)}, u32[]{:S(2)}, u32[]{:S(2)}) collective-permute-start(bf16[1024,1280]{1,0:T(8,128)(2,1)} %add_far.4), channel_id=1, source_target_pairs={{2,4},{4,2},{6,8},{8,6},{10,12},{12,10},{14,16},{16,14},{18,20},{2... | collective-permute-start | bytes 7864328 | tf_op jit(solution)/shard_map/ppermute | solution.py:492
  721.6 85.0 %collective-permute-start.29 = (bf16[1024,1280]{1,0:T(8,128)(2,1)}, bf16[1024,1280]{1,0:T(8,128)(2,1)}, u32[]{:S(2)}, u32[]{:S(2)}) collective-permute-start(bf16[1024,1280]{1,0:T(8,128)(2,1)} %add_far.6), channel_id=1, source_target_pairs={{0,2},{2,0},{4,6},{6,4},{8,10},{10,8},{12,14},{14,12},{16,18},{18,... | collective-permute-start | bytes 7864328 | tf_op jit(solution)/shard_map/ppermute | solution.py:496
  754.3 82.9 %collective-permute-start.32 = (bf16[1024,1280]{1,0:T(8,128)(2,1)}, bf16[1024,1280]{1,0:T(8,128)(2,1)}, u32[]{:S(2)}, u32[]{:S(2)}) collective-permute-start(bf16[1024,1280]{1,0:T(8,128)(2,1)} %add_far.5), channel_id=1, source_target_pairs={{2,4},{4,2},{6,8},{8,6},{10,12},{12,10},{14,16},{16,14},{18,20},{2... | collective-permute-start | bytes 7864328 | tf_op jit(solution)/shard_map/ppermute | solution.py:492
  759.1 78.0 %collective-permute-start.34 = (bf16[1024,1280]{1,0:T(8,128)(2,1)}, bf16[1024,1280]{1,0:T(8,128)(2,1)}, u32[]{:S(2)}, u32[]{:S(2)}) collective-permute-start(bf16[1024,1280]{1,0:T(8,128)(2,1)} %add_far.7), channel_id=1, source_target_pairs={{0,2},{2,0},{4,6},{6,4},{8,10},{10,8},{12,14},{14,12},{16,18},{18,... | collective-permute-start | bytes 7864328 | tf_op jit(solution)/shard_map/ppermute | solution.py:496
  806.1 31.0 %collective-permute-start.31 = (bf16[512,1280]{1,0:T(8,128)(2,1)}, bf16[512,1280]{1,0:T(8,128)(2,1)}, u32[]{:S(2)}, u32[]{:S(2)}) collective-permute-start(bf16[512,1280]{1,0:T(8,128)(2,1)} %copy-done.60), channel_id=1, source_target_pairs={{0,1},{1,0},{2,3},{3,2},{4,5},{5,4},{6,7},{7,6},{8,9},{9,8},{10,11... | collective-permute-start | bytes 3932168 | tf_op jit(solution)/shard_map/ppermute | solution.py:605
  (90 other events, 1192.2 us)
Sparse Core Ops, SparseCore 0:
  10.9 66.0 all-gather.5
  164.5 171.3 all-gather.3
  547.0 183.4 reduce-scatter.2
  868.3 114.1 reduce-scatter.4

commit v5 on v4

--- a/solution.py
+++ b/solution.py
@@ -284,7 +284,7 @@
         in_specs=[once(x.shape) for x in xs] + [weight_spec] + [spec for _, spec in extras],
         out_specs=tuple(spec for _, _, spec in outs),
         out_shape=tuple(jax.ShapeDtypeStruct(shape, kind) for shape, kind, _ in outs),
-        compiler_params=pltpu.CompilerParams(vmem_limit_bytes=50 << 20),
+        compiler_params=pltpu.CompilerParams(vmem_limit_bytes=(26 if weight.shape[0] == 1 else 50) << 20),
         cost_estimate=FREE,
         name=name,
     )(*xs, weight, *[x for x, _ in extras])
@@ -394,7 +394,7 @@
         in_specs=[once(x.shape) for x in xs] + [w_spec],
         out_specs=tuple(pl.BlockSpec((r, width), lambda i: (0, i)) for r, _ in kinds),
         out_shape=tuple(jax.ShapeDtypeStruct((r, n), kind) for r, kind in kinds),
-        compiler_params=pltpu.CompilerParams(vmem_limit_bytes=50 << 20),
+        compiler_params=pltpu.CompilerParams(vmem_limit_bytes=(26 if weight.shape[0] == 1 else 50) << 20),
         cost_estimate=FREE,
         name=name,
     )(*xs, weight)

time: 1000 us -> 995 us (level)
  starting transfers between devices: 233 us -> 206 us
  waiting for transfers between devices: 179 us -> 200 us
  Pallas kernels: 447 us -> 432 us
  local copies, waits for them, and re-layouts: 78.8 us -> 93.5 us
    ppermute x4, starting transfers between devices: 94.7 us -> 72.1 us  [inside(): lax.ppermute(x, 'dp', [(i, i ^ 1) for i in range(lax.axis_size('dp'))])]
    unnamed x154 -> x172, local copies, waits for them, and re-layouts: 52.7 us -> 69.4 us
    ppermute x16, waiting for transfers between devices: 86.9 us -> 101 us  [partner(): return lax.ppermute(x, 'tensor', [(0, 1), (1, 0)])]
    pallas_call x8, Pallas kernels: 77.6 us -> 66.3 us  [back_rows(): pl.pallas_call(kernel, grid=(n // width,), in_specs=[once(x.shape) for x...]
  transfers between devices with their start and end apart: 45 -> 45, of which waited for: 13 -> 16; matrix products, arithmetic and copies ran while one was open for 6% -> 5% of each run, Pallas kernels for 42% -> 41%
where the time goes in v5:
time: 995 us; the launch traced here: 986 us
  Pallas kernels  432 us (43%)
  starting transfers between devices  206 us (21%)
  waiting for transfers between devices  200 us (20%)
  local copies, waits for them, and re-layouts  93.5 us (9%)
  other arithmetic  35.3 us (4%)
  between operations  15.1 us (2%)
    pallas_call x2, Pallas kernels, attend_backward(): pl.pallas_call(functools.partial(backward_kernel, heads, W, QB, KB), out_...  102 us
    ppermute x16, waiting for transfers between devices, partner(): return lax.ppermute(x, 'tensor', [(0, 1), (1, 0)])  101 us
    pallas_call x6, Pallas kernels, weight_terms(): pl.pallas_call(kernel, grid=(depth // height,), in_specs=x_spec + [once(y...  86.8 us
    pallas_call x10, Pallas kernels, dense(): pl.pallas_call(kernel, grid=(n // width,), in_specs=[once(x.shape) for x...  74.9 us
    ppermute x12, starting transfers between devices, over_dp(): return lax.ppermute(x, 'dp', pairs)  74.7 us
    ppermute x4, starting transfers between devices, inside(): lax.ppermute(x, 'dp', [(i, i ^ 1) for i in range(lax.axis_size('dp'))])  72.1 us
    ppermute x12, waiting for transfers between devices, over_dp(): return lax.ppermute(x, 'dp', pairs)  69.7 us
    unnamed x172, local copies, waits for them, and re-layouts  69.4 us
  transfers between devices with their start and end apart: 45, of which 16 were waited for; matrix products, arithmetic and copies ran while one was open for 5% of the time, Pallas kernels for 41%

profile of v5, /device:TPU:0, one launch (start us, length us, event | category | flops | bytes accessed | tf_op | source)
XLA Modules:
  0.0 985.9 jit_solution(6203988601716171102)
XLA Ops:
  20.8 27.3 %collective-permute-done.refs_1_ = bf16[512,1280]{1,0:T(8,128)(2,1)S(1)} collective-permute-done((bf16[512,1280]{1,0:T(8,128)(2,1)S(1)}, bf16[512,1280]{1,0:T(8,128)(2,1)S(1)}, u32[]{:S(2)}, u32[]{:S(2)}) %collective-permute-start) | collective-permute-done | bytes 1310752 | tf_op jit(solution)/shard_map/ppermute | solution.py:605
  49.2 26.2 %collective-permute-done.1.refs_1_.refs_3_ = bf16[512,1280]{1,0:T(8,128)(2,1)S(1)} collective-permute-done((bf16[512,1280]{1,0:T(8,128)(2,1)S(1)}, bf16[512,1280]{1,0:T(8,128)(2,1)S(1)}, u32[]{:S(2)}, u32[]{:S(2)}) %collective-permute-start.1) | collective-permute-done | bytes 1310752 | tf_op jit(solution)/shard_map/ppermute | solution.py:605
  101.6 64.7 %collective-permute-done.4.refs_0_ = bf16[512,1280]{1,0:T(8,128)(2,1)} collective-permute-done((bf16[512,1280]{1,0:T(8,128)(2,1)}, bf16[512,1280]{1,0:T(8,128)(2,1)}, u32[]{:S(2)}, u32[]{:S(2)}) %collective-permute-start.4) | collective-permute-done | bytes 1310752 | tf_op jit(solution)/shard_map/ppermute | solution.py:502
  185.6 11.9 %collective-permute-start.13 = (bf16[1024,1280]{1,0:T(8,128)(2,1)}, bf16[1024,1280]{1,0:T(8,128)(2,1)}, u32[]{:S(2)}, u32[]{:S(2)}) collective-permute-start(bf16[1024,1280]{1,0:T(8,128)(2,1)} %keys_values.3.refs_3_), channel_id=1, source_target_pairs={{0,2},{2,4},{4,6},{6,8},{8,10},{10,12},{12,14},{14,16},{16,18},{18... | collective-permute-start | bytes 7864328 | tf_op jit(solution)/shard_map/ppermute | solution.py:502
  221.9 32.3 %attend_forward.2 = (bf16[1024,640]{1,0:T(8,128)(2,1)}, f32[8,1024]{1,0:T(8,128)}) custom-call(s32[4]{0:T(128)} %get-tuple-element.256.lo_ref, s32[4]{0:T(128)} %get-tuple-element.257.count_ref, s32[2]{0:T(128)} %pad_add_fusion.4.place_ref.swap_ref, s32[2,1024]{1,0:T(2,128)} %pad_add_fusion.se_ref, bf16[1024,640]{1,0:T(8,128)(2,1)} %copy-done.45, ...), custom_call_target="tpu_custom_call" | custom-call | tf_op jit(solution)/shard_map/attend_forward/pallas_call | solution.py:145
  263.4 10.5 %collective-permute-start.12 = (bf16[512,1280]{1,0:T(8,128)(2,1)S(1)}, bf16[512,1280]{1,0:T(8,128)(2,1)}, u32[]{:S(2)}, u32[]{:S(2)}) collective-permute-start(bf16[512,1280]{1,0:T(8,128)(2,1)S(1)} %get-tuple-element.265), channel_id=1, source_target_pairs={{0,4},{4,8},{8,12},{12,16},{16,20},{20,24},{24,28},{1,5},{5,9},{9,... | collective-permute-start | bytes 3932168 | tf_op jit(solution)/shard_map/ppermute | solution.py:502
  277.1 29.3 %collective-permute-start.14 = (bf16[512,1280]{1,0:T(8,128)(2,1)S(1)}, bf16[512,1280]{1,0:T(8,128)(2,1)}, u32[]{:S(2)}, u32[]{:S(2)}) collective-permute-start(bf16[512,1280]{1,0:T(8,128)(2,1)S(1)} %constant_dynamic-slice_fusion.2), channel_id=1, source_target_pairs={{0,2},{4,6},{8,10},{12,14},{16,18},{20,22},{24,26},{28,30},{1,3},{... | collective-permute-start | bytes 3932168 | tf_op jit(solution)/shard_map/ppermute | solution.py:502
  319.4 32.3 %attend_forward.3 = (bf16[1024,640]{1,0:T(8,128)(2,1)}, f32[8,1024]{1,0:T(8,128)}) custom-call(s32[4]{0:T(128)} %get-tuple-element.258.lo_ref, s32[4]{0:T(128)} %get-tuple-element.259.count_ref, s32[2]{0:T(128)} %pad_add_fusion.4.place_ref.swap_ref, s32[2,1024]{1,0:T(2,128)} %pad_add_fusion.1.se_ref, bf16[1024,640]{1,0:T(8,128)(2,1)} %copy-done.44, ...), custom_call_target="tpu_custom_call" | custom-call | tf_op jit(solution)/shard_map/attend_forward/pallas_call | solution.py:145
  360.2 14.0 %widen.2 = (bf16[1024,2560]{1,0:T(8,128)(2,1)}, bf16[1024,2560]{1,0:T(8,128)(2,1)}) custom-call(bf16[512,1280]{1,0:T(8,128)(2,1)} %add_convert_fusion.3.refs_0_, bf16[512,1280]{1,0:T(8,128)(2,1)} %collective-permute-done.11.refs_1_, bf16[2,1280,2560]{2,1,0:T(8,128)(2,1)} %all-gather.4.cloned.1.call-done.refs_2_.refs_1_, f32[1,2560]{1,0:T(1,128)S(1)} %reshape.126.refs_3_), custom_call_target="tpu_custom_call" | custom-call | tf_op jit(solution)/shard_map/widen/pallas_call | solution.py:281
  374.2 12.4 %grad_hidden.2 = (bf16[1024,2560]{1,0:T(8,128)(2,1)}, f32[1,2560]{1,0:T(1,128)S(1)}) custom-call(bf16[512,1280]{1,0:T(8,128)(2,1)} %get-tuple-element.111.refs_0_.base_ref, bf16[512,1280]{1,0:T(8,128)(2,1)} %collective-permute-done.2.refs_1_, bf16[2,1280,2560]{2,1,0:T(8,128)(2,1)} %all-gather.4.cloned.1.call-done.refs_2_.refs_1_, ...), custom_call_target="tpu_custom_call" | custom-call | tf_op jit(solution)/shard_map/grad_hidden/pallas_call | solution.py:281
  386.6 11.7 %grad_normed.2 = (f32[512,1280]{1,0:T(8,128)S(1)}, bf16[512,1280]{1,0:T(8,128)(2,1)}) custom-call(bf16[1024,2560]{1,0:T(8,128)(2,1)} %get-tuple-element.130.refs_0_.refs_2_, bf16[2,1280,2560]{2,1,0:T(8,128)(2,1)} %all-gather.4.cloned.1.call-done.refs_2_.refs_1_), custom_call_target="tpu_custom_call" | custom-call | tf_op jit(solution)/shard_map/grad_normed/pallas_call | solution.py:391
  404.5 11.3 %narrow.2 = (f32[512,1280]{1,0:T(8,128)S(1)}, bf16[512,1280]{1,0:T(8,128)(2,1)S(1)}) custom-call(bf16[1024,2560]{1,0:T(8,128)(2,1)} %get-tuple-element.133.refs_0_.refs_2_, bf16[2,1280,2560]{2,1,0:T(8,128)(2,1)} %all-gather.4.cloned.1.call-done.refs_2_.refs_1_), custom_call_target="tpu_custom_call" | custom-call | tf_op jit(solution)/shard_map/narrow/pallas_call | solution.py:391
  417.3 13.9 %weight_terms.6.refs_3_ = f32[1280,2560]{1,0:T(8,128)} custom-call(bf16[512,1280]{1,0:T(8,128)(2,1)} %get-tuple-element.111.refs_0_.base_ref, bf16[512,1280]{1,0:T(8,128)(2,1)} %collective-permute-done.2.refs_1_, bf16[1024,2560]{1,0:T(8,128)(2,1)} %get-tuple-element.133.refs_0_.refs_2_), custom_call_target="tpu_custom_call" | custom-call | tf_op jit(solution)/shard_map/weight_terms/pallas_call | solution.py:476
  440.5 14.4 %weight_terms.7.refs_3_ = f32[1280,2560]{1,0:T(8,128)} custom-call(bf16[512,1280]{1,0:T(8,128)(2,1)} %add_convert_fusion.3.refs_0_, bf16[512,1280]{1,0:T(8,128)(2,1)} %collective-permute-done.11.refs_1_, bf16[1024,2560]{1,0:T(8,128)(2,1)} %get-tuple-element.130.refs_0_.refs_2_), custom_call_target="tpu_custom_call" | custom-call | tf_op jit(solution)/shard_map/weight_terms/pallas_call | solution.py:476
  459.8 14.0 %widen.3 = (bf16[1024,2560]{1,0:T(8,128)(2,1)}, bf16[1024,2560]{1,0:T(8,128)(2,1)}) custom-call(bf16[512,1280]{1,0:T(8,128)(2,1)} %add_convert_fusion.2.refs_0_, bf16[512,1280]{1,0:T(8,128)(2,1)} %collective-permute-done.21.refs_1_, bf16[2,1280,2560]{2,1,0:T(8,128)(2,1)} %all-gather.4.cloned.1.call-done.refs_2_.refs_1_, f32[1,2560]{1,0:T(1,128)S(1)} %reshape.126.refs_3_), custom_call_target="tpu_custom_call" | custom-call | tf_op jit(solution)/shard_map/widen/pallas_call | solution.py:281
  473.8 12.0 %grad_hidden.3 = (bf16[1024,2560]{1,0:T(8,128)(2,1)}, f32[1,2560]{1,0:T(1,128)S(1)}) custom-call(bf16[512,1280]{1,0:T(8,128)(2,1)S(1)} %copy-done.33, bf16[512,1280]{1,0:T(8,128)(2,1)} %collective-permute-done.3.refs_1_, bf16[2,1280,2560]{2,1,0:T(8,128)(2,1)} %all-gather.4.cloned.1.call-done.refs_2_.refs_1_, bf16[1024,2560]{1,0:T(8,128)(2,1)} %get-tuple-element.143.refs_3_), custom_call_target="tpu_custom_call" | custom-call | tf_op jit(solution)/shard_map/grad_hidden/pallas_call | solution.py:281
  485.8 11.5 %grad_normed.3 = (f32[512,1280]{1,0:T(8,128)S(1)}, bf16[512,1280]{1,0:T(8,128)(2,1)}) custom-call(bf16[1024,2560]{1,0:T(8,128)(2,1)} %get-tuple-element.146.refs_0_.refs_2_, bf16[2,1280,2560]{2,1,0:T(8,128)(2,1)} %all-gather.4.cloned.1.call-done.refs_2_.refs_1_), custom_call_target="tpu_custom_call" | custom-call | tf_op jit(solution)/shard_map/grad_normed/pallas_call | solution.py:391
  497.3 16.0 %weight_terms.8.refs_4_ = bf16[2,1280,2560]{2,1,0:T(8,128)(2,1)} custom-call(bf16[512,1280]{1,0:T(8,128)(2,1)S(1)} %copy-done.33, bf16[512,1280]{1,0:T(8,128)(2,1)} %collective-permute-done.3.refs_1_, bf16[1024,2560]{1,0:T(8,128)(2,1)} %get-tuple-element.166.refs_2_.refs_0_, f32[1280,2560]{1,0:T(8,128)} %weight_terms.6.refs_3_), custom_call_target="tpu_custom_call" | custom-call | tf_op jit(solution)/shard_map/weight_terms/pallas_call | solution.py:476
  513.3 14.6 %collective-permute-done.22.far_ref = bf16[512,1280]{1,0:T(8,128)(2,1)} collective-permute-done((bf16[512,1280]{1,0:T(8,128)(2,1)}, bf16[512,1280]{1,0:T(8,128)(2,1)}, u32[]{:S(2)}, u32[]{:S(2)}) %collective-permute-start.22) | collective-permute-done | bytes 1310752 | tf_op jit(solution)/shard_map/ppermute | solution.py:605
  538.0 15.1 %weight_terms.9 = bf16[2,1280,2560]{2,1,0:T(8,128)(2,1)} custom-call(bf16[512,1280]{1,0:T(8,128)(2,1)} %add_convert_fusion.2.refs_0_, bf16[512,1280]{1,0:T(8,128)(2,1)} %collective-permute-done.21.refs_1_, bf16[1024,2560]{1,0:T(8,128)(2,1)} %get-tuple-element.146.refs_0_.refs_2_, f32[1280,2560]{1,0:T(8,128)} %weight_terms.7.refs_3_, ...), custom_call_target="tpu_custom_call", output_to_operand_aliasing={{}: (4, {})} | custom-call | tf_op jit(solution)/shard_map/weight_terms/pallas_call | solution.py:476
  563.3 51.7 %attend_backward.2 = (bf16[1024,640]{1,0:T(8,128)(2,1)}, bf16[1024,1280]{1,0:T(8,128)(2,1)}, bf16[1024,1280]{1,0:T(8,128)(2,1)}, bf16[1024,1280]{1,0:T(8,128)(2,...) custom-call(s32[4]{0:T(128)} %get-tuple-element.249.lo_ref, s32[4]{0:T(128)} %get-tuple-element.250.count_ref, ...), custom_call_target="tpu_custom_call" | custom-call | tf_op jit(solution)/shard_map/attend_backward/pallas_call | solution.py:230
  615.0 11.7 %collective-permute-start.25 = (bf16[512,1280]{1,0:T(8,128)(2,1)}, bf16[512,1280]{1,0:T(8,128)(2,1)}, u32[]{:S(2)}, u32[]{:S(2)}) collective-permute-start(bf16[512,1280]{1,0:T(8,128)(2,1)} %get-tuple-element.162), channel_id=1, source_target_pairs={{0,2},{2,0},{4,6},{6,4},{8,10},{10,8},{12,14},{14,12},{16,18},{18,... | collective-permute-start | bytes 3932168 | tf_op jit(solution)/shard_map/ppermute | solution.py:496
  643.4 49.9 %attend_backward.3 = (bf16[1024,640]{1,0:T(8,128)(2,1)}, bf16[1024,1280]{1,0:T(8,128)(2,1)}, bf16[1024,1280]{1,0:T(8,128)(2,1)}, bf16[1024,1280]{1,0:T(8,128)(2,...) custom-call(s32[4]{0:T(128)} %get-tuple-element.246.lo_ref, s32[4]{0:T(128)} %get-tuple-element.247.count_ref, ...), custom_call_target="tpu_custom_call" | custom-call | tf_op jit(solution)/shard_map/attend_backward/pallas_call | solution.py:230
  693.4 9.9 %collective-permute-start.26 = (bf16[512,1280]{1,0:T(8,128)(2,1)}, bf16[512,1280]{1,0:T(8,128)(2,1)}, u32[]{:S(2)}, u32[]{:S(2)}) collective-permute-start(bf16[512,1280]{1,0:T(8,128)(2,1)} %get-tuple-element.170), channel_id=1, source_target_pairs={{0,2},{2,0},{4,6},{6,4},{8,10},{10,8},{12,14},{14,12},{16,18},{18,... | collective-permute-start | bytes 3932168 | tf_op jit(solution)/shard_map/ppermute | solution.py:496
  713.5 11.0 %narrow.3 = (f32[512,1280]{1,0:T(8,128)S(1)}, bf16[512,1280]{1,0:T(8,128)(2,1)S(1)}) custom-call(bf16[1024,2560]{1,0:T(8,128)(2,1)} %get-tuple-element.166.refs_2_.refs_0_, bf16[2,1280,2560]{2,1,0:T(8,128)(2,1)} %all-gather.4.cloned.1.call-done.refs_2_.refs_1_), custom_call_target="tpu_custom_call" | custom-call | tf_op jit(solution)/shard_map/narrow/pallas_call | solution.py:391
  725.6 15.9 %weight_terms.10.refs_6_ = f32[1280,2560]{1,0:T(8,128)} custom-call(bf16[512,1280]{1,0:T(8,128)(2,1)S(1)} %copy-done.14, bf16[512,1280]{1,0:T(8,128)(2,1)} %copy-done.26, bf16[512,1280]{1,0:T(8,128)(2,1)} %copy-done.16, bf16[512,1280]{1,0:T(8,128)(2,1)} %copy-done.30, bf16[512,1280]{1,0:T(8,128)(2,1)} %get-tuple-element.140.refs_0_.refs_4_, ...), custom_call_target="tpu_custom_call" | custom-call | tf_op jit(solution)/shard_map/weight_terms/pallas_call | solution.py:476
  749.1 47.2 %collective-permute-start.34 = (bf16[1024,1280]{1,0:T(8,128)(2,1)}, bf16[1024,1280]{1,0:T(8,128)(2,1)}, u32[]{:S(2)}, u32[]{:S(2)}) collective-permute-start(bf16[1024,1280]{1,0:T(8,128)(2,1)} %add_far.7), channel_id=1, source_target_pairs={{0,2},{2,0},{4,6},{6,4},{8,10},{10,8},{12,14},{14,12},{16,18},{18,... | collective-permute-start | bytes 7864328 | tf_op jit(solution)/shard_map/ppermute | solution.py:496
  816.8 10.4 %collective-permute-done.31 = bf16[512,1280]{1,0:T(8,128)(2,1)} collective-permute-done((bf16[512,1280]{1,0:T(8,128)(2,1)}, bf16[512,1280]{1,0:T(8,128)(2,1)}, u32[]{:S(2)}, u32[]{:S(2)}) %collective-permute-start.31) | collective-permute-done | bytes 1310752 | tf_op jit(solution)/shard_map/ppermute | solution.py:605
  841.5 11.6 %weight_terms.11 = bf16[1280,2560]{1,0:T(8,128)(2,1)S(1)} custom-call(bf16[512,1280]{1,0:T(8,128)(2,1)S(1)} %copy-done.15, bf16[512,1280]{1,0:T(8,128)(2,1)S(1)} %copy-done.29, bf16[512,1280]{1,0:T(8,128)(2,1)S(1)} %copy-done.18, bf16[512,1280]{1,0:T(8,128)(2,1)S(1)} %copy-done.32, bf16[1024,1280]{1,0:T(8,128)(2,1)S(1)} %copy-done.20, ...), custom_call_target="tpu_custom_call" | custom-call | tf_op jit(solution)/shard_map/weight_terms/pallas_call | solution.py:476
  881.6 15.2 %collective-permute-done.35.far_ref = bf16[512,1280]{1,0:T(8,128)(2,1)S(1)} collective-permute-done((bf16[512,1280]{1,0:T(8,128)(2,1)S(1)}, bf16[512,1280]{1,0:T(8,128)(2,1)S(1)}, u32[]{:S(2)}, u32[]{:S(2)}) %collective-permute-start.35) | collective-permute-done | bytes 1310752 | tf_op jit(solution)/shard_map/ppermute | solution.py:605
  901.9 21.4 %collective-permute-start.36 = (f32[11520]{0:T(1024)S(1)}, f32[11520]{0:T(1024)S(1)}, u32[]{:S(2)}, u32[]{:S(2)}) collective-permute-start(f32[11520]{0:T(1024)S(1)} %pad_maximum_fusion.4), channel_id=1, source_target_pairs={{0,2},{2,0},{4,6},{6,4},{8,10},{10,8},{12,14},{14,12},{16,18},{18,... | collective-permute-start | bytes 138248 | tf_op jit(solution)/shard_map/ppermute | solution.py:585
  956.4 19.1 %reduce-scatter.5.cloned.1.call-done = bf16[80,2560]{1,0:T(8,128)(2,1)} async-done(((bf16[1280,2560]{1,0:T(8,128)(2,1)}), bf16[80,2560]{1,0:T(8,128)(2,1)}) %reduce-scatter.5.cloned.1.call-update) | async-done | bytes 409616 | tf_op jit(solution)/shard_map/reduce_scatter | solution.py:827
  (364 shorter events, 300.5 us)
Async XLA Ops:
  7.2 69.8 %all-gather.6.cloned.1.call-start = ((), (), s32[]{:S(2)}) async-start(), calls=%async_computation.5 | async-start | bytes 6963200 | tf_op jit(solution)/shard_map/all_gather | solution.py:694
  10.1 350.1 %all-gather.4.cloned.1.call-start = ((), (), s32[]{:S(2)}) async-start(), calls=%async_computation.2 | async-start | bytes 13926400 | tf_op jit(solution)/shard_map/all_gather | solution.py:837
  15.5 32.6 %collective-permute-start = (bf16[512,1280]{1,0:T(8,128)(2,1)S(1)}, bf16[512,1280]{1,0:T(8,128)(2,1)S(1)}, u32[]{:S(2)}, u32[]{:S(2)}) collective-permute-start(bf16[512,1280]{1,0:T(8,128)(2,1)S(1)} %get-tuple-element.260.refs_0_), channel_id=1, source_target_pairs={{0,1},{1,0},{2,3},{3,2},{4,5},{5,4},{6,7},{7,6},{8,9},{9,8},{10,11... | collective-permute-start | bytes 3932168 | tf_op jit(solution)/shard_map/ppermute | solution.py:605
  19.6 55.8 %collective-permute-start.1 = (bf16[512,1280]{1,0:T(8,128)(2,1)S(1)}, bf16[512,1280]{1,0:T(8,128)(2,1)S(1)}, u32[]{:S(2)}, u32[]{:S(2)}) collective-permute-start(bf16[512,1280]{1,0:T(8,128)(2,1)S(1)} %get-tuple-element.261.refs_0_.refs_2_), channel_id=1, source_target_pairs={{0,1},{1,0},{2,3},{3,2},{4,5},{5,4},{6,7},{7,6},{8,9},{9,8},{10,11... | collective-permute-start | bytes 3932168 | tf_op jit(solution)/shard_map/ppermute | solution.py:605
  87.5 78.9 %collective-permute-start.5 = (bf16[1024,1280]{1,0:T(8,128)(2,1)S(1)}, bf16[1024,1280]{1,0:T(8,128)(2,1)}, u32[]{:S(2)}, u32[]{:S(2)}) collective-permute-start(bf16[1024,1280]{1,0:T(8,128)(2,1)S(1)} %keys_values.2.refs_3_), channel_id=1, source_target_pairs={{0,2},{2,4},{4,6},{6,8},{8,10},{10,12},{12,14},{14,16},{16,18},{18... | collective-permute-start | bytes 7864328 | tf_op jit(solution)/shard_map/ppermute | solution.py:502
  91.1 75.2 %collective-permute-start.7 = (bf16[1024,1280]{1,0:T(8,128)(2,1)S(1)}, bf16[1024,1280]{1,0:T(8,128)(2,1)}, u32[]{:S(2)}, u32[]{:S(2)}) collective-permute-start(bf16[1024,1280]{1,0:T(8,128)(2,1)S(1)} %keys_values.2.refs_3_), channel_id=1, source_target_pairs={{2,0},{4,2},{6,4},{8,6},{10,8},{12,10},{14,12},{16,14},{18,16},{20... | collective-permute-start | bytes 7864328 | tf_op jit(solution)/shard_map/ppermute | solution.py:502
  94.1 72.2 %collective-permute-start.4 = (bf16[512,1280]{1,0:T(8,128)(2,1)}, bf16[512,1280]{1,0:T(8,128)(2,1)}, u32[]{:S(2)}, u32[]{:S(2)}) collective-permute-start(bf16[512,1280]{1,0:T(8,128)(2,1)} %get-tuple-element.267), channel_id=1, source_target_pairs={{0,4},{4,8},{8,12},{12,16},{16,20},{20,24},{24,28},{1,5},{5,9},{9,... | collective-permute-start | bytes 3932168 | tf_op jit(solution)/shard_map/ppermute | solution.py:502
  98.9 67.4 %collective-permute-start.8 = (bf16[512,1280]{1,0:T(8,128)(2,1)}, bf16[512,1280]{1,0:T(8,128)(2,1)}, u32[]{:S(2)}, u32[]{:S(2)}) collective-permute-start(bf16[512,1280]{1,0:T(8,128)(2,1)} %get-tuple-element.266), channel_id=1, source_target_pairs={{6,2},{10,6},{14,10},{18,14},{22,18},{26,22},{30,26},{7,3},{11,7},... | collective-permute-start | bytes 3932168 | tf_op jit(solution)/shard_map/ppermute | solution.py:502
  166.4 689.3 %reduce-scatter.3.cloned.1.call-start = ((), (), s32[]{:S(2)}) async-start(), calls=%async_computation.3 | async-start | bytes 13926400 | tf_op jit(solution)/shard_map/reduce_scatter | solution.py:827
  170.0 39.8 %collective-permute-start.2 = (bf16[512,1280]{1,0:T(8,128)(2,1)}, bf16[512,1280]{1,0:T(8,128)(2,1)}, u32[]{:S(2)}, u32[]{:S(2)}) collective-permute-start(bf16[512,1280]{1,0:T(8,128)(2,1)} %get-tuple-element.111.refs_0_.base_ref), channel_id=1, source_target_pairs={{0,1},{1,0},{2,3},{3,2},{4,5},{5,4},{6,7},{7,6},{8,9},{9,8},{10,11... | collective-permute-start | bytes 3932168 | tf_op jit(solution)/shard_map/ppermute | solution.py:605
  171.8 50.2 %collective-permute-start.3 = (bf16[512,1280]{1,0:T(8,128)(2,1)}, bf16[512,1280]{1,0:T(8,128)(2,1)}, u32[]{:S(2)}, u32[]{:S(2)}) collective-permute-start(bf16[512,1280]{1,0:T(8,128)(2,1)} %get-tuple-element.112.refs_0_.base_ref), channel_id=1, source_target_pairs={{0,1},{1,0},{2,3},{3,2},{4,5},{5,4},{6,7},{7,6},{8,9},{9,8},{10,11... | collective-permute-start | bytes 3932168 | tf_op jit(solution)/shard_map/ppermute | solution.py:605
  185.6 90.1 %collective-permute-start.13 = (bf16[1024,1280]{1,0:T(8,128)(2,1)}, bf16[1024,1280]{1,0:T(8,128)(2,1)}, u32[]{:S(2)}, u32[]{:S(2)}) collective-permute-start(bf16[1024,1280]{1,0:T(8,128)(2,1)} %keys_values.3.refs_3_), channel_id=1, source_target_pairs={{0,2},{2,4},{4,6},{6,8},{8,10},{10,12},{12,14},{14,16},{16,18},{18... | collective-permute-start | bytes 7864328 | tf_op jit(solution)/shard_map/ppermute | solution.py:502
  197.5 108.9 %collective-permute-start.15 = (bf16[1024,1280]{1,0:T(8,128)(2,1)}, bf16[1024,1280]{1,0:T(8,128)(2,1)}, u32[]{:S(2)}, u32[]{:S(2)}) collective-permute-start(bf16[1024,1280]{1,0:T(8,128)(2,1)} %keys_values.3.refs_3_), channel_id=1, source_target_pairs={{2,0},{4,2},{6,4},{8,6},{10,8},{12,10},{14,12},{16,14},{18,16},{20... | collective-permute-start | bytes 7864328 | tf_op jit(solution)/shard_map/ppermute | solution.py:502
  258.9 50.3 %collective-permute-start.10 = (bf16[512,1280]{1,0:T(8,128)(2,1)S(1)}, bf16[512,1280]{1,0:T(8,128)(2,1)S(1)}, u32[]{:S(2)}, u32[]{:S(2)}) collective-permute-start(bf16[512,1280]{1,0:T(8,128)(2,1)S(1)} %get-tuple-element.117), channel_id=1, source_target_pairs={{0,1},{1,0},{2,3},{3,2},{4,5},{5,4},{6,7},{7,6},{8,9},{9,8},{10,11... | collective-permute-start | bytes 3932168 | tf_op jit(solution)/shard_map/ppermute | solution.py:605
  263.4 56.0 %collective-permute-start.12 = (bf16[512,1280]{1,0:T(8,128)(2,1)S(1)}, bf16[512,1280]{1,0:T(8,128)(2,1)}, u32[]{:S(2)}, u32[]{:S(2)}) collective-permute-start(bf16[512,1280]{1,0:T(8,128)(2,1)S(1)} %get-tuple-element.265), channel_id=1, source_target_pairs={{0,4},{4,8},{8,12},{12,16},{16,20},{20,24},{24,28},{1,5},{5,9},{9,... | collective-permute-start | bytes 3932168 | tf_op jit(solution)/shard_map/ppermute | solution.py:502
  273.8 45.5 %collective-permute-start.16 = (bf16[512,1280]{1,0:T(8,128)(2,1)S(1)}, bf16[512,1280]{1,0:T(8,128)(2,1)}, u32[]{:S(2)}, u32[]{:S(2)}) collective-permute-start(bf16[512,1280]{1,0:T(8,128)(2,1)S(1)} %get-tuple-element.264), channel_id=1, source_target_pairs={{6,2},{10,6},{14,10},{18,14},{22,18},{26,22},{30,26},{7,3},{11,7},... | collective-permute-start | bytes 3932168 | tf_op jit(solution)/shard_map/ppermute | solution.py:502
  277.1 42.2 %collective-permute-start.14 = (bf16[512,1280]{1,0:T(8,128)(2,1)S(1)}, bf16[512,1280]{1,0:T(8,128)(2,1)}, u32[]{:S(2)}, u32[]{:S(2)}) collective-permute-start(bf16[512,1280]{1,0:T(8,128)(2,1)S(1)} %constant_dynamic-slice_fusion.2), channel_id=1, source_target_pairs={{0,2},{4,6},{8,10},{12,14},{16,18},{20,22},{24,26},{28,30},{1,3},{... | collective-permute-start | bytes 3932168 | tf_op jit(solution)/shard_map/ppermute | solution.py:502
  311.8 48.4 %collective-permute-start.11 = (bf16[512,1280]{1,0:T(8,128)(2,1)}, bf16[512,1280]{1,0:T(8,128)(2,1)}, u32[]{:S(2)}, u32[]{:S(2)}) collective-permute-start(bf16[512,1280]{1,0:T(8,128)(2,1)} %add_convert_fusion.3.refs_0_), channel_id=1, source_target_pairs={{0,1},{1,0},{2,3},{3,2},{4,5},{5,4},{6,7},{7,6},{8,9},{9,8},{10,11... | collective-permute-start | bytes 3932168 | tf_op jit(solution)/shard_map/ppermute | solution.py:605
  358.6 41.2 %collective-permute-start.18 = (bf16[512,1280]{1,0:T(8,128)(2,1)}, bf16[512,1280]{1,0:T(8,128)(2,1)S(1)}, u32[]{:S(2)}, u32[]{:S(2)}) collective-permute-start(bf16[512,1280]{1,0:T(8,128)(2,1)} %get-tuple-element.126), channel_id=1, source_target_pairs={{0,1},{1,0},{2,3},{3,2},{4,5},{5,4},{6,7},{7,6},{8,9},{9,8},{10,11... | collective-permute-start | bytes 3932168 | tf_op jit(solution)/shard_map/ppermute | solution.py:605
  402.9 56.9 %collective-permute-start.21 = (bf16[512,1280]{1,0:T(8,128)(2,1)}, bf16[512,1280]{1,0:T(8,128)(2,1)}, u32[]{:S(2)}, u32[]{:S(2)}) collective-permute-start(bf16[512,1280]{1,0:T(8,128)(2,1)} %add_convert_fusion.2.refs_0_), channel_id=1, source_target_pairs={{0,1},{1,0},{2,3},{3,2},{4,5},{5,4},{6,7},{7,6},{8,9},{9,8},{10,11... | collective-permute-start | bytes 3932168 | tf_op jit(solution)/shard_map/ppermute | solution.py:605
  440.5 56.8 %collective-permute-start.20 = (bf16[512,1280]{1,0:T(8,128)(2,1)}, bf16[512,1280]{1,0:T(8,128)(2,1)S(1)}, u32[]{:S(2)}, u32[]{:S(2)}) collective-permute-start(bf16[512,1280]{1,0:T(8,128)(2,1)} %get-tuple-element.140.refs_0_.refs_4_), channel_id=1, source_target_pairs={{0,1},{1,0},{2,3},{3,2},{4,5},{5,4},{6,7},{7,6},{8,9},{9,8},{10,11... | collective-permute-start | bytes 3932168 | tf_op jit(solution)/shard_map/ppermute | solution.py:605
  553.1 422.4 %reduce-scatter.5.cloned.1.call-start = ((), (), s32[]{:S(2)}) async-start(), calls=%async_computation.4 | async-start | bytes 6963200 | tf_op jit(solution)/shard_map/reduce_scatter | solution.py:827
  553.1 77.3 %collective-permute-start.24 = (bf16[512,1280]{1,0:T(8,128)(2,1)}, bf16[512,1280]{1,0:T(8,128)(2,1)}, u32[]{:S(2)}, u32[]{:S(2)}) collective-permute-start(bf16[512,1280]{1,0:T(8,128)(2,1)} %copy-done.48), channel_id=1, source_target_pairs={{0,1},{1,0},{2,3},{3,2},{4,5},{5,4},{6,7},{7,6},{8,9},{9,8},{10,11... | collective-permute-start | bytes 3932168 | tf_op jit(solution)/shard_map/ppermute | solution.py:605
  626.7 86.7 %collective-permute-start.23 = (bf16[512,1280]{1,0:T(8,128)(2,1)}, bf16[512,1280]{1,0:T(8,128)(2,1)}, u32[]{:S(2)}, u32[]{:S(2)}) collective-permute-start(bf16[512,1280]{1,0:T(8,128)(2,1)} %copy-done.70), channel_id=1, source_target_pairs={{0,1},{1,0},{2,3},{3,2},{4,5},{5,4},{6,7},{7,6},{8,9},{9,8},{10,11... | collective-permute-start | bytes 3932168 | tf_op jit(solution)/shard_map/ppermute | solution.py:605
  628.5 78.9 %collective-permute-start.28 = (bf16[512,1280]{1,0:T(8,128)(2,1)}, bf16[512,1280]{1,0:T(8,128)(2,1)}, u32[]{:S(2)}, u32[]{:S(2)}) collective-permute-start(bf16[512,1280]{1,0:T(8,128)(2,1)} %get-tuple-element.174), channel_id=1, source_target_pairs={{2,4},{4,2},{6,8},{8,6},{10,12},{12,10},{14,16},{16,14},{18,20},{2... | collective-permute-start | bytes 3932168 | tf_op jit(solution)/shard_map/ppermute | solution.py:492
  693.4 48.1 %collective-permute-start.26 = (bf16[512,1280]{1,0:T(8,128)(2,1)}, bf16[512,1280]{1,0:T(8,128)(2,1)}, u32[]{:S(2)}, u32[]{:S(2)}) collective-permute-start(bf16[512,1280]{1,0:T(8,128)(2,1)} %get-tuple-element.170), channel_id=1, source_target_pairs={{0,2},{2,0},{4,6},{6,4},{8,10},{10,8},{12,14},{14,12},{16,18},{18,... | collective-permute-start | bytes 3932168 | tf_op jit(solution)/shard_map/ppermute | solution.py:496
  703.2 43.2 %collective-permute-start.33 = (bf16[512,1280]{1,0:T(8,128)(2,1)}, bf16[512,1280]{1,0:T(8,128)(2,1)}, u32[]{:S(2)}, u32[]{:S(2)}) collective-permute-start(bf16[512,1280]{1,0:T(8,128)(2,1)} %get-tuple-element.185), channel_id=1, source_target_pairs={{2,4},{4,2},{6,8},{8,6},{10,12},{12,10},{14,16},{16,14},{18,20},{2... | collective-permute-start | bytes 3932168 | tf_op jit(solution)/shard_map/ppermute | solution.py:492
  705.0 91.3 %collective-permute-start.27 = (bf16[1024,1280]{1,0:T(8,128)(2,1)}, bf16[1024,1280]{1,0:T(8,128)(2,1)}, u32[]{:S(2)}, u32[]{:S(2)}) collective-permute-start(bf16[1024,1280]{1,0:T(8,128)(2,1)} %add_far.4), channel_id=1, source_target_pairs={{2,4},{4,2},{6,8},{8,6},{10,12},{12,10},{14,16},{16,14},{18,20},{2... | collective-permute-start | bytes 7864328 | tf_op jit(solution)/shard_map/ppermute | solution.py:492
  710.1 86.2 %collective-permute-start.29 = (bf16[1024,1280]{1,0:T(8,128)(2,1)}, bf16[1024,1280]{1,0:T(8,128)(2,1)}, u32[]{:S(2)}, u32[]{:S(2)}) collective-permute-start(bf16[1024,1280]{1,0:T(8,128)(2,1)} %add_far.6), channel_id=1, source_target_pairs={{0,2},{2,0},{4,6},{6,4},{8,10},{10,8},{12,14},{14,12},{16,18},{18,... | collective-permute-start | bytes 7864328 | tf_op jit(solution)/shard_map/ppermute | solution.py:496
  744.2 83.0 %collective-permute-start.32 = (bf16[1024,1280]{1,0:T(8,128)(2,1)}, bf16[1024,1280]{1,0:T(8,128)(2,1)}, u32[]{:S(2)}, u32[]{:S(2)}) collective-permute-start(bf16[1024,1280]{1,0:T(8,128)(2,1)} %add_far.5), channel_id=1, source_target_pairs={{2,4},{4,2},{6,8},{8,6},{10,12},{12,10},{14,16},{16,14},{18,20},{2... | collective-permute-start | bytes 7864328 | tf_op jit(solution)/shard_map/ppermute | solution.py:492
  749.1 78.2 %collective-permute-start.34 = (bf16[1024,1280]{1,0:T(8,128)(2,1)}, bf16[1024,1280]{1,0:T(8,128)(2,1)}, u32[]{:S(2)}, u32[]{:S(2)}) collective-permute-start(bf16[1024,1280]{1,0:T(8,128)(2,1)} %add_far.7), channel_id=1, source_target_pairs={{0,2},{2,0},{4,6},{6,4},{8,10},{10,8},{12,14},{14,12},{16,18},{18,... | collective-permute-start | bytes 7864328 | tf_op jit(solution)/shard_map/ppermute | solution.py:496
  796.3 31.0 %collective-permute-start.31 = (bf16[512,1280]{1,0:T(8,128)(2,1)}, bf16[512,1280]{1,0:T(8,128)(2,1)}, u32[]{:S(2)}, u32[]{:S(2)}) collective-permute-start(bf16[512,1280]{1,0:T(8,128)(2,1)} %copy-done.72), channel_id=1, source_target_pairs={{0,1},{1,0},{2,3},{3,2},{4,5},{5,4},{6,7},{7,6},{8,9},{9,8},{10,11... | collective-permute-start | bytes 3932168 | tf_op jit(solution)/shard_map/ppermute | solution.py:605
  (99 other events, 912.9 us)
Sparse Core Ops, SparseCore 0:
  10.9 66.0 all-gather.5
  166.5 168.2 all-gather.3
  553.2 163.9 reduce-scatter.2
  858.4 116.9 reduce-scatter.4
